TPU v7x, 256 devices: a whole 4x4x8 slice. The times are simulated.
256 devices in a mesh: dp: 4 (over z_hi, core), space: 64 (over y, x, z_lo).
Axes of the slice: x: 4, y: 4, z: 8 (z_hi: 2, z_lo: 4; z = z_hi * 4 + z_lo), core: 2. Of those that a mesh axis runs over, the one named last changes fastest.
Arguments:
- activations: bfloat16 [4, 32, 256, 16, 128], P('dp', None, 'space'), may hold values from -16 to 16
- cotangent: bfloat16 [4, 32, 256, 16, 128], P('dp', None, 'space'), may hold values from -16 to 16
- weight: bfloat16 [32, 864], replicated, may hold values from -0.21875 to 0.21875
Outputs:
- conv_out: bfloat16 [4, 32, 256, 16, 128], P('dp', None, 'space')
- input_grad: bfloat16 [4, 32, 256, 16, 128], P('dp', None, 'space')
- precond_grad: float32 [32, 864], replicated
All inputs are finite; a program needn't handle non-finite values. Where the computation divides by a largest or mean magnitude, that divisor is 1e-20 or more.
Results may differ from a plain program's by a relative error of at most 0.0049.
Values may be sent and summed in bfloat16 or wider, within the bound.
No kernel may reach another device: no remote copies, remote signals or barrier semaphores. Data moves between devices by JAX's collectives and lax.ppermute only.
A program may use at most 64 MiB of HBM per device.

v0:
```python
import jax
import jax.numpy as jnp
from jax import lax
from jax.sharding import PartitionSpec as P

ITERS = 3


DAMPING = 0.1
block_rows = 8


def extended(x, sides, width):
    for axis, dim in sides:
        size, length = (lax.axis_size(axis), x.shape[dim])
        up = [(i, (i + 1) % size) for i in range(size - 1)]
        down = [(j, i) for i, j in up]
        last = lax.slice_in_dim(x, length - width, length, axis=dim)
        initial = lax.slice_in_dim(x, 0, width, axis=dim)
        before = lax.ppermute(last, axis, up)
        after = lax.ppermute(initial, axis, down)
        x = jnp.concatenate([before, x, after], axis=dim)
    return x


def shift_depth(volume, offset):
    widths = [(0, 0)] * (volume.ndim - 1)
    if offset < 0:
        return jnp.pad(volume[..., :-1], widths + [(1, 0)])
    if offset > 0:
        return jnp.pad(volume[..., 1:], widths + [(0, 1)])
    return volume


def block_patches(source, plane_at, row_at):
    zero_index = jnp.asarray(0, jnp.int32)
    window = lax.dynamic_slice(
        source,
        (zero_index, plane_at, row_at, zero_index),
        (source.shape[0], 3, block_rows + 2, source.shape[3]),
    )
    pieces = []
    for first in range(3):
        for second in range(3):
            for third_tap in range(3):
                pieces.append(
                    shift_depth(window[:, first, second : second + block_rows, :], third_tap - 1)
                )
    stacked = jnp.stack(pieces, 0)
    return stacked.reshape(27 * source.shape[0], block_rows * source.shape[3])


def newton_inverse(factor, order_size):
    eye_matrix = jnp.eye(order_size, dtype=jnp.float32)
    scaled = factor * (order_size / jnp.trace(factor)) + DAMPING * eye_matrix
    row_bound = jnp.max(jnp.sum(jnp.abs(scaled), axis=1))
    iterate = eye_matrix / row_bound
    for sweep in range(ITERS):
        left_part = jnp.dot(iterate, scaled, precision=lax.Precision.HIGHEST)
        iterate = 2.0 * iterate - jnp.dot(left_part, iterate, precision=lax.Precision.HIGHEST)
    return iterate


def fold_rows(left_part, running, shard_rows):
    columns = lax.slice_in_dim(left_part, 0, shard_rows.shape[0], axis=1)
    return running + jnp.dot(
        columns, shard_rows, precision=lax.Precision.HIGHEST, preferred_element_type=jnp.float32
    )


def body(activations, cotangent, weight):
    samples, channels, planes, height, depth = activations.shape
    order_size = 27 * channels
    stacked = jnp.stack([activations, cotangent], 0)
    haloed = extended(stacked, (("space", 3),), 1)
    padded = jnp.pad(haloed, ((0, 0), (0, 0), (0, 0), (0, 0), (1, 1), (0, 0)))
    flipped = (
        weight.reshape(channels, 27, channels)[:, ::-1, :]
        .transpose(2, 1, 0)
        .reshape(channels, order_size)
    )
    blocks = height // block_rows
    contract = (((1,), (1,)), ((), ()))

    def step(carry, counter):
        act_sum, grad_sum, wgrad_sum = carry
        sample = counter // (planes * blocks)
        remain = counter % (planes * blocks)
        plane_at = remain // blocks
        row_at = remain % blocks * block_rows
        volumes = lax.dynamic_index_in_dim(padded, sample, 1, keepdims=False)
        act_patch = block_patches(volumes[0], plane_at, row_at)
        cot_patch = block_patches(volumes[1], plane_at, row_at)
        center = cot_patch[13 * channels : 14 * channels]
        out_block = jnp.dot(weight, act_patch, preferred_element_type=jnp.float32).astype(
            jnp.bfloat16
        )
        back_block = jnp.dot(flipped, cot_patch, preferred_element_type=jnp.float32).astype(
            jnp.bfloat16
        )
        act_sum = act_sum + lax.dot_general(
            act_patch, act_patch, contract, preferred_element_type=jnp.float32
        )
        grad_sum = grad_sum + lax.dot_general(
            center, center, contract, preferred_element_type=jnp.float32
        )
        wgrad_sum = wgrad_sum + lax.dot_general(
            center, act_patch, contract, preferred_element_type=jnp.float32
        )
        return ((act_sum, grad_sum, wgrad_sum), (out_block, back_block))

    start_carry = (
        jnp.zeros((order_size, order_size), jnp.float32),
        jnp.zeros((channels, channels), jnp.float32),
        jnp.zeros((channels, order_size), jnp.float32),
    )
    sums, results = lax.scan(
        step, start_carry, jnp.arange(samples * planes * blocks, dtype=jnp.int32)
    )

    def arrange(stacked_blocks):
        shaped = stacked_blocks.reshape(samples, planes, blocks, channels, block_rows, depth)
        return shaped.transpose(0, 3, 1, 2, 4, 5).reshape(samples, channels, planes, height, depth)

    conv_out = arrange(results[0])
    input_grad = arrange(results[1])
    cells_total = samples * planes * height * depth * lax.axis_size("dp") * lax.axis_size("space")
    groups = lax.axis_size("space")
    share_rows = (order_size + groups - 1) // groups
    padded_order = share_rows * groups
    extra = padded_order - order_size
    column_ids = jnp.arange(padded_order, dtype=jnp.int32)
    owner_of = column_ids // share_rows
    slot_of = column_ids % share_rows
    is_filler = (slot_of == share_rows - 1) & (owner_of < extra)
    source_ids = jnp.clip(column_ids - jnp.minimum(owner_of, extra), 0, order_size - 1)
    real_ids = jnp.arange(order_size, dtype=jnp.int32)
    front_count = extra * (share_rows - 1)
    place_ids = jnp.where(
        real_ids < front_count,
        real_ids // max(share_rows - 1, 1) * share_rows + real_ids % max(share_rows - 1, 1),
        real_ids + extra,
    )
    first_own = lax.axis_index("space") * share_rows
    row_ids = first_own + jnp.arange(share_rows, dtype=jnp.int32)
    identity_rows = (row_ids[:, None] == column_ids[None, :]).astype(jnp.float32)
    act_sum, grad_sum, wgrad_sum = lax.psum((sums[0], sums[1], sums[2]), ("dp", "space"))
    act_factor = act_sum / cells_total
    grad_factor = grad_sum / cells_total
    weight_grad = wgrad_sum / cells_total
    eye_matrix = jnp.eye(order_size, dtype=jnp.float32)
    scaled = act_factor * (order_size / jnp.trace(act_factor)) + DAMPING * eye_matrix
    row_bound = jnp.max(jnp.sum(jnp.abs(scaled), axis=1))
    moved = jnp.take(jnp.take(scaled, source_ids, axis=0), source_ids, axis=1)
    filler_any = is_filler[:, None] | is_filler[None, :]
    scaled_pad = jnp.where(filler_any, 0.0, moved) + jnp.diag(is_filler.astype(jnp.float32))
    own_rows = identity_rows / row_bound
    for sweep in range(ITERS):
        left_part = jnp.dot(own_rows, scaled_pad, precision=lax.Precision.HIGHEST)
        if sweep == 0:
            product = left_part * (1.0 / row_bound)
        else:
            product = fold_rows(
                left_part,
                jnp.zeros((share_rows, padded_order), jnp.float32),
                lax.all_gather(own_rows, "space", axis=0, tiled=True),
            )
        own_rows = 2.0 * own_rows - product
    inverse_grad = newton_inverse(grad_factor, channels)
    grad_pad = jnp.where(is_filler[None, :], 0.0, jnp.take(weight_grad, source_ids, axis=1))
    right_pad = fold_rows(
        grad_pad,
        jnp.zeros((channels, padded_order), jnp.float32),
        lax.all_gather(own_rows, "space", axis=0, tiled=True),
    )
    right_part = jnp.take(right_pad, place_ids, axis=1)
    applied = jnp.dot(inverse_grad, right_part, precision=lax.Precision.HIGHEST)
    quadratic = jnp.sum(applied * weight_grad)
    precond_grad = applied * jnp.sqrt(channels * order_size / quadratic)
    return (conv_out, input_grad, precond_grad)


def solution(mesh):
    return jax.shard_map(
        body,
        mesh=mesh,
        in_specs=(P("dp", None, "space", None, None), P("dp", None, "space", None, None), P()),
        out_specs=(P("dp", None, "space", None, None), P("dp", None, "space", None, None), P()),
        check_vma=False,
    )
```

profile of v0, /device:TPU:32, one launch (start us, length us, event | category | flops | bytes accessed | tf_op | source)
XLA Modules:
  0.0 1709.3 jit_solution(920452319659107486)
XLA Ops:
  9.2 3.8 collective-permute-start
  19.8 6.6 collective-permute-done.1
  28.3 284.3 %while.22 = (s32[]{:T(128)}, f32[864,864]{1,0:T(8,128)}, f32[32,32]{1,0:T(8,128)S(1)}, f32[32,864]{1,0:T(8,128)}, bf16[8,32,1024]{2,1,0:T(8,128)(2,1)}, /*index=...) while((s32[]{:T(128)}, f32[864,864]{1,0:T(8,128)}, ...), condition=%wide.region_1.2_spmd.clone, body=%wide.region_0.1_spmd.clone.sunk | while | flops 1702406144 | bytes 41757328 | solution.py:117
  56.3 3.7 select_add_fusion.8
  90.2 5.6 select_add_fusion.8
  126.0 5.6 select_add_fusion.8
  161.7 5.6 select_add_fusion.8
  197.5 5.6 select_add_fusion.8
  233.3 5.6 select_add_fusion.8
  269.1 5.6 select_add_fusion.8
  304.9 5.6 select_add_fusion.8
  312.9 267.0 %all-reduce.40.cloned.1.call-done = (f32[864,864]{1,0:T(8,128)}, f32[32,864]{1,0:T(8,128)}) async-done(((f32[864,864]{1,0:T(8,128)}, f32[32,864]{1,0:T(8,128)}), (f32[864,864]{1,0:T(8,128)}, f32[32,864]{1,0:T(8,128)})) %all-reduce.40.cloned.1.call-update) | async-done | bytes 3096592 | tf_op jit(solution)/shard_map/psum | solution.py:147
  585.6 4.0 gather_fusion.1
  589.6 3.8 broadcast_select_fusion
  596.8 4.0 gather_fusion.2
  608.2 3.6 fusion.127
  611.8 352.9 %all-gather.7.cloned.1.call-done = f32[64,14,896]{2,1,0:T(8,128)} async-done(((f32[1,14,896]{2,1,0:T(8,128)}), f32[64,14,896]{2,1,0:T(8,128)}) %all-gather.7.cloned.1.call-update) | async-done | bytes 3211280 | tf_op jit(solution)/shard_map/all_gather | solution.py:166
  964.7 4.6 reshape.283
  969.3 4.1 convolution_subtract_fusion.1
  973.7 3.6 fusion.128
  977.3 350.2 %all-gather.9.cloned.1.call-done = f32[64,14,896]{2,1,0:T(8,128)} async-done(((f32[1,14,896]{2,1,0:T(8,128)}), f32[64,14,896]{2,1,0:T(8,128)}) %all-gather.9.cloned.1.call-update) | async-done | bytes 3211280 | tf_op jit(solution)/shard_map/all_gather | solution.py:166
  1332.8 74.9 %psum.21 = f32[32,32]{1,0:T(8,128)S(1)} all-reduce(f32[32,32]{1,0:T(8,128)S(1)} %get-tuple-element.175), channel_id=1, replica_groups=mesh['dp'=4,'space'=64] {'dp','space'}, use_global_device_ids=true, to_apply=%region_2.3 | all-reduce | flops 1024 | bytes 8192 | tf_op jit(solution)/shard_map/psum | solution.py:147
  1417.5 269.7 %all-gather.11.cloned.1.call-done = f32[64,14,896]{2,1,0:T(8,128)} async-done(((f32[1,14,896]{2,1,0:T(8,128)}), f32[64,14,896]{2,1,0:T(8,128)}) %all-gather.11.cloned.1.call-update) | async-done | bytes 3211280 | tf_op jit(solution)/shard_map/all_gather | solution.py:174
  1690.0 7.2 fusion.47
  (791 shorter events, 271.4 us)
Async XLA Ops:
  7.2 7.9 copy-start.7
  7.2 572.8 %all-reduce.40.cloned.1.call-start = ((), (), s32[]{:S(2)}) async-start(), calls=%async_computation.3 | async-start | bytes 6422528 | tf_op jit(solution)/shard_map/psum | solution.py:147
  9.2 9.9 collective-permute-start
  13.0 13.4 collective-permute-start.1
  31.8 12.1 copy-start.1
  65.6 12.1 copy-start.1
  90.2 5.6 copy-start.8
  101.4 12.1 copy-start.1
  126.0 5.6 copy-start.8
  137.2 12.1 copy-start.1
  161.7 5.6 copy-start.8
  172.9 12.1 copy-start.1
  197.5 5.6 copy-start.8
  208.7 12.1 copy-start.1
  233.3 5.6 copy-start.8
  244.5 12.1 copy-start.1
  280.3 12.1 copy-start.1
  304.9 5.6 copy-start.8
  312.6 652.1 %all-gather.7.cloned.1.call-start = ((), (), s32[]{:S(2)}) async-start(), calls=%async_computation | async-start | bytes 3727360 | tf_op jit(solution)/shard_map/all_gather | solution.py:166
  608.2 719.4 %all-gather.9.cloned.1.call-start = ((), (), s32[]{:S(2)}) async-start(), calls=%async_computation.1 | async-start | bytes 3727360 | tf_op jit(solution)/shard_map/all_gather | solution.py:166
  611.8 357.5 %copy-start.3 = (f32[14,896]{1,0:T(8,128)S(1)}, f32[14,896]{1,0:T(8,128)}, u32[]{:S(2)}) copy-start(f32[14,896]{1,0:T(8,128)} %fusion.46) | copy-start | bytes 150532
  973.4 713.7 %all-gather.11.cloned.1.call-start = ((), (), s32[]{:S(2)}) async-start(), calls=%async_computation.2 | async-start | bytes 3727360 | tf_op jit(solution)/shard_map/all_gather | solution.py:174
  977.3 353.2 %copy-start.2 = (f32[14,896]{1,0:T(8,128)S(1)}, f32[14,896]{1,0:T(8,128)}, u32[]{:S(2)}) copy-start(f32[14,896]{1,0:T(8,128)} %convolution_subtract_fusion.1) | copy-start | bytes 150532
  1332.7 79.8 %copy-start.4 = (bf16[8,32,1024]{2,1,0:T(8,128)(2,1)S(1)}, bf16[8,32,1024]{2,1,0:T(8,128)(2,1)}, u32[]{:S(2)}) copy-start(bf16[8,32,1024]{2,1,0:T(8,128)(2,1)} %get-tuple-element.173) | copy-start | bytes 1572868
  (12 other events, 18.5 us)
Sparse Core Ops, SparseCore 0:
  312.7 267.2 all-reduce.39
  608.3 356.3 all-gather.6
  973.6 353.9 all-gather.8
  1332.8 354.2 all-gather.10
where the time goes:
time: 1720 us; the launch traced here: 1710 us
  waiting for transfers between devices  1250 us (73%)
  local copies, waits for them, and re-layouts  210 us (12%)
  matrix products  118 us (7%)
  blocking collectives  74.9 us (4%)
  loops' own time  17.7 us (1%)
  between operations  17.5 us (1%)
    all_gather x3, waiting for transfers between devices, body(): lax.all_gather(own_rows, 'space', axis=0, tiled=True)  973 us
    psum x1, waiting for transfers between devices, body(): lax.psum((sums[0], sums[1], sums[2]), ('dp', 'space'))  267 us
    while x464, local copies, waits for them, and re-layouts  128 us
    psum x1, blocking collectives, body(): lax.psum((sums[0], sums[1], sums[2]), ('dp', 'space'))  74.9 us
    dot_general x8, matrix products, step(): lax.dot_general(act_patch, act_patch, contract, preferred_element_type=jn...  42.7 us
  transfers between devices with their start and end apart: 6, of which 6 were waited for; matrix products, arithmetic and copies ran while one was open for 1% of the time, Pallas kernels for 0%

commit v1 on v0

v1 whole, which is shorter than its diff:
```python
import functools

import jax
import jax.numpy as jnp
from jax import lax
from jax.experimental import pallas as pl
from jax.experimental.pallas import tpu as pltpu
from jax.sharding import Mesh
from jax.sharding import PartitionSpec as P

ITERS = 3
DAMPING = 0.1
C = 32
PLANES = 4
ROWS = 16
LANES = 128
RPAD = ROWS + 4
TAPS = 3 * C
ORDER = 27 * C
WIDE = 9 * LANES
CELLS = 2097152
MIB = 1024 * 1024
NT = (((1,), (1,)), ((), ()))
f32 = jnp.float32
bf16 = jnp.bfloat16


CLASSES = []
for _x in ("0", "f", "l"):
    for _y in ("0", "f", "l", 1, 2):
        CLASSES.append((_x, _y))
for _x in (1, 2):
    for _y in ("0", "f", "l", 1, 2, -1, -2):
        CLASSES.append((_x, _y))
SLOT = {key: index for index, key in enumerate(CLASSES)}
GRAD = 27
BLOCKS = 32
HALF = BLOCKS // 2


def lane(row):
    return row * LANES


def fill_taps(dst, col, plane, rows=ROWS):
    flat = plane.reshape(rows * C, LANES)
    wide = flat.astype(f32)
    at = lax.broadcasted_iota(jnp.int32, wide.shape, 1)
    before = jnp.where(at == 0, 0.0, pltpu.roll(wide, 1, 1)).astype(bf16)
    after = jnp.where(at == LANES - 1, 0.0, pltpu.roll(wide, LANES - 1, 1)).astype(bf16)
    for y in range(rows):
        here = pl.ds(col + lane(y), LANES)
        part = slice(y * C, (y + 1) * C)
        dst[0:C, here] = before[part]
        dst[C : 2 * C, here] = flat[part]
        dst[2 * C : 3 * C, here] = after[part]


def fill_rows(dst, col, plane):
    for y in range(ROWS):
        dst[:, pl.ds(col + lane(y), LANES)] = plane[y]


def zero_rows(dst, col):
    zero = jnp.zeros((dst.shape[0], 2 * LANES), dst.dtype)
    dst[:, pl.ds(col, 2 * LANES)] = zero
    dst[:, pl.ds(col + lane(ROWS + 2), 2 * LANES)] = zero


def plane_at(index, row=0):
    return lane(index * RPAD + 2 + row)


def dot_nt(left, right):
    return lax.dot_general(left, right, NT, preferred_element_type=f32)


WIDTH = ROWS * LANES


def shifted(ref, index, rows, width=WIDTH):
    return jnp.concatenate([ref[:, pl.ds(plane_at(index, dy), width)] for dy in rows], 0)


A_P0, A_P3, A_X0 = 0, 5, 10
A_X1, A_X2 = 15, 22
A_BLOCKS = 29


def gram_inner(act_ref, cot_ref, out_ref, wg_ref, taps, cots):
    for x in range(PLANES):
        col = lane(x * RPAD)
        zero_rows(taps, col)
        zero_rows(cots, col)
        fill_taps(taps, plane_at(x), act_ref[x])
        fill_rows(cots, plane_at(x), cot_ref[x])

    def put(slot, value):
        out_ref[slot] = value

    def blocks(value, count):
        return [value[i * TAPS : (i + 1) * TAPS] for i in range(count)]

    near = (-1, 0, 1)
    sums = {}

    def add(key, value):
        sums[key] = value if key not in sums else sums[key] + value

    for x in range(PLANES):
        stay = jnp.concatenate(
            [taps[:, pl.ds(plane_at(x), WIDTH)], cots[:, pl.ds(plane_at(x), WIDTH)]], 0
        )
        level = dot_nt(shifted(taps, x, (0, 1, 2)), stay)
        zero, one, two = blocks(level, 3)
        cot_rows = [dot_nt(shifted(cots, x, near), stay)]
        if x + 1 < PLANES:
            up = dot_nt(shifted(taps, x + 1, (0, 1, 2, -1, -2)), stay)
            add("x1", up)
            cot_rows.append(dot_nt(shifted(cots, x + 1, near), stay))
            add("w2", cot_rows[1])
        if x >= 1:
            add("w0", dot_nt(shifted(cots, x - 1, near), stay))
        add("w1", cot_rows[0])
        if x + 2 < PLANES:
            add("x2", dot_nt(shifted(taps, x + 2, (0, 1, 2, -1, -2)), stay))
        edge = {}
        for name, row in (("F", 0), ("L", ROWS - 1)):
            stay_row = taps[:, pl.ds(plane_at(x, row), LANES)]
            count = min(3, PLANES - x)
            moving = jnp.concatenate(
                [taps[:, pl.ds(plane_at(x + i, row), LANES)] for i in range(count)], 0
            )
            edge_sum = blocks(jnp.pad(dot_nt(moving, stay_row), ((0, 0), (0, C))), count)
            edge[name] = edge_sum[0]
            for i in range(1, count):
                add((name, i), edge_sum[i])
        for i, value in enumerate((zero, edge["F"], edge["L"], one, two)):
            add(("level", i), value)
            if x == 0:
                put(A_P0 + i, value)
            if x == PLANES - 1:
                put(A_P3 + i, value)
    for i in range(5):
        put(A_X0 + i, sums[("level", i)])
    for base, name, i in ((A_X1, "x1", 1), (A_X2, "x2", 2)):
        whole = blocks(sums[name], 5)
        for j, value in enumerate((whole[0], sums[("F", i)], sums[("L", i)], *whole[1:])):
            put(base + j, value)
    wg_ref[0] = sums["w2"]
    wg_ref[1] = sums["w1"]
    wg_ref[2] = sums["w0"]


def gram_outer(
    core_ref, first_ref, last_ref, in_ref, wg_ref, act_ref, low_ref, high_ref, cot_ref,
    keep_ref, send_ref, taps, cots, out_ref,
):
    for index in range(6):
        zero_rows(taps, lane(index * RPAD))
        if index in (0, 2, 3, 4, 5):
            plane = low_ref[0] if index == 0 else high_ref[0] if index == 5 else act_ref[index - 1]
            fill_taps(taps, plane_at(index), plane)
    for slot, x in ((0, 0), (1, 3)):
        zero_rows(cots, lane(slot * RPAD))
        fill_rows(cots, plane_at(slot), cot_ref[x])

    def stay(index):
        return taps[:, pl.ds(plane_at(index), WIDTH)]

    five = (0, 1, 2, -1, -2)
    near = (-1, 0, 1)
    own = core_ref[0]
    first = first_ref[0].astype(f32)
    last = last_ref[0].astype(f32)

    def blocks(value, count):
        return [value[i * TAPS : (i + 1) * TAPS] for i in range(count)]

    def padded(value):
        return jnp.concatenate([value, jnp.zeros((value.shape[0], LANES - TAPS), f32)], 1)

    low = stay(0)
    gap = jnp.zeros((LANES - TAPS, WIDTH), bf16)
    top = dot_nt(shifted(taps, 5, five), jnp.concatenate([stay(4), gap, stay(3), gap], 0))
    x1 = blocks(top[:, :LANES], 5)
    x2 = blocks(top[:, LANES:] + dot_nt(shifted(taps, 2, five), jnp.concatenate([low, gap], 0)), 5)
    w_low = dot_nt(shifted(cots, 0, near), low)
    w_high = dot_nt(shifted(cots, 1, near), stay(5))

    def edge(left, right, row):
        return padded(dot_nt(
            taps[:, pl.ds(plane_at(left, row), LANES)], taps[:, pl.ds(plane_at(right, row), LANES)]
        ))

    wide = jnp.zeros((TAPS, LANES - TAPS), f32)
    wsums = (
        wg_ref[0] + jnp.concatenate([w_low, wide], 1),
        wg_ref[1],
        wg_ref[2] + jnp.concatenate([w_high, wide], 1),
    )
    at = lax.broadcasted_iota(jnp.int32, (TAPS, LANES), 1)

    def piece(t):
        if t > GRAD:
            return jnp.zeros((C, LANES), f32)
        if t == GRAD:
            return wsums[1][C : 2 * C]
        a, b, c = t // 9, t // 3 % 3, t % 3
        return pltpu.roll(wsums[a][(2 - b) * C : (3 - b) * C], TAPS - c * C, 1)

    def put(slot, value):
        extra = piece(slot)
        high = extra.astype(bf16).astype(f32)
        extra = jnp.concatenate([high, extra - high, jnp.zeros((C, LANES), f32)], 0)
        out_ref[(slot // HALF) ^ own, slot % HALF] = jnp.where(at < TAPS, value, extra).astype(bf16)

    def cut(value):
        return value

    for base, dx, parts, pairs in (
        (A_X1, 1, x1, ((5, 4),)),
        (A_X2, 2, x2, ((5, 3), (2, 0))),
    ):
        whole = cut(in_ref[base]) + parts[0]
        put(SLOT[(dx, "0")], whole)
        for j, (name, row) in enumerate((("f", 0), ("l", ROWS - 1))):
            edge_sum = cut(in_ref[base + 1 + j])
            for left, right in pairs:
                edge_sum = edge_sum + edge(left, right, row)
            put(SLOT[(dx, name)], whole - edge_sum)
        for j, dy in enumerate((1, 2, -1, -2)):
            put(SLOT[(dx, dy)], cut(in_ref[base + 3 + j]) + parts[1 + j])
    for name in ("0", "f", "l"):
        values = [cut(in_ref[A_X0 + i]) for i in range(5)]
        if name == "f":
            values = [v - first * cut(in_ref[A_P0 + i]) for i, v in enumerate(values)]
        if name == "l":
            values = [v - last * cut(in_ref[A_P3 + i]) for i, v in enumerate(values)]
        put(SLOT[(name, "0")], values[0])
        put(SLOT[(name, "f")], values[0] - values[1])
        put(SLOT[(name, "l")], values[0] - values[2])
        put(SLOT[(name, 1)], values[3])
        put(SLOT[(name, 2)], values[4])
    for slot in range(len(CLASSES), BLOCKS):
        put(slot, jnp.zeros((TAPS, LANES), f32))
    keep_ref[...] = out_ref[0]
    send_ref[...] = out_ref[1]


def settle(value):
    at = lax.broadcasted_iota(jnp.int32, (C, LANES), 1)
    first, second = value[:C], value[C : 2 * C]
    both = first + second
    high = both.astype(bf16).astype(f32)
    first = jnp.where(at < TAPS, first, high)
    second = jnp.where(at < TAPS, second, both - high)
    return jnp.concatenate([first, second, value[2 * C :]], 0).astype(bf16)


def add_kernel(keep_ref, arrived_ref, out_ref):
    for i in range(HALF):
        out_ref[i] = settle(keep_ref[i].astype(f32) + arrived_ref[i].astype(f32))


def sum_kernel(parts_ref, out_ref):
    total = parts_ref[0].astype(f32)
    for i in range(1, parts_ref.shape[0]):
        total = total + parts_ref[i].astype(f32)
    total = settle(total)
    for i in range(out_ref.shape[0]):
        out_ref[i] = total


def conv_kernel(which, x_ref, low_ref, high_ref, w_ref, out_ref, taps):
    for index in range(PLANES + 2):
        zero_rows(taps, lane(index * RPAD))
        plane = low_ref[which] if index == 0 else high_ref[which] if index == PLANES + 1 else x_ref[index - 1]
        fill_taps(taps, plane_at(index), plane)
    weight = w_ref[...]
    step = 2
    for x in range(PLANES):
        for y in range(0, ROWS, step):
            patch = jnp.concatenate(
                [
                    taps[:, pl.ds(plane_at(x + 1 + dx, y + dy), step * LANES)]
                    for dx in (-1, 0, 1)
                    for dy in (-1, 0, 1)
                ],
                0,
            )
            value = jnp.dot(weight, patch, preferred_element_type=f32).astype(bf16)
            for i in range(step):
                out_ref[x, y + i] = value[:, lane(i) : lane(i + 1)]


def split(value):
    high = value.astype(bf16)
    return high, (value - high.astype(f32)).astype(bf16)


def class_of(offset):
    return {0: "0", 1: "f", -1: "l"}[offset]


def finish_kernel(core_ref, mine_ref, other_ref, out_ref, both, factor):
    own = core_ref[0]
    both[own] = mine_ref[...]
    both[1 - own] = other_ref[...]

    def block(slot):
        return both[slot // HALF, slot % HALF]

    at = lax.broadcasted_iota(jnp.int32, (TAPS, LANES), 1)
    offsets = [(a, b) for a in (-1, 0, 1) for b in (-1, 0, 1)]
    tail = jnp.zeros((LANES - TAPS, LANES), bf16)
    cache = {}

    def padded(slot):
        if slot not in cache:
            value = jnp.where(at < TAPS, block(slot), jnp.zeros((), bf16))
            full = jnp.concatenate([value, tail], 0)
            cache[slot] = (full, full.T)
        return cache[slot]

    for i, (ax, ay) in enumerate(offsets):
        for j, (bx, by) in enumerate(offsets):
            dx, dy = bx - ax, by - ay
            if dx < 0 or (dx == 0 and dy < 0):
                continue
            key = (class_of(ax) if dx == 0 else dx, class_of(ay) if dy == 0 else dy)
            full, turned = padded(SLOT[key])
            factor[lane(j) : lane(j + 1), lane(i) : lane(i + 1)] = full
            if i != j:
                factor[lane(i) : lane(i + 1), lane(j) : lane(j + 1)] = turned

    def extra(t):
        here = both.at[t // HALF, t % HALF]
        return here[0:C, :].astype(f32) + here[C : 2 * C, :].astype(f32)

    pieces = []
    for i in range(9):
        rows = jnp.zeros((C, LANES), f32)
        for c in range(3):
            moved = pltpu.roll(extra(3 * i + c), C + c * C, 1)
            rows = jnp.where(at[:C] // C == c, moved, rows)
        pieces.append(rows)
    wgrad = jnp.concatenate(pieces, 1) * (1.0 / CELLS)

    grad = extra(GRAD)[:, TAPS:LANES]
    row_id = lax.broadcasted_iota(jnp.int32, (C, C), 0)
    col_id = lax.broadcasted_iota(jnp.int32, (C, C), 1)
    eye = jnp.where(row_id == col_id, 1.0, 0.0).astype(f32)
    scaled = grad * (C / jnp.sum(grad * eye)) + DAMPING * eye
    bound = jnp.max(jnp.sum(jnp.abs(scaled), axis=1))
    inverse = eye / bound
    for _ in range(ITERS):
        half = jnp.dot(inverse, scaled, precision=lax.Precision.HIGHEST, preferred_element_type=f32)
        inverse = 2.0 * inverse - jnp.dot(
            half, inverse, precision=lax.Precision.HIGHEST, preferred_element_type=f32
        )

    trace = jnp.zeros((), f32)
    sums = jnp.zeros((1, WIDE), f32)
    diag_row = lax.broadcasted_iota(jnp.int32, (LANES, LANES), 0)
    diag_col = lax.broadcasted_iota(jnp.int32, (LANES, LANES), 1)
    diagonal = jnp.zeros((LANES, LANES), f32)
    for i in range(9):
        rows = factor[lane(i) : lane(i + 1), :].astype(f32)
        sums = sums + jnp.sum(jnp.abs(rows), axis=0, keepdims=True)
        diagonal = diagonal + jnp.where(diag_row == diag_col, rows[:, lane(i) : lane(i + 1)], 0.0)
    trace = jnp.sum(diagonal)
    scale = ORDER / trace
    bound = scale * jnp.max(sums) + DAMPING
    step = scale / bound
    keep = 1.0 - DAMPING / bound
    value = wgrad
    for _ in range(2**ITERS - 1):
        high, low = split(value)
        product = jnp.dot(jnp.concatenate([high, low], 0), factor[...], preferred_element_type=f32)
        value = wgrad + keep * value - step * (product[:C] + product[C:])
    right = value * (1.0 / bound)
    applied = jnp.dot(inverse, right, precision=lax.Precision.HIGHEST, preferred_element_type=f32)
    quadratic = jnp.sum(applied * wgrad)
    result = applied * jnp.sqrt(C * ORDER / quadratic)
    out_ref[...] = jnp.concatenate([result[:, lane(i) : lane(i) + TAPS] for i in range(9)], 1)


SMEM = pl.BlockSpec(memory_space=pltpu.SMEM)
WHOLE = pl.BlockSpec(memory_space=pltpu.VMEM)


def call(kernel, shapes, scratch, inputs, scalars=0, flops=0, mib=16):
    return pl.pallas_call(
        kernel,
        out_shape=shapes,
        in_specs=[SMEM] * scalars + [WHOLE] * (len(inputs) - scalars),
        out_specs=jax.tree.map(lambda _: WHOLE, shapes),
        scratch_shapes=scratch,
        compiler_params=pltpu.CompilerParams(vmem_limit_bytes=mib * MIB),
        cost_estimate=pl.CostEstimate(flops=flops, bytes_accessed=1 << 20, transcendentals=0),
    )(*inputs)


def conv(which, planes, low, high, weight):
    return call(
        functools.partial(conv_kernel, which),
        jax.ShapeDtypeStruct(planes.shape, bf16),
        [pltpu.VMEM((TAPS, 6 * RPAD * LANES), bf16)],
        (planes, low, high, weight),
        flops=2 * C * ORDER * PLANES * ROWS * LANES,
    )


def body(activations, cotangent, weight):
    space = ("y", "x", "z_lo")
    size = lax.axis_size(space)
    up = [(i, i + 1) for i in range(size - 1)]
    down = [(j, i) for i, j in up]

    def outer_planes(x):
        pair = jnp.stack([activations[0, :, x], cotangent[0, :, x]], 0)
        return pair.transpose(0, 2, 1, 3)

    low = lax.ppermute(outer_planes(PLANES - 1), space, up)
    high = lax.ppermute(outer_planes(0), space, down)
    act = activations[0].transpose(1, 2, 0, 3)
    cot = cotangent[0].transpose(1, 2, 0, 3)
    where = lax.axis_index(space)
    core = lax.axis_index("core").astype(jnp.int32).reshape(1)
    first = (where == 0).astype(jnp.int32).reshape(1)
    last = (where == size - 1).astype(jnp.int32).reshape(1)

    sums, wsums = call(
        gram_inner,
        (
            jax.ShapeDtypeStruct((A_BLOCKS, TAPS, LANES), f32),
            jax.ShapeDtypeStruct((3, TAPS, LANES), f32),
        ),
        [
            pltpu.VMEM((TAPS, PLANES * RPAD * LANES), bf16),
            pltpu.VMEM((C, PLANES * RPAD * LANES), bf16),
        ],
        (act, cot),
        flops=24 * 10**9 // 4,
        mib=24,
    )
    blocks_half = jax.ShapeDtypeStruct((HALF, TAPS, LANES), bf16)
    keep, send = call(
        gram_outer,
        (blocks_half, blocks_half),
        [
            pltpu.VMEM((TAPS, 6 * RPAD * LANES), bf16),
            pltpu.VMEM((C, 2 * RPAD * LANES), bf16),
            pltpu.VMEM((2, HALF, TAPS, LANES), bf16),
        ],
        (core, first, last, sums, wsums, act, low, high, cot),
        scalars=3,
        flops=10**9,
        mib=24,
    )

    hold = lax.optimization_barrier
    swap = [(0, 1), (1, 0)]
    arrived = lax.ppermute(send, "core", swap)
    mine = call(add_kernel, blocks_half, [], (keep, arrived), mib=4)
    mine, act, low, high, weight = hold((mine, act, low, high, weight))
    parts = lax.all_to_all(mine, ("y", "x"), 0, 0, tiled=True)
    out = conv(0, act, low, high, weight)
    flipped = weight.reshape(C, 27, C)[:, ::-1, :].transpose(2, 1, 0).reshape(C, ORDER)
    parts, out, flipped = hold((parts, out, flipped))
    depth = lax.axis_size(("z_hi", "z_lo"))
    block = call(sum_kernel, jax.ShapeDtypeStruct((depth, TAPS, LANES), bf16), [], (parts,), mib=4)
    block, cot, low, high = hold((block, cot, low, high))
    parts = lax.all_to_all(block, ("z_hi", "z_lo"), 0, 0, tiled=True)
    back = conv(1, cot, low, high, flipped)
    parts, back = hold((parts, back))
    block = call(sum_kernel, blocks_half, [], (parts,), mib=4)
    block, out, back = hold((block, out, back))
    whole = lax.all_to_all(block, ("y", "x"), 0, 0, tiled=True)

    def arrange(planes):
        return planes.transpose(2, 0, 1, 3)[None]

    out, back = arrange(out), arrange(back)
    whole, out, back = hold((whole, out, back))
    other = lax.ppermute(whole, "core", swap)
    precond = call(
        finish_kernel,
        jax.ShapeDtypeStruct((C, ORDER), f32),
        [pltpu.VMEM((2, HALF, TAPS, LANES), bf16), pltpu.VMEM((WIDE, WIDE), bf16)],
        (core, whole, other),
        scalars=1,
        flops=10**9,
    )
    return out, back, precond


def solution(mesh):
    fine = Mesh(mesh.devices.reshape(2, 2, 4, 4, 4), ("z_hi", "core", "y", "x", "z_lo"))
    spec = P(("z_hi", "core"), None, ("y", "x", "z_lo"), None, None)
    return jax.shard_map(
        body,
        mesh=fine,
        in_specs=(spec, spec, P()),
        out_specs=(spec, spec, P()),
        check_vma=False,
    )
```

time: 1720 us -> 85.5 us (0.05)
  the two profiles are of different devices: /device:TPU:32 before, /device:TPU:1 now
where the time goes in v1:
time: 85.5 us; the launch traced here: 85.1 us
  starting transfers between devices  24.9 us (29%)
  waiting for transfers between devices  20.3 us (24%)
  Pallas kernels  20.2 us (24%)
  blocking collectives  11.1 us (13%)
  local copies, waits for them, and re-layouts  7.72 us (9%)
    pallas_call x8, Pallas kernels, call(): pl.pallas_call(kernel, out_shape=shapes, in_specs=[SMEM] * scalars + [WHO...  20.2 us
    all_to_all x1, blocking collectives, body(): whole = lax.all_to_all(block, ('y', 'x'), 0, 0, tiled=True)  11.1 us
    all_to_all x1, starting transfers between devices, body(): parts = lax.all_to_all(block, ('z_hi', 'z_lo'), 0, 0, tiled=True)  7.73 us
    ppermute x1, waiting for transfers between devices, body(): high = lax.ppermute(outer_planes(0), space, down)  7.02 us
    all_to_all x1, starting transfers between devices, body(): parts = lax.all_to_all(mine, ('y', 'x'), 0, 0, tiled=True)  6.75 us
    unnamed x9, local copies, waits for them, and re-layouts  6.47 us
    all_to_all x1, waiting for transfers between devices, body(): parts = lax.all_to_all(block, ('z_hi', 'z_lo'), 0, 0, tiled=True)  6.17 us
    all_to_all x1, waiting for transfers between devices, body(): parts = lax.all_to_all(mine, ('y', 'x'), 0, 0, tiled=True)  5.76 us
  transfers between devices with their start and end apart: 6, of which 4 were waited for; matrix products, arithmetic and copies ran while one was open for 4% of the time, Pallas kernels for 12%

profile of v1, /device:TPU:1, one launch (start us, length us, event | category | flops | bytes accessed | tf_op | source)
XLA Modules:
  0.0 85.1 jit_solution(6363062966173140780)
XLA Ops:
  0.6 2.0 %fusion = (bf16[1,32,4,16,128]{4,1,3,2,0:T(8,128)(2,1)S(1)}, bf16[4,16,32,128]{3,2,1,0:T(8,128)(2,1)S(1)}, bf16[4,16,32,128]{3,2,1,0:T(8,128)(2,1)S(1)}, bf16[1,32,4,16,128]{4,1,3,2,0:T(8,128)(2,1)S(1)}) fusion(bf16[1,32,4,16,128]{4,3,2,1,0:T(8,128)(2,1)} %param.3, bf16[1,32,4,16,128]{4,3,2,1,0:T(8,128)(2,1)} %param.4), kind=kLoop, calls=%fused_computation.8 | loop fusion | bytes 3145728 | tf_op args[0]
  2.7 4.4 %collective-permute-start = (bf16[2,16,32,128]{3,2,1,0:T(8,128)(2,1)S(1)}, bf16[2,16,32,128]{3,2,1,0:T(8,128)(2,1)S(1)}, u32[]{:S(2)}, u32[]{:S(2)}) collective-permute-start(bf16[2,16,32,128]{3,2,1,0:T(8,128)(2,1)S(1)} %maximum_bitcast_fusion), channel_id=1, source_target_pairs={{0,1},{1,2},{2,3},{3,4},{4,5},{5,6},{6,7},{7,8},{8,9},{9,10},{10,1... | collective-permute-start | bytes 786440 | tf_op jit(solution)/shard_map/ppermute | solution.py:425
  7.2 1.3 %collective-permute-start.1 = (bf16[2,16,32,128]{3,2,1,0:T(8,128)(2,1)S(1)}, bf16[2,16,32,128]{3,2,1,0:T(8,128)(2,1)S(1)}, u32[]{:S(2)}, u32[]{:S(2)}) collective-permute-start(bf16[2,16,32,128]{3,2,1,0:T(8,128)(2,1)S(1)} %maximum_bitcast_fusion.1), channel_id=1, source_target_pairs={{1,0},{2,1},{3,2},{4,3},{5,4},{6,5},{7,6},{8,7},{9,8},{10,9},{11,1... | collective-permute-start | bytes 786440 | tf_op jit(solution)/shard_map/ppermute | solution.py:426
  8.5 5.6 %shard_map.58 = (f32[29,96,128]{2,1,0:T(8,128)S(1)}, f32[3,96,128]{2,1,0:T(8,128)S(1)}) custom-call(bf16[4,16,32,128]{3,2,1,0:T(8,128)(2,1)S(1)} %get-tuple-element.32.act_ref.x_ref, bf16[4,16,32,128]{3,2,1,0:T(8,128)(2,1)S(1)} %get-tuple-element.38.cot_ref.x_ref), custom_call_target="tpu_custom_call" | custom-call | flops 6000000000 | bytes 1048576 | tf_op jit(solution)/shard_map/pallas_call | solution.py:394
  14.1 1.1 %copy-done.1 = f32[29,96,128]{2,1,0:T(8,128)} copy-done((f32[29,96,128]{2,1,0:T(8,128)}, f32[29,96,128]{2,1,0:T(8,128)S(1)}, u32[]{:S(2)}) %copy-start.1) | copy-done | bytes 1425432
  15.2 7.0 %collective-permute-done.1.high_ref = bf16[2,16,32,128]{3,2,1,0:T(8,128)(2,1)S(1)} collective-permute-done((bf16[2,16,32,128]{3,2,1,0:T(8,128)(2,1)S(1)}, bf16[2,16,32,128]{3,2,1,0:T(8,128)(2,1)S(1)}, u32[]{:S(2)}, u32[]{:S(2)}) %collective-permute-start.1) | collective-permute-done | bytes 262176 | tf_op jit(solution)/shard_map/ppermute | solution.py:426
  22.2 1.4 %copy-done.2 = f32[29,96,128]{2,1,0:T(8,128)S(1)} copy-done((f32[29,96,128]{2,1,0:T(8,128)S(1)}, f32[29,96,128]{2,1,0:T(8,128)}, u32[]{:S(2)}) %copy-start.2) | copy-done | bytes 1425432
  23.6 1.7 %shard_map.59 = (bf16[16,96,128]{2,1,0:T(8,128)(2,1)S(1)}, bf16[16,96,128]{2,1,0:T(8,128)(2,1)S(1)}) custom-call(s32[1]{0:T(128)} %bitcast.core_ref, s32[1]{0:T(128)} %bitcast.1.first_ref, s32[1]{0:T(128)} %bitcast.2.last_ref, f32[29,96,128]{2,1,0:T(8,128)S(1)} %copy-done.2, f32[3,96,128]{2,1,0:T(8,128)S(1)} %get-tuple-element.28.wg_ref, ...), custom_call_target="tpu_custom_call" | custom-call | flops 1000000000 | bytes 1048576 | tf_op jit(solution)/shard_map/pallas_call | solution.py:394
  25.3 0.6 collective-permute-start.2
  25.9 1.3 %collective-permute-done.2.arrived_ref = bf16[16,96,128]{2,1,0:T(8,128)(2,1)S(1)} collective-permute-done((bf16[16,96,128]{2,1,0:T(8,128)(2,1)S(1)}, bf16[16,96,128]{2,1,0:T(8,128)(2,1)S(1)}, u32[]{:S(2)}, u32[]{:S(2)}) %collective-permute-start.2) | collective-permute-done | bytes 393248 | tf_op jit(solution)/shard_map/ppermute | solution.py:465
  27.2 0.9 %shard_map.60 = bf16[16,96,128]{2,1,0:T(8,128)(2,1)} custom-call(bf16[16,96,128]{2,1,0:T(8,128)(2,1)S(1)} %get-tuple-element.29.keep_ref, bf16[16,96,128]{2,1,0:T(8,128)(2,1)S(1)} %collective-permute-done.2.arrived_ref), custom_call_target="tpu_custom_call" | custom-call | bytes 1048576 | tf_op jit(solution)/shard_map/pallas_call | solution.py:394
  28.1 6.8 %all-to-all-start = ((bf16[16,96,128]{2,1,0:T(8,128)(2,1)}), bf16[16,96,128]{2,1,0:T(8,128)(2,1)S(1)}, u32[]{:S(2)}, u32[]{:S(2)}) async-start(bf16[16,96,128]{2,1,0:T(8,128)(2,1)} %shard_map.60), calls=%async_computation | async-start | bytes 786432 | tf_op jit(solution)/shard_map/all_to_all | solution.py:468
  35.3 0.6 copy.21
  36.1 2.5 %shard_map.61 = bf16[4,16,32,128]{3,2,1,0:T(8,128)(2,1)S(1)} custom-call(bf16[4,16,32,128]{3,2,1,0:T(8,128)(2,1)S(1)} %get-tuple-element.32.act_ref.x_ref, bf16[2,16,32,128]{3,2,1,0:T(8,128)(2,1)S(1)} %collective-permute-done.low_ref, bf16[2,16,32,128]{3,2,1,0:T(8,128)(2,1)S(1)} %collective-permute-done.1.high_ref, bf16[32,864]{1,0:T(8,128)(2,1)S(1)} %copy-done), custom_call_target="tpu_custom_call" | custom-call | flops 452984832 | bytes 1048576 | tf_op jit(solution)/shard_map/pallas_call | solution.py:394
  38.6 5.8 %all-to-all-done.parts_ref = bf16[16,96,128]{2,1,0:T(8,128)(2,1)S(1)} async-done(((bf16[16,96,128]{2,1,0:T(8,128)(2,1)}), bf16[16,96,128]{2,1,0:T(8,128)(2,1)S(1)}, u32[]{:S(2)}, u32[]{:S(2)}) %all-to-all-start) | async-done | bytes 393248 | tf_op jit(solution)/shard_map/all_to_all | solution.py:468
  44.4 0.7 shard_map.62
  45.1 7.7 %all-to-all-start.1 = ((bf16[8,96,128]{2,1,0:T(8,128)(2,1)}), bf16[8,96,128]{2,1,0:T(8,128)(2,1)S(1)}, u32[]{:S(2)}, u32[]{:S(2)}) async-start(bf16[8,96,128]{2,1,0:T(8,128)(2,1)} %shard_map.62), calls=%async_computation.1 | async-start | bytes 393216 | tf_op jit(solution)/shard_map/all_to_all | solution.py:475
  52.8 2.5 %shard_map.63 = bf16[4,16,32,128]{3,2,1,0:T(8,128)(2,1)S(1)} custom-call(bf16[4,16,32,128]{3,2,1,0:T(8,128)(2,1)S(1)} %get-tuple-element.38.cot_ref.x_ref, bf16[2,16,32,128]{3,2,1,0:T(8,128)(2,1)S(1)} %collective-permute-done.low_ref, bf16[2,16,32,128]{3,2,1,0:T(8,128)(2,1)S(1)} %collective-permute-done.1.high_ref, bf16[32,864]{1,0:T(8,128)(2,1)S(1)} %reshape.31.w_ref), custom_call_target="tpu_custom_call" | custom-call | flops 452984832 | bytes 1048576 | tf_op jit(solution)/shard_map/pallas_call | solution.py:394
  55.4 6.2 %all-to-all-done.1.parts_ref = bf16[8,96,128]{2,1,0:T(8,128)(2,1)S(1)} async-done(((bf16[8,96,128]{2,1,0:T(8,128)(2,1)}), bf16[8,96,128]{2,1,0:T(8,128)(2,1)S(1)}, u32[]{:S(2)}, u32[]{:S(2)}) %all-to-all-start.1) | async-done | bytes 196640 | tf_op jit(solution)/shard_map/all_to_all | solution.py:475
  61.6 11.1 %all_to_all.15.mine_ref = bf16[16,96,128]{2,1,0:T(8,128)(2,1)S(1)} all-to-all(bf16[16,96,128]{2,1,0:T(8,128)(2,1)S(1)} %shard_map.64), channel_id=1, replica_groups=mesh['z_hi'=2,'core'=2,'y'=4,'x'=4,'z_lo'=4] {'y','x'}, dimensions={0} | all-to-all | bytes 786432 | tf_op jit(solution)/shard_map/all_to_all | solution.py:480
  72.7 4.1 %collective-permute-start.3 = (bf16[16,96,128]{2,1,0:T(8,128)(2,1)S(1)}, bf16[16,96,128]{2,1,0:T(8,128)(2,1)S(1)}, u32[]{:S(2)}, u32[]{:S(2)}) collective-permute-start(bf16[16,96,128]{2,1,0:T(8,128)(2,1)S(1)} %all_to_all.15.mine_ref), channel_id=1, source_target_pairs={{0,64},{64,0},{1,65},{65,1},{2,66},{66,2},{3,67},{67,3},{4,68},{68... | collective-permute-start | bytes 1179656 | tf_op jit(solution)/shard_map/ppermute | solution.py:487
  76.9 1.0 %copy.22 = bf16[1,32,4,16,128]{4,3,2,1,0:T(8,128)(2,1)} copy(bf16[1,32,4,16,128]{4,1,3,2,0:T(8,128)(2,1)S(1)} %bitcast.30) | data formatting | bytes 1048576
  77.9 1.0 %copy.23 = bf16[1,32,4,16,128]{4,3,2,1,0:T(8,128)(2,1)} copy(bf16[1,32,4,16,128]{4,1,3,2,0:T(8,128)(2,1)S(1)} %bitcast.31) | data formatting | bytes 1048576
  78.9 6.2 %shard_map.65 = f32[32,864]{1,0:T(8,128)} custom-call(s32[1]{0:T(128)} %bitcast.core_ref, bf16[16,96,128]{2,1,0:T(8,128)(2,1)S(1)} %all_to_all.15.mine_ref, bf16[16,96,128]{2,1,0:T(8,128)(2,1)S(1)} %collective-permute-done.3.other_ref), custom_call_target="tpu_custom_call" | custom-call | flops 1000000000 | bytes 1048576 | tf_op jit(solution)/shard_map/pallas_call | solution.py:394
  (14 shorter events, 0.8 us)
Async XLA Ops:
  2.7 12.4 %collective-permute-start = (bf16[2,16,32,128]{3,2,1,0:T(8,128)(2,1)S(1)}, bf16[2,16,32,128]{3,2,1,0:T(8,128)(2,1)S(1)}, u32[]{:S(2)}, u32[]{:S(2)}) collective-permute-start(bf16[2,16,32,128]{3,2,1,0:T(8,128)(2,1)S(1)} %maximum_bitcast_fusion), channel_id=1, source_target_pairs={{0,1},{1,2},{2,3},{3,4},{4,5},{5,6},{6,7},{7,8},{8,9},{9,10},{10,1... | collective-permute-start | bytes 786440 | tf_op jit(solution)/shard_map/ppermute | solution.py:425
  7.2 15.0 %collective-permute-start.1 = (bf16[2,16,32,128]{3,2,1,0:T(8,128)(2,1)S(1)}, bf16[2,16,32,128]{3,2,1,0:T(8,128)(2,1)S(1)}, u32[]{:S(2)}, u32[]{:S(2)}) collective-permute-start(bf16[2,16,32,128]{3,2,1,0:T(8,128)(2,1)S(1)} %maximum_bitcast_fusion.1), channel_id=1, source_target_pairs={{1,0},{2,1},{3,2},{4,3},{5,4},{6,5},{7,6},{8,7},{9,8},{10,9},{11,1... | collective-permute-start | bytes 786440 | tf_op jit(solution)/shard_map/ppermute | solution.py:426
  14.1 1.1 %copy-start.1 = (f32[29,96,128]{2,1,0:T(8,128)}, f32[29,96,128]{2,1,0:T(8,128)S(1)}, u32[]{:S(2)}) copy-start(f32[29,96,128]{2,1,0:T(8,128)S(1)} %get-tuple-element.27.in_ref) | copy-start | bytes 4276228
  22.2 1.4 %copy-start.2 = (f32[29,96,128]{2,1,0:T(8,128)S(1)}, f32[29,96,128]{2,1,0:T(8,128)}, u32[]{:S(2)}) copy-start(f32[29,96,128]{2,1,0:T(8,128)} %copy-done.1) | copy-start | bytes 4276228
  25.3 9.6 %copy-start = (bf16[32,864]{1,0:T(8,128)(2,1)S(1)}, bf16[32,864]{1,0:T(8,128)(2,1)}, u32[]{:S(2)}) copy-start(bf16[32,864]{1,0:T(8,128)(2,1)} %w_ref) | copy-start | bytes 165892
  25.3 1.9 %collective-permute-start.2 = (bf16[16,96,128]{2,1,0:T(8,128)(2,1)S(1)}, bf16[16,96,128]{2,1,0:T(8,128)(2,1)S(1)}, u32[]{:S(2)}, u32[]{:S(2)}) collective-permute-start(bf16[16,96,128]{2,1,0:T(8,128)(2,1)S(1)} %get-tuple-element.30), channel_id=1, source_target_pairs={{0,64},{64,0},{1,65},{65,1},{2,66},{66,2},{3,67},{67,3},{4,68},{68... | collective-permute-start | bytes 1179656 | tf_op jit(solution)/shard_map/ppermute | solution.py:465
  28.1 16.3 %all-to-all-start = ((bf16[16,96,128]{2,1,0:T(8,128)(2,1)}), bf16[16,96,128]{2,1,0:T(8,128)(2,1)S(1)}, u32[]{:S(2)}, u32[]{:S(2)}) async-start(bf16[16,96,128]{2,1,0:T(8,128)(2,1)} %shard_map.60), calls=%async_computation | async-start | bytes 786432 | tf_op jit(solution)/shard_map/all_to_all | solution.py:468
  45.1 16.4 %all-to-all-start.1 = ((bf16[8,96,128]{2,1,0:T(8,128)(2,1)}), bf16[8,96,128]{2,1,0:T(8,128)(2,1)S(1)}, u32[]{:S(2)}, u32[]{:S(2)}) async-start(bf16[8,96,128]{2,1,0:T(8,128)(2,1)} %shard_map.62), calls=%async_computation.1 | async-start | bytes 393216 | tf_op jit(solution)/shard_map/all_to_all | solution.py:475
  72.7 6.1 %collective-permute-start.3 = (bf16[16,96,128]{2,1,0:T(8,128)(2,1)S(1)}, bf16[16,96,128]{2,1,0:T(8,128)(2,1)S(1)}, u32[]{:S(2)}, u32[]{:S(2)}) collective-permute-start(bf16[16,96,128]{2,1,0:T(8,128)(2,1)S(1)} %all_to_all.15.mine_ref), channel_id=1, source_target_pairs={{0,64},{64,0},{1,65},{65,1},{2,66},{66,2},{3,67},{67,3},{4,68},{68... | collective-permute-start | bytes 1179656 | tf_op jit(solution)/shard_map/ppermute | solution.py:487

commit v2 on v1

--- a/solution.py
+++ b/solution.py
@@ -20,6 +20,7 @@
 WIDE = 9 * LANES
 CELLS = 2097152
 MIB = 1024 * 1024
+MIB_INNER, MIB_OUTER = 16, 16
 NT = (((1,), (1,)), ((), ()))
 f32 = jnp.float32
 bf16 = jnp.bfloat16
@@ -42,23 +43,29 @@
     return row * LANES
 
 
-def fill_taps(dst, col, plane, rows=ROWS):
-    flat = plane.reshape(rows * C, LANES)
-    wide = flat.astype(f32)
-    at = lax.broadcasted_iota(jnp.int32, wide.shape, 1)
-    before = jnp.where(at == 0, 0.0, pltpu.roll(wide, 1, 1)).astype(bf16)
-    after = jnp.where(at == LANES - 1, 0.0, pltpu.roll(wide, LANES - 1, 1)).astype(bf16)
-    for y in range(rows):
+def turned(plane, store):
+    store[...] = plane.astype(f32).reshape(C * ROWS, LANES)
+    return [store[pl.ds(y, C, stride=ROWS), :] for y in range(ROWS)]
+
+
+def rows_of(plane):
+    return [plane[y].astype(f32) for y in range(ROWS)]
+
+
+def fill_taps(dst, col, rows):
+    at = lax.broadcasted_iota(jnp.int32, (C, LANES), 1)
+    for y in range(ROWS):
         here = pl.ds(col + lane(y), LANES)
-        part = slice(y * C, (y + 1) * C)
-        dst[0:C, here] = before[part]
-        dst[C : 2 * C, here] = flat[part]
-        dst[2 * C : 3 * C, here] = after[part]
-
-
-def fill_rows(dst, col, plane):
+        before = jnp.where(at == 0, 0.0, pltpu.roll(rows[y], 1, 1))
+        after = jnp.where(at == LANES - 1, 0.0, pltpu.roll(rows[y], LANES - 1, 1))
+        dst[0:C, here] = before.astype(bf16)
+        dst[C : 2 * C, here] = rows[y].astype(bf16)
+        dst[2 * C : 3 * C, here] = after.astype(bf16)
+
+
+def fill_rows(dst, col, rows):
     for y in range(ROWS):
-        dst[:, pl.ds(col + lane(y), LANES)] = plane[y]
+        dst[:, pl.ds(col + lane(y), LANES)] = rows[y].astype(bf16)
 
 
 def zero_rows(dst, col):
@@ -87,13 +94,31 @@
 A_BLOCKS = 29
 
 
-def gram_inner(act_ref, cot_ref, out_ref, wg_ref, taps, cots):
+def gram_inner(
+    act_hbm, cot_hbm, out_ref, wg_ref, turned_act, turned_cot,
+    taps, cots, store, act_ref, cot_ref, sems,
+):
+    fetches = []
     for x in range(PLANES):
-        col = lane(x * RPAD)
-        zero_rows(taps, col)
-        zero_rows(cots, col)
-        fill_taps(taps, plane_at(x), act_ref[x])
-        fill_rows(cots, plane_at(x), cot_ref[x])
+        for i, (source, target) in enumerate(((act_hbm, act_ref), (cot_hbm, cot_ref))):
+            fetches.append(
+                pltpu.make_async_copy(source.at[:, x], target.at[x], sems.at[2 * x + i])
+            )
+    for fetch in fetches:
+        fetch.start()
+    for x in range(PLANES):
+        zero_rows(taps, lane(x * RPAD))
+        zero_rows(cots, lane(x * RPAD))
+    for x in range(PLANES):
+        fetches[2 * x].wait()
+        fetches[2 * x + 1].wait()
+        rows = turned(act_ref[x], store.at[2 * x])
+        fill_taps(taps, plane_at(x), rows)
+        cot_rows = turned(cot_ref[x], store.at[2 * x + 1])
+        fill_rows(cots, plane_at(x), cot_rows)
+        for y in range(ROWS):
+            turned_act[x, y] = rows[y].astype(bf16)
+            turned_cot[x, y] = cot_rows[y].astype(bf16)
 
     def put(slot, value):
         out_ref[slot] = value
@@ -153,17 +178,20 @@
 
 
 def gram_outer(
-    core_ref, first_ref, last_ref, in_ref, wg_ref, act_ref, low_ref, high_ref, cot_ref,
-    keep_ref, send_ref, taps, cots, out_ref,
+    core_ref, first_ref, last_ref, in_ref, wg_ref, act_ref, high_ref, cot_ref,
+    keep_ref, send_ref, taps, cots, out_ref, store,
 ):
-    for index in range(6):
+    for index in range(4):
         zero_rows(taps, lane(index * RPAD))
-        if index in (0, 2, 3, 4, 5):
-            plane = low_ref[0] if index == 0 else high_ref[0] if index == 5 else act_ref[index - 1]
-            fill_taps(taps, plane_at(index), plane)
-    for slot, x in ((0, 0), (1, 3)):
+        if index < 2:
+            rows = rows_of(act_ref[index + 2])
+        else:
+            rows = turned(high_ref[index - 2], store.at[index - 2])
+        fill_taps(taps, plane_at(index), rows)
+    for slot in range(2):
         zero_rows(cots, lane(slot * RPAD))
-        fill_rows(cots, plane_at(slot), cot_ref[x])
+    fill_rows(cots, plane_at(0), rows_of(cot_ref[PLANES - 1]))
+    fill_rows(cots, plane_at(1), turned(high_ref[2], store.at[2]))
 
     def stay(index):
         return taps[:, pl.ds(plane_at(index), WIDTH)]
@@ -180,13 +208,14 @@
     def padded(value):
         return jnp.concatenate([value, jnp.zeros((value.shape[0], LANES - TAPS), f32)], 1)
 
-    low = stay(0)
     gap = jnp.zeros((LANES - TAPS, WIDTH), bf16)
-    top = dot_nt(shifted(taps, 5, five), jnp.concatenate([stay(4), gap, stay(3), gap], 0))
-    x1 = blocks(top[:, :LANES], 5)
-    x2 = blocks(top[:, LANES:] + dot_nt(shifted(taps, 2, five), jnp.concatenate([low, gap], 0)), 5)
-    w_low = dot_nt(shifted(cots, 0, near), low)
-    w_high = dot_nt(shifted(cots, 1, near), stay(5))
+    two, three = stay(0), stay(1)
+    four = dot_nt(shifted(taps, 2, five), jnp.concatenate([three, gap, two, gap], 0))
+    beyond = dot_nt(shifted(taps, 3, five), jnp.concatenate([three, gap], 0))
+    x1 = blocks(four[:, :LANES], 5)
+    x2 = blocks(four[:, LANES:] + beyond, 5)
+    w_low = dot_nt(shifted(cots, 1, near), three)
+    w_high = dot_nt(shifted(cots, 0, near), stay(2))
 
     def edge(left, right, row):
         return padded(dot_nt(
@@ -219,8 +248,8 @@
         return value
 
     for base, dx, parts, pairs in (
-        (A_X1, 1, x1, ((5, 4),)),
-        (A_X2, 2, x2, ((5, 3), (2, 0))),
+        (A_X1, 1, x1, ((2, 1),)),
+        (A_X2, 2, x2, ((2, 0), (3, 1))),
     ):
         whole = cut(in_ref[base]) + parts[0]
         put(SLOT[(dx, "0")], whole)
@@ -272,14 +301,20 @@
         out_ref[i] = total
 
 
-def conv_kernel(which, x_ref, low_ref, high_ref, w_ref, out_ref, taps):
+def conv_kernel(which, x_ref, low_ref, high_ref, w_ref, out_ref, taps, store):
     for index in range(PLANES + 2):
         zero_rows(taps, lane(index * RPAD))
-        plane = low_ref[which] if index == 0 else high_ref[which] if index == PLANES + 1 else x_ref[index - 1]
-        fill_taps(taps, plane_at(index), plane)
+        if index == 0:
+            rows = turned(low_ref[which], store.at[PLANES])
+        elif index == PLANES + 1:
+            rows = turned(high_ref[2 * which], store.at[PLANES + 1])
+        else:
+            rows = rows_of(x_ref[index - 1])
+        fill_taps(taps, plane_at(index), rows)
     weight = w_ref[...]
     step = 2
     for x in range(PLANES):
+        plane = store.at[x]
         for y in range(0, ROWS, step):
             patch = jnp.concatenate(
                 [
@@ -289,9 +324,11 @@
                 ],
                 0,
             )
-            value = jnp.dot(weight, patch, preferred_element_type=f32).astype(bf16)
+            value = jnp.dot(weight, patch, preferred_element_type=f32)
             for i in range(step):
-                out_ref[x, y + i] = value[:, lane(i) : lane(i + 1)]
+                plane[(y + i) * C : (y + i + 1) * C, :] = value[:, lane(i) : lane(i + 1)]
+        for channel in range(C):
+            out_ref[channel, x] = plane[pl.ds(channel, ROWS, stride=C), :].astype(bf16)
 
 
 def split(value):
@@ -388,27 +425,67 @@
 
 SMEM = pl.BlockSpec(memory_space=pltpu.SMEM)
 WHOLE = pl.BlockSpec(memory_space=pltpu.VMEM)
-
-
-def call(kernel, shapes, scratch, inputs, scalars=0, flops=0, mib=16):
+IN_HBM = pl.BlockSpec(memory_space=pltpu.HBM)
+
+
+def call(kernel, shapes, scratch, inputs, scalars=0, flops=0, mib=16, specs=None, out_specs=None):
     return pl.pallas_call(
         kernel,
         out_shape=shapes,
-        in_specs=[SMEM] * scalars + [WHOLE] * (len(inputs) - scalars),
-        out_specs=jax.tree.map(lambda _: WHOLE, shapes),
+        in_specs=specs or [SMEM] * scalars + [WHOLE] * (len(inputs) - scalars),
+        out_specs=out_specs or jax.tree.map(lambda _: WHOLE, shapes),
         scratch_shapes=scratch,
         compiler_params=pltpu.CompilerParams(vmem_limit_bytes=mib * MIB),
         cost_estimate=pl.CostEstimate(flops=flops, bytes_accessed=1 << 20, transcendentals=0),
     )(*inputs)
 
 
+def edge_kernel(act, cot, down_out, up_out, down, up, sems):
+    hops = []
+    for k, (source, plane, buffer, target, slot) in enumerate((
+        (act, 0, down, down_out, 0),
+        (act, 1, down, down_out, 1),
+        (cot, 0, down, down_out, 2),
+        (act, PLANES - 1, up, up_out, 0),
+        (cot, PLANES - 1, up, up_out, 1),
+    )):
+        hops.append((
+            pltpu.make_async_copy(source.at[:, plane], buffer.at[slot], sems.at[2 * k]),
+            pltpu.make_async_copy(buffer.at[slot], target.at[slot], sems.at[2 * k + 1]),
+        ))
+    for fetch, _ in hops:
+        fetch.start()
+    for fetch, put in hops:
+        fetch.wait()
+        put.start()
+    for _, put in hops:
+        put.wait()
+
+
+def edge_planes(act, cot):
+    down, up = (3, C, ROWS, LANES), (2, C, ROWS, LANES)
+    return call(
+        edge_kernel,
+        (pltpu.HBM(down, bf16), pltpu.HBM(up, bf16)),
+        [pltpu.VMEM(down, bf16), pltpu.VMEM(up, bf16), pltpu.SemaphoreType.DMA((10,))],
+        (act, cot),
+        mib=4,
+        specs=[IN_HBM] * 2,
+        out_specs=(IN_HBM, IN_HBM),
+    )
+
+
 def conv(which, planes, low, high, weight):
     return call(
         functools.partial(conv_kernel, which),
-        jax.ShapeDtypeStruct(planes.shape, bf16),
-        [pltpu.VMEM((TAPS, 6 * RPAD * LANES), bf16)],
+        jax.ShapeDtypeStruct((C, PLANES, ROWS, LANES), bf16),
+        [
+            pltpu.VMEM((TAPS, 6 * RPAD * LANES), bf16),
+            pltpu.VMEM((PLANES + 2, C * ROWS, LANES), f32),
+        ],
         (planes, low, high, weight),
         flops=2 * C * ORDER * PLANES * ROWS * LANES,
+        mib=12,
     )
 
 
@@ -417,73 +494,71 @@
     size = lax.axis_size(space)
     up = [(i, i + 1) for i in range(size - 1)]
     down = [(j, i) for i, j in up]
-
-    def outer_planes(x):
-        pair = jnp.stack([activations[0, :, x], cotangent[0, :, x]], 0)
-        return pair.transpose(0, 2, 1, 3)
-
-    low = lax.ppermute(outer_planes(PLANES - 1), space, up)
-    high = lax.ppermute(outer_planes(0), space, down)
-    act = activations[0].transpose(1, 2, 0, 3)
-    cot = cotangent[0].transpose(1, 2, 0, 3)
+    hold = lax.optimization_barrier
+
+    act = pltpu.with_memory_space_constraint(activations[0], pltpu.HBM)
+    cot = pltpu.with_memory_space_constraint(cotangent[0], pltpu.HBM)
+    for_below, for_above = edge_planes(act, cot)
+    high = lax.ppermute(for_below, space, down)
     where = lax.axis_index(space)
     core = lax.axis_index("core").astype(jnp.int32).reshape(1)
     first = (where == 0).astype(jnp.int32).reshape(1)
     last = (where == size - 1).astype(jnp.int32).reshape(1)
 
-    sums, wsums = call(
+    turned_shape = pltpu.VMEM((PLANES, ROWS, C, LANES), bf16)
+    sums, wsums, turned_act, turned_cot = call(
         gram_inner,
         (
-            jax.ShapeDtypeStruct((A_BLOCKS, TAPS, LANES), f32),
-            jax.ShapeDtypeStruct((3, TAPS, LANES), f32),
+            pltpu.VMEM((A_BLOCKS, TAPS, LANES), f32),
+            pltpu.VMEM((3, TAPS, LANES), f32),
+            turned_shape,
+            turned_shape,
         ),
         [
             pltpu.VMEM((TAPS, PLANES * RPAD * LANES), bf16),
             pltpu.VMEM((C, PLANES * RPAD * LANES), bf16),
+            pltpu.VMEM((2 * PLANES, C * ROWS, LANES), f32),
+            pltpu.VMEM((PLANES, C, ROWS, LANES), bf16),
+            pltpu.VMEM((PLANES, C, ROWS, LANES), bf16),
+            pltpu.SemaphoreType.DMA((2 * PLANES,)),
         ],
         (act, cot),
+        specs=[IN_HBM] * 2,
         flops=24 * 10**9 // 4,
-        mib=24,
-    )
+        mib=MIB_INNER,
+    )
+    for_above, sums, wsums = hold((for_above, sums, wsums))
+    low = lax.ppermute(for_above, space, up)
     blocks_half = jax.ShapeDtypeStruct((HALF, TAPS, LANES), bf16)
     keep, send = call(
         gram_outer,
         (blocks_half, blocks_half),
         [
-            pltpu.VMEM((TAPS, 6 * RPAD * LANES), bf16),
+            pltpu.VMEM((TAPS, 4 * RPAD * LANES), bf16),
             pltpu.VMEM((C, 2 * RPAD * LANES), bf16),
             pltpu.VMEM((2, HALF, TAPS, LANES), bf16),
+            pltpu.VMEM((3, C * ROWS, LANES), f32),
         ],
-        (core, first, last, sums, wsums, act, low, high, cot),
+        (core, first, last, sums, wsums, turned_act, high, turned_cot),
         scalars=3,
         flops=10**9,
-        mib=24,
-    )
-
-    hold = lax.optimization_barrier
+        mib=MIB_OUTER,
+    )
+
     swap = [(0, 1), (1, 0)]
     arrived = lax.ppermute(send, "core", swap)
     mine = call(add_kernel, blocks_half, [], (keep, arrived), mib=4)
-    mine, act, low, high, weight = hold((mine, act, low, high, weight))
     parts = lax.all_to_all(mine, ("y", "x"), 0, 0, tiled=True)
+    depth = lax.axis_size(("z_hi", "z_lo"))
+    block = call(sum_kernel, jax.ShapeDtypeStruct((depth, TAPS, LANES), bf16), [], (parts,), mib=4)
+    block, act, cot, high, weight = hold((block, turned_act, turned_cot, high, weight))
+    parts = lax.all_to_all(block, ("z_hi", "z_lo"), 0, 0, tiled=True)
     out = conv(0, act, low, high, weight)
     flipped = weight.reshape(C, 27, C)[:, ::-1, :].transpose(2, 1, 0).reshape(C, ORDER)
-    parts, out, flipped = hold((parts, out, flipped))
-    depth = lax.axis_size(("z_hi", "z_lo"))
-    block = call(sum_kernel, jax.ShapeDtypeStruct((depth, TAPS, LANES), bf16), [], (parts,), mib=4)
-    block, cot, low, high = hold((block, cot, low, high))
-    parts = lax.all_to_all(block, ("z_hi", "z_lo"), 0, 0, tiled=True)
     back = conv(1, cot, low, high, flipped)
-    parts, back = hold((parts, back))
+    parts, out, back = hold((parts, out, back))
     block = call(sum_kernel, blocks_half, [], (parts,), mib=4)
-    block, out, back = hold((block, out, back))
     whole = lax.all_to_all(block, ("y", "x"), 0, 0, tiled=True)
-
-    def arrange(planes):
-        return planes.transpose(2, 0, 1, 3)[None]
-
-    out, back = arrange(out), arrange(back)
-    whole, out, back = hold((whole, out, back))
     other = lax.ppermute(whole, "core", swap)
     precond = call(
         finish_kernel,
@@ -493,7 +568,7 @@
         scalars=1,
         flops=10**9,
     )
-    return out, back, precond
+    return out[None], back[None], precond
 
 
 def solution(mesh):

time: 85.5 us -> 81.6 us (0.954)
  waiting for transfers between devices: 20.3 us -> 13.6 us
  local copies, waits for them, and re-layouts: 7.72 us -> 1.23 us
  Pallas kernels: 20.2 us -> 26.3 us
  starting transfers between devices: 24.9 us -> 28.1 us
    unnamed x9 -> x4, local copies, waits for them, and re-layouts: 6.47 us -> 0.01 us
    all_to_all x1, waiting for transfers between devices: 6.17 us -> 0.01 us  [body(): parts = lax.all_to_all(block, ('z_hi', 'z_lo'), 0, 0, tiled=True)]
    pallas_call x8 -> x9, Pallas kernels: 20.2 us -> 26.3 us  [call(): pl.pallas_call(kernel, out_shape=shapes, in_specs=specs or [SMEM] * scala...]
    ppermute x2, waiting for transfers between devices: 7.02 us -> 2.87 us  [the longest x1 2.87 us: body(): high = lax.ppermute(for_below, space, down)]
    ppermute x2, starting transfers between devices: 5.68 us -> 2.78 us  [the longest x1 1.49 us: body(): low = lax.ppermute(for_above, space, up)]
    ppermute x1, starting transfers between devices: 0.58 us -> 3.23 us  [body(): arrived = lax.ppermute(send, 'core', swap)]
    all_to_all x1, waiting for transfers between devices: 5.76 us -> 8 us  [body(): parts = lax.all_to_all(mine, ('y', 'x'), 0, 0, tiled=True)]
    all_to_all x1, starting transfers between devices: 6.75 us -> 8.82 us  [body(): parts = lax.all_to_all(mine, ('y', 'x'), 0, 0, tiled=True)]
  transfers between devices with their start and end apart: 6 -> 6, of which waited for: 4 -> 4; matrix products, arithmetic and copies ran while one was open for 4% -> 2% of each run, Pallas kernels for 12% -> 19%
where the time goes in v2:
time: 81.6 us; the launch traced here: 81.2 us
  starting transfers between devices  28.1 us (34%)
  Pallas kernels  26.3 us (32%)
  waiting for transfers between devices  13.6 us (17%)
  blocking collectives  11.2 us (14%)
  local copies, waits for them, and re-layouts  1.23 us (2%)
    pallas_call x9, Pallas kernels, call(): pl.pallas_call(kernel, out_shape=shapes, in_specs=specs or [SMEM] * scala...  26.3 us
    all_to_all x1, blocking collectives, body(): whole = lax.all_to_all(block, ('y', 'x'), 0, 0, tiled=True)  11.2 us
    all_to_all x1, starting transfers between devices, body(): parts = lax.all_to_all(block, ('z_hi', 'z_lo'), 0, 0, tiled=True)  9.14 us
    all_to_all x1, starting transfers between devices, body(): parts = lax.all_to_all(mine, ('y', 'x'), 0, 0, tiled=True)  8.82 us
    all_to_all x1, waiting for transfers between devices, body(): parts = lax.all_to_all(mine, ('y', 'x'), 0, 0, tiled=True)  8 us
    ppermute x1, starting transfers between devices, body(): other = lax.ppermute(whole, 'core', swap)  4.12 us
    ppermute x1, starting transfers between devices, body(): arrived = lax.ppermute(send, 'core', swap)  3.23 us
    ppermute x1, waiting for transfers between devices, body(): high = lax.ppermute(for_below, space, down)  2.87 us
  transfers between devices with their start and end apart: 6, of which 4 were waited for; matrix products, arithmetic and copies ran while one was open for 2% of the time, Pallas kernels for 19%

profile of v2, /device:TPU:1, one launch (start us, length us, event | category | flops | bytes accessed | tf_op | source)
XLA Modules:
  0.0 81.2 jit_solution(13150258478140283063)
XLA Ops:
  0.6 1.9 %shard_map.58 = (bf16[3,32,16,128]{3,2,1,0:T(8,128)(2,1)}, bf16[2,32,16,128]{3,2,1,0:T(8,128)(2,1)}) custom-call(bf16[32,4,16,128]{3,2,1,0:T(8,128)(2,1)} %bitcast.11, bf16[32,4,16,128]{3,2,1,0:T(8,128)(2,1)} %bitcast.13), custom_call_target="tpu_custom_call" | custom-call | bytes 1048576 | tf_op jit(solution)/shard_map/pallas_call | solution.py:432
  2.6 1.3 %collective-permute-start = (bf16[3,32,16,128]{3,2,1,0:T(8,128)(2,1)}, bf16[3,32,16,128]{3,2,1,0:T(8,128)(2,1)S(1)}, u32[]{:S(2)}, u32[]{:S(2)}) collective-permute-start(bf16[3,32,16,128]{3,2,1,0:T(8,128)(2,1)} %get-tuple-element.28), channel_id=1, source_target_pairs={{1,0},{2,1},{3,2},{4,3},{5,4},{6,5},{7,6},{8,7},{9,8},{10,9},{11,1... | collective-permute-start | bytes 1179656 | tf_op jit(solution)/shard_map/ppermute | solution.py:502
  3.9 7.3 %shard_map.59 = (f32[29,96,128]{2,1,0:T(8,128)S(1)}, f32[3,96,128]{2,1,0:T(8,128)S(1)}, bf16[4,16,32,128]{3,2,1,0:T(8,128)(2,1)S(1)}, bf16[4,16,32,128]{3,2,1,0:T(8,128)(2,1)S(1)}) custom-call(bf16[32,4,16,128]{3,2,1,0:T(8,128)(2,1)} %bitcast.12, bf16[32,4,16,128]{3,2,1,0:T(8,128)(2,1)} %bitcast.14), custom_call_target="tpu_custom_call" | custom-call | flops 6000000000 | bytes 1048576 | tf_op jit(solution)/shard_map/pallas_call | solution.py:432
  11.2 2.9 %collective-permute-done.high_ref = bf16[3,32,16,128]{3,2,1,0:T(8,128)(2,1)S(1)} collective-permute-done((bf16[3,32,16,128]{3,2,1,0:T(8,128)(2,1)}, bf16[3,32,16,128]{3,2,1,0:T(8,128)(2,1)S(1)}, u32[]{:S(2)}, u32[]{:S(2)}) %collective-permute-start) | collective-permute-done | bytes 393248 | tf_op jit(solution)/shard_map/ppermute | solution.py:502
  14.1 1.8 %shard_map.60 = (bf16[16,96,128]{2,1,0:T(8,128)(2,1)S(1)}, bf16[16,96,128]{2,1,0:T(8,128)(2,1)S(1)}) custom-call(s32[1]{0:T(128)} %bitcast.core_ref, s32[1]{0:T(128)} %bitcast.1.first_ref, s32[1]{0:T(128)} %bitcast.2.last_ref, f32[29,96,128]{2,1,0:T(8,128)S(1)} %get-tuple-element.25.in_ref, f32[3,96,128]{2,1,0:T(8,128)S(1)} %get-tuple-element.26.wg_ref, ...), custom_call_target="tpu_custom_call" | custom-call | flops 1000000000 | bytes 1048576 | tf_op jit(solution)/shard_map/pallas_call | solution.py:432
  15.9 0.0 copy-start.1
  15.9 3.2 %collective-permute-start.1 = (bf16[16,96,128]{2,1,0:T(8,128)(2,1)S(1)}, bf16[16,96,128]{2,1,0:T(8,128)(2,1)S(1)}, u32[]{:S(2)}, u32[]{:S(2)}) collective-permute-start(bf16[16,96,128]{2,1,0:T(8,128)(2,1)S(1)} %get-tuple-element.31), channel_id=1, source_target_pairs={{0,64},{64,0},{1,65},{65,1},{2,66},{66,2},{3,67},{67,3},{4,68},{68... | collective-permute-start | bytes 1179656 | tf_op jit(solution)/shard_map/ppermute | solution.py:549
  19.1 1.3 %collective-permute-done.1.arrived_ref = bf16[16,96,128]{2,1,0:T(8,128)(2,1)S(1)} collective-permute-done((bf16[16,96,128]{2,1,0:T(8,128)(2,1)S(1)}, bf16[16,96,128]{2,1,0:T(8,128)(2,1)S(1)}, u32[]{:S(2)}, u32[]{:S(2)}) %collective-permute-start.1) | collective-permute-done | bytes 393248 | tf_op jit(solution)/shard_map/ppermute | solution.py:549
  20.4 0.9 %shard_map.61 = bf16[16,96,128]{2,1,0:T(8,128)(2,1)} custom-call(bf16[16,96,128]{2,1,0:T(8,128)(2,1)S(1)} %get-tuple-element.30.keep_ref, bf16[16,96,128]{2,1,0:T(8,128)(2,1)S(1)} %collective-permute-done.1.arrived_ref), custom_call_target="tpu_custom_call" | custom-call | bytes 1048576 | tf_op jit(solution)/shard_map/pallas_call | solution.py:432
  21.3 8.8 %all-to-all-start = ((bf16[16,96,128]{2,1,0:T(8,128)(2,1)}), bf16[16,96,128]{2,1,0:T(8,128)(2,1)S(1)}, u32[]{:S(2)}, u32[]{:S(2)}) async-start(bf16[16,96,128]{2,1,0:T(8,128)(2,1)} %shard_map.61), calls=%async_computation | async-start | bytes 786432 | tf_op jit(solution)/shard_map/all_to_all | solution.py:551
  30.2 1.5 %collective-permute-start.2 = (bf16[2,32,16,128]{3,2,1,0:T(8,128)(2,1)S(1)}, bf16[2,32,16,128]{3,2,1,0:T(8,128)(2,1)S(1)}, u32[]{:S(2)}, u32[]{:S(2)}) collective-permute-start(bf16[2,32,16,128]{3,2,1,0:T(8,128)(2,1)S(1)} %copy-done.1), channel_id=1, source_target_pairs={{0,1},{1,2},{2,3},{3,4},{4,5},{5,6},{6,7},{7,8},{8,9},{9,10},{10,1... | collective-permute-start | bytes 786440 | tf_op jit(solution)/shard_map/ppermute | solution.py:531
  31.7 8.0 %all-to-all-done.parts_ref = bf16[16,96,128]{2,1,0:T(8,128)(2,1)S(1)} async-done(((bf16[16,96,128]{2,1,0:T(8,128)(2,1)}), bf16[16,96,128]{2,1,0:T(8,128)(2,1)S(1)}, u32[]{:S(2)}, u32[]{:S(2)}) %all-to-all-start) | async-done | bytes 393248 | tf_op jit(solution)/shard_map/all_to_all | solution.py:551
  39.7 0.7 shard_map.62
  40.4 9.1 %all-to-all-start.1 = ((bf16[8,96,128]{2,1,0:T(8,128)(2,1)}), bf16[8,96,128]{2,1,0:T(8,128)(2,1)S(1)}, u32[]{:S(2)}, u32[]{:S(2)}) async-start(bf16[8,96,128]{2,1,0:T(8,128)(2,1)} %shard_map.62), calls=%async_computation.1 | async-start | bytes 393216 | tf_op jit(solution)/shard_map/all_to_all | solution.py:555
  49.6 0.2 reshape.30
  49.8 0.2 rev.3
  50.0 0.6 copy.7
  50.6 0.2 reshape.31.w_ref
  50.8 3.7 %shard_map.63 = bf16[32,4,16,128]{3,2,1,0:T(8,128)(2,1)} custom-call(bf16[4,16,32,128]{3,2,1,0:T(8,128)(2,1)S(1)} %get-tuple-element.33.act_ref.x_ref, bf16[2,32,16,128]{3,2,1,0:T(8,128)(2,1)S(1)} %collective-permute-done.2.low_ref, bf16[3,32,16,128]{3,2,1,0:T(8,128)(2,1)S(1)} %collective-permute-done.high_ref, bf16[32,864]{1,0:T(8,128)(2,1)S(1)} %copy-done), custom_call_target="tpu_custom_call" | custom-call | flops 452984832 | bytes 1048576 | tf_op jit(solution)/shard_map/pallas_call | solution.py:432
  54.5 3.7 %shard_map.64 = bf16[32,4,16,128]{3,2,1,0:T(8,128)(2,1)} custom-call(bf16[4,16,32,128]{3,2,1,0:T(8,128)(2,1)S(1)} %get-tuple-element.37.cot_ref.x_ref, bf16[2,32,16,128]{3,2,1,0:T(8,128)(2,1)S(1)} %collective-permute-done.2.low_ref, bf16[3,32,16,128]{3,2,1,0:T(8,128)(2,1)S(1)} %collective-permute-done.high_ref, bf16[32,864]{1,0:T(8,128)(2,1)S(1)} %reshape.31.w_ref), custom_call_target="tpu_custom_call" | custom-call | flops 452984832 | bytes 1048576 | tf_op jit(solution)/shard_map/pallas_call | solution.py:432
  58.3 11.2 %all_to_all.15.mine_ref = bf16[16,96,128]{2,1,0:T(8,128)(2,1)S(1)} all-to-all(bf16[16,96,128]{2,1,0:T(8,128)(2,1)S(1)} %shard_map.65), channel_id=1, replica_groups=mesh['z_hi'=2,'core'=2,'y'=4,'x'=4,'z_lo'=4] {'y','x'}, dimensions={0} | all-to-all | bytes 786432 | tf_op jit(solution)/shard_map/all_to_all | solution.py:561
  69.5 4.1 %collective-permute-start.3 = (bf16[16,96,128]{2,1,0:T(8,128)(2,1)S(1)}, bf16[16,96,128]{2,1,0:T(8,128)(2,1)S(1)}, u32[]{:S(2)}, u32[]{:S(2)}) collective-permute-start(bf16[16,96,128]{2,1,0:T(8,128)(2,1)S(1)} %all_to_all.15.mine_ref), channel_id=1, source_target_pairs={{0,64},{64,0},{1,65},{65,1},{2,66},{66,2},{3,67},{67,3},{4,68},{68... | collective-permute-start | bytes 1179656 | tf_op jit(solution)/shard_map/ppermute | solution.py:562
  73.6 1.3 %collective-permute-done.3.other_ref = bf16[16,96,128]{2,1,0:T(8,128)(2,1)S(1)} collective-permute-done((bf16[16,96,128]{2,1,0:T(8,128)(2,1)S(1)}, bf16[16,96,128]{2,1,0:T(8,128)(2,1)S(1)}, u32[]{:S(2)}, u32[]{:S(2)}) %collective-permute-start.3) | collective-permute-done | bytes 393248 | tf_op jit(solution)/shard_map/ppermute | solution.py:562
  74.9 6.2 %shard_map.66 = f32[32,864]{1,0:T(8,128)} custom-call(s32[1]{0:T(128)} %bitcast.core_ref, bf16[16,96,128]{2,1,0:T(8,128)(2,1)S(1)} %all_to_all.15.mine_ref, bf16[16,96,128]{2,1,0:T(8,128)(2,1)S(1)} %collective-permute-done.3.other_ref), custom_call_target="tpu_custom_call" | custom-call | flops 1000000000 | bytes 1048576 | tf_op jit(solution)/shard_map/pallas_call | solution.py:432
  (6 shorter events, 0.1 us)
Async XLA Ops:
  2.6 11.5 %collective-permute-start = (bf16[3,32,16,128]{3,2,1,0:T(8,128)(2,1)}, bf16[3,32,16,128]{3,2,1,0:T(8,128)(2,1)S(1)}, u32[]{:S(2)}, u32[]{:S(2)}) collective-permute-start(bf16[3,32,16,128]{3,2,1,0:T(8,128)(2,1)} %get-tuple-element.28), channel_id=1, source_target_pairs={{1,0},{2,1},{3,2},{4,3},{5,4},{6,5},{7,6},{8,7},{9,8},{10,9},{11,1... | collective-permute-start | bytes 1179656 | tf_op jit(solution)/shard_map/ppermute | solution.py:502
  15.9 14.3 %copy-start.1 = (bf16[2,32,16,128]{3,2,1,0:T(8,128)(2,1)S(1)}, bf16[2,32,16,128]{3,2,1,0:T(8,128)(2,1)}, u32[]{:S(2)}) copy-start(bf16[2,32,16,128]{3,2,1,0:T(8,128)(2,1)} %get-tuple-element.34) | copy-start | bytes 786436
  15.9 4.6 %collective-permute-start.1 = (bf16[16,96,128]{2,1,0:T(8,128)(2,1)S(1)}, bf16[16,96,128]{2,1,0:T(8,128)(2,1)S(1)}, u32[]{:S(2)}, u32[]{:S(2)}) collective-permute-start(bf16[16,96,128]{2,1,0:T(8,128)(2,1)S(1)} %get-tuple-element.31), channel_id=1, source_target_pairs={{0,64},{64,0},{1,65},{65,1},{2,66},{66,2},{3,67},{67,3},{4,68},{68... | collective-permute-start | bytes 1179656 | tf_op jit(solution)/shard_map/ppermute | solution.py:549
  20.4 29.1 %copy-start = (bf16[32,864]{1,0:T(8,128)(2,1)S(1)}, bf16[32,864]{1,0:T(8,128)(2,1)}, u32[]{:S(2)}) copy-start(bf16[32,864]{1,0:T(8,128)(2,1)} %w_ref) | copy-start | bytes 165892
  21.3 18.3 %all-to-all-start = ((bf16[16,96,128]{2,1,0:T(8,128)(2,1)}), bf16[16,96,128]{2,1,0:T(8,128)(2,1)S(1)}, u32[]{:S(2)}, u32[]{:S(2)}) async-start(bf16[16,96,128]{2,1,0:T(8,128)(2,1)} %shard_map.61), calls=%async_computation | async-start | bytes 786432 | tf_op jit(solution)/shard_map/all_to_all | solution.py:551
  30.2 20.6 %collective-permute-start.2 = (bf16[2,32,16,128]{3,2,1,0:T(8,128)(2,1)S(1)}, bf16[2,32,16,128]{3,2,1,0:T(8,128)(2,1)S(1)}, u32[]{:S(2)}, u32[]{:S(2)}) collective-permute-start(bf16[2,32,16,128]{3,2,1,0:T(8,128)(2,1)S(1)} %copy-done.1), channel_id=1, source_target_pairs={{0,1},{1,2},{2,3},{3,4},{4,5},{5,6},{6,7},{7,8},{8,9},{9,10},{10,1... | collective-permute-start | bytes 786440 | tf_op jit(solution)/shard_map/ppermute | solution.py:531
  40.4 17.9 %all-to-all-start.1 = ((bf16[8,96,128]{2,1,0:T(8,128)(2,1)}), bf16[8,96,128]{2,1,0:T(8,128)(2,1)S(1)}, u32[]{:S(2)}, u32[]{:S(2)}) async-start(bf16[8,96,128]{2,1,0:T(8,128)(2,1)} %shard_map.62), calls=%async_computation.1 | async-start | bytes 393216 | tf_op jit(solution)/shard_map/all_to_all | solution.py:555
  69.5 5.5 %collective-permute-start.3 = (bf16[16,96,128]{2,1,0:T(8,128)(2,1)S(1)}, bf16[16,96,128]{2,1,0:T(8,128)(2,1)S(1)}, u32[]{:S(2)}, u32[]{:S(2)}) collective-permute-start(bf16[16,96,128]{2,1,0:T(8,128)(2,1)S(1)} %all_to_all.15.mine_ref), channel_id=1, source_target_pairs={{0,64},{64,0},{1,65},{65,1},{2,66},{66,2},{3,67},{67,3},{4,68},{68... | collective-permute-start | bytes 1179656 | tf_op jit(solution)/shard_map/ppermute | solution.py:562

commit v3 on v2

--- a/solution.py
+++ b/solution.py
@@ -94,8 +94,22 @@
 A_BLOCKS = 29
 
 
+def flip_taps(w_ref, flipped_ref):
+    wide = jnp.concatenate([w_ref[...].astype(f32), jnp.zeros((C, 7 * LANES - ORDER), f32)], 1)
+    tall = jnp.concatenate([wide, jnp.zeros((LANES - C, 7 * LANES), f32)], 0).T
+    for group in range(7):
+        total = jnp.zeros((C, LANES), f32)
+        for place in range(4):
+            tap = 26 - 4 * group - place
+            if tap >= 0:
+                block = tall[tap * C : (tap + 1) * C, :]
+                total = total + (pltpu.roll(block, place * C, 1) if place else block)
+        width = min(LANES, ORDER - lane(group))
+        flipped_ref[:, lane(group) : lane(group) + width] = total[:, :width].astype(bf16)
+
+
 def gram_inner(
-    act_hbm, cot_hbm, out_ref, wg_ref, turned_act, turned_cot,
+    act_hbm, cot_hbm, w_ref, out_ref, wg_ref, turned_act, turned_cot, flipped_ref, above_ref,
     taps, cots, store, act_ref, cot_ref, sems,
 ):
     fetches = []
@@ -106,6 +120,7 @@
             )
     for fetch in fetches:
         fetch.start()
+    flip_taps(w_ref, flipped_ref)
     for x in range(PLANES):
         zero_rows(taps, lane(x * RPAD))
         zero_rows(cots, lane(x * RPAD))
@@ -116,6 +131,9 @@
         fill_taps(taps, plane_at(x), rows)
         cot_rows = turned(cot_ref[x], store.at[2 * x + 1])
         fill_rows(cots, plane_at(x), cot_rows)
+        if x == PLANES - 1:
+            above_ref[0] = act_ref[x]
+            above_ref[1] = cot_ref[x]
         for y in range(ROWS):
             turned_act[x, y] = rows[y].astype(bf16)
             turned_cot[x, y] = cot_rows[y].astype(bf16)
@@ -301,24 +319,30 @@
         out_ref[i] = total
 
 
-def conv_kernel(which, x_ref, low_ref, high_ref, w_ref, out_ref, taps, store):
-    for index in range(PLANES + 2):
-        zero_rows(taps, lane(index * RPAD))
+def conv_kernel(
+    act_ref, cot_ref, low_ref, high_ref, w_ref, flipped_ref, out_ref, back_ref,
+    act_taps, cot_taps, store, halos,
+):
+    step = 2
+
+    def fill(which, index):
+        planes, dst = ((act_ref, act_taps), (cot_ref, cot_taps))[which]
+        zero_rows(dst, lane(index * RPAD))
         if index == 0:
-            rows = turned(low_ref[which], store.at[PLANES])
+            rows = turned(low_ref[which], halos.at[which, 0])
         elif index == PLANES + 1:
-            rows = turned(high_ref[2 * which], store.at[PLANES + 1])
+            rows = turned(high_ref[2 * which], halos.at[which, 1])
         else:
-            rows = rows_of(x_ref[index - 1])
-        fill_taps(taps, plane_at(index), rows)
-    weight = w_ref[...]
-    step = 2
-    for x in range(PLANES):
-        plane = store.at[x]
+            rows = rows_of(planes[index - 1])
+        fill_taps(dst, plane_at(index), rows)
+
+    def products(which, x, weight):
+        src = (act_taps, cot_taps)[which]
+        plane = store.at[which, x]
         for y in range(0, ROWS, step):
             patch = jnp.concatenate(
                 [
-                    taps[:, pl.ds(plane_at(x + 1 + dx, y + dy), step * LANES)]
+                    src[:, pl.ds(plane_at(x + 1 + dx, y + dy), step * LANES)]
                     for dx in (-1, 0, 1)
                     for dy in (-1, 0, 1)
                 ],
@@ -327,8 +351,27 @@
             value = jnp.dot(weight, patch, preferred_element_type=f32)
             for i in range(step):
                 plane[(y + i) * C : (y + i + 1) * C, :] = value[:, lane(i) : lane(i + 1)]
+
+    def put(which, x):
+        target = (out_ref, back_ref)[which]
         for channel in range(C):
-            out_ref[channel, x] = plane[pl.ds(channel, ROWS, stride=C), :].astype(bf16)
+            target[channel, x] = store[which, x, pl.ds(channel, ROWS, stride=C), :].astype(bf16)
+
+    weights = (w_ref[...], flipped_ref[...])
+    fills = [(which, index) for which in (0, 1) for index in range(PLANES + 2)]
+    for _ in range(3):
+        fill(*fills.pop(0))
+    before = None
+    for which in (0, 1):
+        for x in range(PLANES):
+            products(which, x, weights[which])
+            for _ in range(2 if which == 0 and x < 3 else 1):
+                if fills:
+                    fill(*fills.pop(0))
+            if before:
+                put(*before)
+            before = (which, x)
+    put(*before)
 
 
 def split(value):
@@ -340,40 +383,50 @@
     return {0: "0", 1: "f", -1: "l"}[offset]
 
 
-def finish_kernel(core_ref, mine_ref, other_ref, out_ref, both, factor):
+def finish_kernel(core_ref, mine_ref, other_ref, out_ref, factor):
     own = core_ref[0]
-    both[own] = mine_ref[...]
-    both[1 - own] = other_ref[...]
-
-    def block(slot):
-        return both[slot // HALF, slot % HALF]
+
+    def chosen(slot, rows=slice(None)):
+        here = own == slot // HALF
+        return jnp.where(here, mine_ref[slot % HALF, rows, :], other_ref[slot % HALF, rows, :])
 
     at = lax.broadcasted_iota(jnp.int32, (TAPS, LANES), 1)
     offsets = [(a, b) for a in (-1, 0, 1) for b in (-1, 0, 1)]
-    tail = jnp.zeros((LANES - TAPS, LANES), bf16)
+    tail = jnp.zeros((LANES - TAPS, LANES), f32)
+    diag_row = lax.broadcasted_iota(jnp.int32, (LANES, LANES), 0)
+    diag_col = lax.broadcasted_iota(jnp.int32, (LANES, LANES), 1)
     cache = {}
 
-    def padded(slot):
+    def size(value):
+        return jnp.sum(jnp.abs(value), axis=0, keepdims=True)
+
+    def padded(slot, symmetric):
         if slot not in cache:
-            value = jnp.where(at < TAPS, block(slot), jnp.zeros((), bf16))
+            value = jnp.where(at < TAPS, chosen(slot).astype(f32), 0.0)
             full = jnp.concatenate([value, tail], 0)
-            cache[slot] = (full, full.T)
+            turned = full if symmetric else full.T
+            cache[slot] = (full.astype(bf16), turned.astype(bf16), size(full), size(turned), full)
         return cache[slot]
 
+    sums = [jnp.zeros((1, LANES), f32) for _ in offsets]
+    diagonal = jnp.zeros((LANES, LANES), f32)
     for i, (ax, ay) in enumerate(offsets):
         for j, (bx, by) in enumerate(offsets):
             dx, dy = bx - ax, by - ay
             if dx < 0 or (dx == 0 and dy < 0):
                 continue
             key = (class_of(ax) if dx == 0 else dx, class_of(ay) if dy == 0 else dy)
-            full, turned = padded(SLOT[key])
+            full, turned, size_full, size_turned, wide = padded(SLOT[key], i == j)
             factor[lane(j) : lane(j + 1), lane(i) : lane(i + 1)] = full
+            sums[i] = sums[i] + size_full
             if i != j:
                 factor[lane(i) : lane(i + 1), lane(j) : lane(j + 1)] = turned
+                sums[j] = sums[j] + size_turned
+            else:
+                diagonal = diagonal + jnp.where(diag_row == diag_col, wide, 0.0)
 
     def extra(t):
-        here = both.at[t // HALF, t % HALF]
-        return here[0:C, :].astype(f32) + here[C : 2 * C, :].astype(f32)
+        return chosen(t, slice(0, C)).astype(f32) + chosen(t, slice(C, 2 * C)).astype(f32)
 
     pieces = []
     for i in range(9):
@@ -384,40 +437,33 @@
         pieces.append(rows)
     wgrad = jnp.concatenate(pieces, 1) * (1.0 / CELLS)
 
+    def exact(left, right):
+        return jnp.dot(left, right, precision=lax.Precision.HIGHEST, preferred_element_type=f32)
+
     grad = extra(GRAD)[:, TAPS:LANES]
     row_id = lax.broadcasted_iota(jnp.int32, (C, C), 0)
     col_id = lax.broadcasted_iota(jnp.int32, (C, C), 1)
     eye = jnp.where(row_id == col_id, 1.0, 0.0).astype(f32)
     scaled = grad * (C / jnp.sum(grad * eye)) + DAMPING * eye
-    bound = jnp.max(jnp.sum(jnp.abs(scaled), axis=1))
-    inverse = eye / bound
-    for _ in range(ITERS):
-        half = jnp.dot(inverse, scaled, precision=lax.Precision.HIGHEST, preferred_element_type=f32)
-        inverse = 2.0 * inverse - jnp.dot(
-            half, inverse, precision=lax.Precision.HIGHEST, preferred_element_type=f32
-        )
-
-    trace = jnp.zeros((), f32)
-    sums = jnp.zeros((1, WIDE), f32)
-    diag_row = lax.broadcasted_iota(jnp.int32, (LANES, LANES), 0)
-    diag_col = lax.broadcasted_iota(jnp.int32, (LANES, LANES), 1)
-    diagonal = jnp.zeros((LANES, LANES), f32)
-    for i in range(9):
-        rows = factor[lane(i) : lane(i + 1), :].astype(f32)
-        sums = sums + jnp.sum(jnp.abs(rows), axis=0, keepdims=True)
-        diagonal = diagonal + jnp.where(diag_row == diag_col, rows[:, lane(i) : lane(i + 1)], 0.0)
-    trace = jnp.sum(diagonal)
-    scale = ORDER / trace
-    bound = scale * jnp.max(sums) + DAMPING
+    inverse = eye / jnp.max(jnp.sum(jnp.abs(scaled), axis=1))
+
+    scale = ORDER / jnp.sum(diagonal)
+    bound = scale * jnp.max(jnp.concatenate(sums, 0)) + DAMPING
     step = scale / bound
     keep = 1.0 - DAMPING / bound
     value = wgrad
-    for _ in range(2**ITERS - 1):
+    half = None
+    for sweep in range(2**ITERS - 1):
         high, low = split(value)
         product = jnp.dot(jnp.concatenate([high, low], 0), factor[...], preferred_element_type=f32)
+        if sweep < 2 * ITERS:
+            if sweep % 2 == 0:
+                half = exact(inverse, scaled)
+            else:
+                inverse = 2.0 * inverse - exact(half, inverse)
         value = wgrad + keep * value - step * (product[:C] + product[C:])
     right = value * (1.0 / bound)
-    applied = jnp.dot(inverse, right, precision=lax.Precision.HIGHEST, preferred_element_type=f32)
+    applied = exact(inverse, right)
     quadratic = jnp.sum(applied * wgrad)
     result = applied * jnp.sqrt(C * ORDER / quadratic)
     out_ref[...] = jnp.concatenate([result[:, lane(i) : lane(i) + TAPS] for i in range(9)], 1)
@@ -440,52 +486,43 @@
     )(*inputs)
 
 
-def edge_kernel(act, cot, down_out, up_out, down, up, sems):
-    hops = []
-    for k, (source, plane, buffer, target, slot) in enumerate((
-        (act, 0, down, down_out, 0),
-        (act, 1, down, down_out, 1),
-        (cot, 0, down, down_out, 2),
-        (act, PLANES - 1, up, up_out, 0),
-        (cot, PLANES - 1, up, up_out, 1),
-    )):
-        hops.append((
-            pltpu.make_async_copy(source.at[:, plane], buffer.at[slot], sems.at[2 * k]),
-            pltpu.make_async_copy(buffer.at[slot], target.at[slot], sems.at[2 * k + 1]),
-        ))
-    for fetch, _ in hops:
-        fetch.start()
-    for fetch, put in hops:
-        fetch.wait()
-        put.start()
-    for _, put in hops:
-        put.wait()
+def edge_kernel(act, cot, down, sems):
+    copies = [
+        pltpu.make_async_copy(source.at[:, plane], down.at[k], sems.at[k])
+        for k, (source, plane) in enumerate(((act, 0), (act, 1), (cot, 0)))
+    ]
+    for copy in copies:
+        copy.start()
+    for copy in copies:
+        copy.wait()
 
 
 def edge_planes(act, cot):
-    down, up = (3, C, ROWS, LANES), (2, C, ROWS, LANES)
     return call(
         edge_kernel,
-        (pltpu.HBM(down, bf16), pltpu.HBM(up, bf16)),
-        [pltpu.VMEM(down, bf16), pltpu.VMEM(up, bf16), pltpu.SemaphoreType.DMA((10,))],
+        pltpu.VMEM((3, C, ROWS, LANES), bf16),
+        [pltpu.SemaphoreType.DMA((3,))],
         (act, cot),
         mib=4,
         specs=[IN_HBM] * 2,
-        out_specs=(IN_HBM, IN_HBM),
     )
 
 
-def conv(which, planes, low, high, weight):
+def conv(act, cot, low, high, weight, flipped):
+    taps = pltpu.VMEM((TAPS, 6 * RPAD * LANES), bf16)
+    shape = jax.ShapeDtypeStruct((C, PLANES, ROWS, LANES), bf16)
     return call(
-        functools.partial(conv_kernel, which),
-        jax.ShapeDtypeStruct((C, PLANES, ROWS, LANES), bf16),
+        conv_kernel,
+        (shape, shape),
         [
-            pltpu.VMEM((TAPS, 6 * RPAD * LANES), bf16),
-            pltpu.VMEM((PLANES + 2, C * ROWS, LANES), f32),
+            taps,
+            taps,
+            pltpu.VMEM((2, PLANES, C * ROWS, LANES), f32),
+            pltpu.VMEM((2, 2, C * ROWS, LANES), f32),
         ],
-        (planes, low, high, weight),
-        flops=2 * C * ORDER * PLANES * ROWS * LANES,
-        mib=12,
+        (act, cot, low, high, weight, flipped),
+        flops=4 * C * ORDER * PLANES * ROWS * LANES,
+        mib=20,
     )
 
 
@@ -498,7 +535,7 @@
 
     act = pltpu.with_memory_space_constraint(activations[0], pltpu.HBM)
     cot = pltpu.with_memory_space_constraint(cotangent[0], pltpu.HBM)
-    for_below, for_above = edge_planes(act, cot)
+    for_below = edge_planes(act, cot)
     high = lax.ppermute(for_below, space, down)
     where = lax.axis_index(space)
     core = lax.axis_index("core").astype(jnp.int32).reshape(1)
@@ -506,13 +543,15 @@
     last = (where == size - 1).astype(jnp.int32).reshape(1)
 
     turned_shape = pltpu.VMEM((PLANES, ROWS, C, LANES), bf16)
-    sums, wsums, turned_act, turned_cot = call(
+    sums, wsums, turned_act, turned_cot, flipped, for_above = call(
         gram_inner,
         (
             pltpu.VMEM((A_BLOCKS, TAPS, LANES), f32),
             pltpu.VMEM((3, TAPS, LANES), f32),
             turned_shape,
             turned_shape,
+            jax.ShapeDtypeStruct((C, ORDER), bf16),
+            jax.ShapeDtypeStruct((2, C, ROWS, LANES), bf16),
         ),
         [
             pltpu.VMEM((TAPS, PLANES * RPAD * LANES), bf16),
@@ -522,8 +561,8 @@
             pltpu.VMEM((PLANES, C, ROWS, LANES), bf16),
             pltpu.SemaphoreType.DMA((2 * PLANES,)),
         ],
-        (act, cot),
-        specs=[IN_HBM] * 2,
+        (act, cot, weight),
+        specs=[IN_HBM, IN_HBM, WHOLE],
         flops=24 * 10**9 // 4,
         mib=MIB_INNER,
     )
@@ -553,9 +592,7 @@
     block = call(sum_kernel, jax.ShapeDtypeStruct((depth, TAPS, LANES), bf16), [], (parts,), mib=4)
     block, act, cot, high, weight = hold((block, turned_act, turned_cot, high, weight))
     parts = lax.all_to_all(block, ("z_hi", "z_lo"), 0, 0, tiled=True)
-    out = conv(0, act, low, high, weight)
-    flipped = weight.reshape(C, 27, C)[:, ::-1, :].transpose(2, 1, 0).reshape(C, ORDER)
-    back = conv(1, cot, low, high, flipped)
+    out, back = conv(act, cot, low, high, weight, flipped)
     parts, out, back = hold((parts, out, back))
     block = call(sum_kernel, blocks_half, [], (parts,), mib=4)
     whole = lax.all_to_all(block, ("y", "x"), 0, 0, tiled=True)
@@ -563,7 +600,7 @@
     precond = call(
         finish_kernel,
         jax.ShapeDtypeStruct((C, ORDER), f32),
-        [pltpu.VMEM((2, HALF, TAPS, LANES), bf16), pltpu.VMEM((WIDE, WIDE), bf16)],
+        [pltpu.VMEM((WIDE, WIDE), bf16)],
         (core, whole, other),
         scalars=1,
         flops=10**9,

time: 81.6 us -> 79.4 us (0.973)
  Pallas kernels: 26.3 us -> 23.2 us
  waiting for transfers between devices: 13.6 us -> 15.7 us
  local copies, waits for them, and re-layouts: 1.23 us -> 0.01 us
    pallas_call x9 -> x8, Pallas kernels: 26.3 us -> 23.2 us  [call(): pl.pallas_call(kernel, out_shape=shapes, in_specs=specs or [SMEM] * scala...]
    all_to_all x1, waiting for transfers between devices: 0.01 us -> 2.47 us  [body(): parts = lax.all_to_all(block, ('z_hi', 'z_lo'), 0, 0, tiled=True)]
  transfers between devices with their start and end apart: 6 -> 6, of which waited for: 4 -> 5; matrix products, arithmetic and copies ran while one was open for 2% -> 0% of each run, Pallas kernels for 19% -> 18%
where the time goes in v3:
time: 79.4 us; the launch traced here: 79 us
  starting transfers between devices  28.2 us (36%)
  Pallas kernels  23.2 us (29%)
  waiting for transfers between devices  15.7 us (20%)
  blocking collectives  11.1 us (14%)
    pallas_call x8, Pallas kernels, call(): pl.pallas_call(kernel, out_shape=shapes, in_specs=specs or [SMEM] * scala...  23.2 us
    all_to_all x1, blocking collectives, body(): whole = lax.all_to_all(block, ('y', 'x'), 0, 0, tiled=True)  11.1 us
    all_to_all x1, starting transfers between devices, body(): parts = lax.all_to_all(block, ('z_hi', 'z_lo'), 0, 0, tiled=True)  9.25 us
    all_to_all x1, starting transfers between devices, body(): parts = lax.all_to_all(mine, ('y', 'x'), 0, 0, tiled=True)  8.71 us
    all_to_all x1, waiting for transfers between devices, body(): parts = lax.all_to_all(mine, ('y', 'x'), 0, 0, tiled=True)  7.9 us
    ppermute x1, starting transfers between devices, body(): other = lax.ppermute(whole, 'core', swap)  4.14 us
    ppermute x1, starting transfers between devices, body(): arrived = lax.ppermute(send, 'core', swap)  3.24 us
    ppermute x1, waiting for transfers between devices, body(): high = lax.ppermute(for_below, space, down)  2.62 us
  transfers between devices with their start and end apart: 6, of which 5 were waited for; matrix products, arithmetic and copies ran while one was open for 0% of the time, Pallas kernels for 18%

profile of v3, /device:TPU:1, one launch (start us, length us, event | category | flops | bytes accessed | tf_op | source)
XLA Modules:
  0.0 79.0 jit_solution(12238178369145974586)
XLA Ops:
  0.6 0.0 copy-start
  0.6 1.1 %shard_map.59 = bf16[3,32,16,128]{3,2,1,0:T(8,128)(2,1)S(1)} custom-call(bf16[32,4,16,128]{3,2,1,0:T(8,128)(2,1)} %bitcast.7, bf16[32,4,16,128]{3,2,1,0:T(8,128)(2,1)} %bitcast.9), custom_call_target="tpu_custom_call" | custom-call | bytes 1048576 | tf_op jit(solution)/shard_map/pallas_call | solution.py:478
  1.7 1.3 %collective-permute-start = (bf16[3,32,16,128]{3,2,1,0:T(8,128)(2,1)S(1)}, bf16[3,32,16,128]{3,2,1,0:T(8,128)(2,1)S(1)}, u32[]{:S(2)}, u32[]{:S(2)}) collective-permute-start(bf16[3,32,16,128]{3,2,1,0:T(8,128)(2,1)S(1)} %shard_map.59), channel_id=1, source_target_pairs={{1,0},{2,1},{3,2},{4,3},{5,4},{6,5},{7,6},{8,7},{9,8},{10,9},{11,1... | collective-permute-start | bytes 1179656 | tf_op jit(solution)/shard_map/ppermute | solution.py:539
  3.0 0.0 copy-done
  3.0 7.3 %shard_map.58 = (f32[29,96,128]{2,1,0:T(8,128)S(1)}, f32[3,96,128]{2,1,0:T(8,128)S(1)}, bf16[4,16,32,128]{3,2,1,0:T(8,128)(2,1)S(1)}, bf16[4,16,32,128]{3,2,1,0:...) custom-call(bf16[32,4,16,128]{3,2,1,0:T(8,128)(2,1)} %bitcast.8, ...), custom_call_target="tpu_custom_call" | custom-call | flops 6000000000 | bytes 1048576 | tf_op jit(solution)/shard_map/pallas_call | solution.py:478
  10.4 2.6 %collective-permute-done.high_ref = bf16[3,32,16,128]{3,2,1,0:T(8,128)(2,1)S(1)} collective-permute-done((bf16[3,32,16,128]{3,2,1,0:T(8,128)(2,1)S(1)}, bf16[3,32,16,128]{3,2,1,0:T(8,128)(2,1)S(1)}, u32[]{:S(2)}, u32[]{:S(2)}) %collective-permute-start) | collective-permute-done | bytes 393248 | tf_op jit(solution)/shard_map/ppermute | solution.py:539
  13.0 1.8 %shard_map.60 = (bf16[16,96,128]{2,1,0:T(8,128)(2,1)S(1)}, bf16[16,96,128]{2,1,0:T(8,128)(2,1)S(1)}) custom-call(s32[1]{0:T(128)} %bitcast.core_ref, s32[1]{0:T(128)} %bitcast.1.first_ref, s32[1]{0:T(128)} %bitcast.2.last_ref, f32[29,96,128]{2,1,0:T(8,128)S(1)} %get-tuple-element.27.in_ref, f32[3,96,128]{2,1,0:T(8,128)S(1)} %get-tuple-element.28.wg_ref, ...), custom_call_target="tpu_custom_call" | custom-call | flops 1000000000 | bytes 1048576 | tf_op jit(solution)/shard_map/pallas_call | solution.py:478
  14.8 3.2 %collective-permute-start.1 = (bf16[16,96,128]{2,1,0:T(8,128)(2,1)S(1)}, bf16[16,96,128]{2,1,0:T(8,128)(2,1)S(1)}, u32[]{:S(2)}, u32[]{:S(2)}) collective-permute-start(bf16[16,96,128]{2,1,0:T(8,128)(2,1)S(1)} %get-tuple-element.32), channel_id=1, source_target_pairs={{0,64},{64,0},{1,65},{65,1},{2,66},{66,2},{3,67},{67,3},{4,68},{68... | collective-permute-start | bytes 1179656 | tf_op jit(solution)/shard_map/ppermute | solution.py:588
  18.1 1.3 %collective-permute-done.1.arrived_ref = bf16[16,96,128]{2,1,0:T(8,128)(2,1)S(1)} collective-permute-done((bf16[16,96,128]{2,1,0:T(8,128)(2,1)S(1)}, bf16[16,96,128]{2,1,0:T(8,128)(2,1)S(1)}, u32[]{:S(2)}, u32[]{:S(2)}) %collective-permute-start.1) | collective-permute-done | bytes 393248 | tf_op jit(solution)/shard_map/ppermute | solution.py:588
  19.4 0.9 %shard_map.61 = bf16[16,96,128]{2,1,0:T(8,128)(2,1)} custom-call(bf16[16,96,128]{2,1,0:T(8,128)(2,1)S(1)} %get-tuple-element.31.keep_ref, bf16[16,96,128]{2,1,0:T(8,128)(2,1)S(1)} %collective-permute-done.1.arrived_ref), custom_call_target="tpu_custom_call" | custom-call | bytes 1048576 | tf_op jit(solution)/shard_map/pallas_call | solution.py:478
  20.3 8.7 %all-to-all-start = ((bf16[16,96,128]{2,1,0:T(8,128)(2,1)}), bf16[16,96,128]{2,1,0:T(8,128)(2,1)S(1)}, u32[]{:S(2)}, u32[]{:S(2)}) async-start(bf16[16,96,128]{2,1,0:T(8,128)(2,1)} %shard_map.61), calls=%async_computation | async-start | bytes 786432 | tf_op jit(solution)/shard_map/all_to_all | solution.py:590
  29.0 1.6 %collective-permute-start.2 = (bf16[2,32,16,128]{3,2,1,0:T(8,128)(2,1)S(1)}, bf16[2,32,16,128]{3,2,1,0:T(8,128)(2,1)S(1)}, u32[]{:S(2)}, u32[]{:S(2)}) collective-permute-start(bf16[2,32,16,128]{3,2,1,0:T(8,128)(2,1)S(1)} %get-tuple-element.36), channel_id=1, source_target_pairs={{0,1},{1,2},{2,3},{3,4},{4,5},{5,6},{6,7},{7,8},{8,9},{9,10},{10,1... | collective-permute-start | bytes 786440 | tf_op jit(solution)/shard_map/ppermute | solution.py:570
  30.6 7.9 %all-to-all-done.parts_ref = bf16[16,96,128]{2,1,0:T(8,128)(2,1)S(1)} async-done(((bf16[16,96,128]{2,1,0:T(8,128)(2,1)}), bf16[16,96,128]{2,1,0:T(8,128)(2,1)S(1)}, u32[]{:S(2)}, u32[]{:S(2)}) %all-to-all-start) | async-done | bytes 393248 | tf_op jit(solution)/shard_map/all_to_all | solution.py:590
  38.5 0.7 shard_map.62
  39.3 9.3 %all-to-all-start.1 = ((bf16[8,96,128]{2,1,0:T(8,128)(2,1)}), bf16[8,96,128]{2,1,0:T(8,128)(2,1)S(1)}, u32[]{:S(2)}, u32[]{:S(2)}) async-start(bf16[8,96,128]{2,1,0:T(8,128)(2,1)} %shard_map.62), calls=%async_computation.1 | async-start | bytes 393216 | tf_op jit(solution)/shard_map/all_to_all | solution.py:594
  48.5 0.0 collective-permute-done.2.low_ref
  48.5 6.2 %shard_map.63 = (bf16[32,4,16,128]{3,2,1,0:T(8,128)(2,1)}, bf16[32,4,16,128]{3,2,1,0:T(8,128)(2,1)}) custom-call(bf16[4,16,32,128]{3,2,1,0:T(8,128)(2,1)S(1)} %get-tuple-element.34.act_ref, bf16[4,16,32,128]{3,2,1,0:T(8,128)(2,1)S(1)} %get-tuple-element.35.cot_ref, bf16[2,32,16,128]{3,2,1,0:T(8,128)(2,1)S(1)} %collective-permute-done.2.low_ref, ...), custom_call_target="tpu_custom_call" | custom-call | flops 905969664 | bytes 1048576 | tf_op jit(solution)/shard_map/pallas_call | solution.py:478
  54.8 2.5 %all-to-all-done.1.parts_ref = bf16[8,96,128]{2,1,0:T(8,128)(2,1)S(1)} async-done(((bf16[8,96,128]{2,1,0:T(8,128)(2,1)}), bf16[8,96,128]{2,1,0:T(8,128)(2,1)S(1)}, u32[]{:S(2)}, u32[]{:S(2)}) %all-to-all-start.1) | async-done | bytes 196640 | tf_op jit(solution)/shard_map/all_to_all | solution.py:594
  57.3 11.1 %all_to_all.15.mine_ref = bf16[16,96,128]{2,1,0:T(8,128)(2,1)S(1)} all-to-all(bf16[16,96,128]{2,1,0:T(8,128)(2,1)S(1)} %shard_map.64), channel_id=1, replica_groups=mesh['z_hi'=2,'core'=2,'y'=4,'x'=4,'z_lo'=4] {'y','x'}, dimensions={0} | all-to-all | bytes 786432 | tf_op jit(solution)/shard_map/all_to_all | solution.py:598
  68.4 4.1 %collective-permute-start.3 = (bf16[16,96,128]{2,1,0:T(8,128)(2,1)S(1)}, bf16[16,96,128]{2,1,0:T(8,128)(2,1)S(1)}, u32[]{:S(2)}, u32[]{:S(2)}) collective-permute-start(bf16[16,96,128]{2,1,0:T(8,128)(2,1)S(1)} %all_to_all.15.mine_ref), channel_id=1, source_target_pairs={{0,64},{64,0},{1,65},{65,1},{2,66},{66,2},{3,67},{67,3},{4,68},{68... | collective-permute-start | bytes 1179656 | tf_op jit(solution)/shard_map/ppermute | solution.py:599
  72.6 1.3 %collective-permute-done.3.other_ref = bf16[16,96,128]{2,1,0:T(8,128)(2,1)S(1)} collective-permute-done((bf16[16,96,128]{2,1,0:T(8,128)(2,1)S(1)}, bf16[16,96,128]{2,1,0:T(8,128)(2,1)S(1)}, u32[]{:S(2)}, u32[]{:S(2)}) %collective-permute-start.3) | collective-permute-done | bytes 393248 | tf_op jit(solution)/shard_map/ppermute | solution.py:599
  73.9 5.1 %shard_map.65 = f32[32,864]{1,0:T(8,128)} custom-call(s32[1]{0:T(128)} %bitcast.core_ref, bf16[16,96,128]{2,1,0:T(8,128)(2,1)S(1)} %all_to_all.15.mine_ref, bf16[16,96,128]{2,1,0:T(8,128)(2,1)S(1)} %collective-permute-done.3.other_ref), custom_call_target="tpu_custom_call" | custom-call | flops 1000000000 | bytes 1048576 | tf_op jit(solution)/shard_map/pallas_call | solution.py:478
  (1 shorter events, 0.0 us)
Async XLA Ops:
  0.6 2.4 %copy-start = (bf16[32,864]{1,0:T(8,128)(2,1)S(1)}, bf16[32,864]{1,0:T(8,128)(2,1)}, u32[]{:S(2)}) copy-start(bf16[32,864]{1,0:T(8,128)(2,1)} %w_ref.2) | copy-start | bytes 165892
  1.7 11.3 %collective-permute-start = (bf16[3,32,16,128]{3,2,1,0:T(8,128)(2,1)S(1)}, bf16[3,32,16,128]{3,2,1,0:T(8,128)(2,1)S(1)}, u32[]{:S(2)}, u32[]{:S(2)}) collective-permute-start(bf16[3,32,16,128]{3,2,1,0:T(8,128)(2,1)S(1)} %shard_map.59), channel_id=1, source_target_pairs={{1,0},{2,1},{3,2},{4,3},{5,4},{6,5},{7,6},{8,7},{9,8},{10,9},{11,1... | collective-permute-start | bytes 1179656 | tf_op jit(solution)/shard_map/ppermute | solution.py:539
  14.8 4.6 %collective-permute-start.1 = (bf16[16,96,128]{2,1,0:T(8,128)(2,1)S(1)}, bf16[16,96,128]{2,1,0:T(8,128)(2,1)S(1)}, u32[]{:S(2)}, u32[]{:S(2)}) collective-permute-start(bf16[16,96,128]{2,1,0:T(8,128)(2,1)S(1)} %get-tuple-element.32), channel_id=1, source_target_pairs={{0,64},{64,0},{1,65},{65,1},{2,66},{66,2},{3,67},{67,3},{4,68},{68... | collective-permute-start | bytes 1179656 | tf_op jit(solution)/shard_map/ppermute | solution.py:588
  20.3 18.2 %all-to-all-start = ((bf16[16,96,128]{2,1,0:T(8,128)(2,1)}), bf16[16,96,128]{2,1,0:T(8,128)(2,1)S(1)}, u32[]{:S(2)}, u32[]{:S(2)}) async-start(bf16[16,96,128]{2,1,0:T(8,128)(2,1)} %shard_map.61), calls=%async_computation | async-start | bytes 786432 | tf_op jit(solution)/shard_map/all_to_all | solution.py:590
  29.0 19.5 %collective-permute-start.2 = (bf16[2,32,16,128]{3,2,1,0:T(8,128)(2,1)S(1)}, bf16[2,32,16,128]{3,2,1,0:T(8,128)(2,1)S(1)}, u32[]{:S(2)}, u32[]{:S(2)}) collective-permute-start(bf16[2,32,16,128]{3,2,1,0:T(8,128)(2,1)S(1)} %get-tuple-element.36), channel_id=1, source_target_pairs={{0,1},{1,2},{2,3},{3,4},{4,5},{5,6},{6,7},{7,8},{8,9},{9,10},{10,1... | collective-permute-start | bytes 786440 | tf_op jit(solution)/shard_map/ppermute | solution.py:570
  39.3 18.0 %all-to-all-start.1 = ((bf16[8,96,128]{2,1,0:T(8,128)(2,1)}), bf16[8,96,128]{2,1,0:T(8,128)(2,1)S(1)}, u32[]{:S(2)}, u32[]{:S(2)}) async-start(bf16[8,96,128]{2,1,0:T(8,128)(2,1)} %shard_map.62), calls=%async_computation.1 | async-start | bytes 393216 | tf_op jit(solution)/shard_map/all_to_all | solution.py:594
  68.4 5.5 %collective-permute-start.3 = (bf16[16,96,128]{2,1,0:T(8,128)(2,1)S(1)}, bf16[16,96,128]{2,1,0:T(8,128)(2,1)S(1)}, u32[]{:S(2)}, u32[]{:S(2)}) collective-permute-start(bf16[16,96,128]{2,1,0:T(8,128)(2,1)S(1)} %all_to_all.15.mine_ref), channel_id=1, source_target_pairs={{0,64},{64,0},{1,65},{65,1},{2,66},{66,2},{3,67},{67,3},{4,68},{68... | collective-permute-start | bytes 1179656 | tf_op jit(solution)/shard_map/ppermute | solution.py:599

commit v4 on v3

--- a/solution.py
+++ b/solution.py
@@ -48,6 +48,11 @@
     return [store[pl.ds(y, C, stride=ROWS), :] for y in range(ROWS)]
 
 
+def halo_planes(odd, one_ref, two_ref):
+    one, two = one_ref[...].astype(f32), two_ref[...].astype(f32)
+    return jnp.where(odd, two, one), jnp.where(odd, one, two)
+
+
 def rows_of(plane):
     return [plane[y].astype(f32) for y in range(ROWS)]
 
@@ -109,7 +114,8 @@
 
 
 def gram_inner(
-    act_hbm, cot_hbm, w_ref, out_ref, wg_ref, turned_act, turned_cot, flipped_ref, above_ref,
+    odd_ref, act_hbm, cot_hbm, w_ref,
+    out_ref, wg_ref, turned_act, turned_cot, flipped_ref, one_ref, two_ref,
     taps, cots, store, act_ref, cot_ref, sems,
 ):
     fetches = []
@@ -131,9 +137,6 @@
         fill_taps(taps, plane_at(x), rows)
         cot_rows = turned(cot_ref[x], store.at[2 * x + 1])
         fill_rows(cots, plane_at(x), cot_rows)
-        if x == PLANES - 1:
-            above_ref[0] = act_ref[x]
-            above_ref[1] = cot_ref[x]
         for y in range(ROWS):
             turned_act[x, y] = rows[y].astype(bf16)
             turned_cot[x, y] = cot_rows[y].astype(bf16)
@@ -144,6 +147,9 @@
     def blocks(value, count):
         return [value[i * TAPS : (i + 1) * TAPS] for i in range(count)]
 
+    plane = odd_ref[0] * (PLANES - 1)
+    one_ref[...] = cot_ref[plane]
+    two_ref[...] = cot_ref[PLANES - 1 - plane]
     near = (-1, 0, 1)
     sums = {}
 
@@ -196,20 +202,23 @@
 
 
 def gram_outer(
-    core_ref, first_ref, last_ref, in_ref, wg_ref, act_ref, high_ref, cot_ref,
+    core_ref, first_ref, last_ref, odd_ref, in_ref, wg_ref, act_ref, one_ref, two_ref, cot_ref,
     keep_ref, send_ref, taps, cots, out_ref, store,
 ):
-    for index in range(4):
+    below, above = halo_planes(odd_ref[0] == 1, one_ref, two_ref)
+    for index in range(6):
         zero_rows(taps, lane(index * RPAD))
-        if index < 2:
-            rows = rows_of(act_ref[index + 2])
-        else:
-            rows = turned(high_ref[index - 2], store.at[index - 2])
-        fill_taps(taps, plane_at(index), rows)
-    for slot in range(2):
+        if index in (0, 2, 3, 4, 5):
+            if index == 0:
+                rows = turned(below, store.at[0])
+            elif index == 5:
+                rows = turned(above, store.at[1])
+            else:
+                rows = rows_of(act_ref[index - 1])
+            fill_taps(taps, plane_at(index), rows)
+    for slot, x in ((0, 0), (1, 3)):
         zero_rows(cots, lane(slot * RPAD))
-    fill_rows(cots, plane_at(0), rows_of(cot_ref[PLANES - 1]))
-    fill_rows(cots, plane_at(1), turned(high_ref[2], store.at[2]))
+        fill_rows(cots, plane_at(slot), rows_of(cot_ref[x]))
 
     def stay(index):
         return taps[:, pl.ds(plane_at(index), WIDTH)]
@@ -226,14 +235,13 @@
     def padded(value):
         return jnp.concatenate([value, jnp.zeros((value.shape[0], LANES - TAPS), f32)], 1)
 
+    low = stay(0)
     gap = jnp.zeros((LANES - TAPS, WIDTH), bf16)
-    two, three = stay(0), stay(1)
-    four = dot_nt(shifted(taps, 2, five), jnp.concatenate([three, gap, two, gap], 0))
-    beyond = dot_nt(shifted(taps, 3, five), jnp.concatenate([three, gap], 0))
-    x1 = blocks(four[:, :LANES], 5)
-    x2 = blocks(four[:, LANES:] + beyond, 5)
-    w_low = dot_nt(shifted(cots, 1, near), three)
-    w_high = dot_nt(shifted(cots, 0, near), stay(2))
+    top = dot_nt(shifted(taps, 5, five), jnp.concatenate([stay(4), gap, stay(3), gap], 0))
+    x1 = blocks(top[:, :LANES], 5)
+    x2 = blocks(top[:, LANES:] + dot_nt(shifted(taps, 2, five), jnp.concatenate([low, gap], 0)), 5)
+    w_low = dot_nt(shifted(cots, 0, near), low)
+    w_high = dot_nt(shifted(cots, 1, near), stay(5))
 
     def edge(left, right, row):
         return padded(dot_nt(
@@ -266,8 +274,8 @@
         return value
 
     for base, dx, parts, pairs in (
-        (A_X1, 1, x1, ((2, 1),)),
-        (A_X2, 2, x2, ((2, 0), (3, 1))),
+        (A_X1, 1, x1, ((5, 4),)),
+        (A_X2, 2, x2, ((5, 3), (2, 0))),
     ):
         whole = cut(in_ref[base]) + parts[0]
         put(SLOT[(dx, "0")], whole)
@@ -305,6 +313,18 @@
     return jnp.concatenate([first, second, value[2 * C :]], 0).astype(bf16)
 
 
+def settle_all(value):
+    row = lax.broadcasted_iota(jnp.int32, value.shape, value.ndim - 2)
+    at = lax.broadcasted_iota(jnp.int32, value.shape, value.ndim - 1)
+    swapped = jnp.concatenate(
+        [value[..., C : 2 * C, :], value[..., :C, :], value[..., 2 * C :, :]], -2
+    )
+    both = value + swapped
+    high = lax.reduce_precision(both, 8, 7)
+    piece = jnp.where(row < C, high, both - high)
+    return jnp.where((at < TAPS) | (row >= 2 * C), value, piece).astype(bf16)
+
+
 def add_kernel(keep_ref, arrived_ref, out_ref):
     for i in range(HALF):
         out_ref[i] = settle(keep_ref[i].astype(f32) + arrived_ref[i].astype(f32))
@@ -320,7 +340,8 @@
 
 
 def conv_kernel(
-    act_ref, cot_ref, low_ref, high_ref, w_ref, flipped_ref, out_ref, back_ref,
+    odd_ref, act_ref, cot_ref, act_one, act_two, cot_one, cot_two, w_ref, flipped_ref,
+    out_ref, back_ref,
     act_taps, cot_taps, store, halos,
 ):
     step = 2
@@ -328,10 +349,10 @@
     def fill(which, index):
         planes, dst = ((act_ref, act_taps), (cot_ref, cot_taps))[which]
         zero_rows(dst, lane(index * RPAD))
-        if index == 0:
-            rows = turned(low_ref[which], halos.at[which, 0])
-        elif index == PLANES + 1:
-            rows = turned(high_ref[2 * which], halos.at[which, 1])
+        if index in (0, PLANES + 1):
+            pair = ((act_one, act_two), (cot_one, cot_two))[which]
+            side = index // (PLANES + 1)
+            rows = turned(halo_planes(odd_ref[0] == 1, *pair)[side], halos.at[which, side])
         else:
             rows = rows_of(planes[index - 1])
         fill_taps(dst, plane_at(index), rows)
@@ -486,10 +507,11 @@
     )(*inputs)
 
 
-def edge_kernel(act, cot, down, sems):
+def edge_kernel(odd_ref, act, one_ref, two_ref, sems):
+    plane = odd_ref[0] * (PLANES - 1)
     copies = [
-        pltpu.make_async_copy(source.at[:, plane], down.at[k], sems.at[k])
-        for k, (source, plane) in enumerate(((act, 0), (act, 1), (cot, 0)))
+        pltpu.make_async_copy(act.at[:, plane], one_ref, sems.at[0]),
+        pltpu.make_async_copy(act.at[:, PLANES - 1 - plane], two_ref, sems.at[1]),
     ]
     for copy in copies:
         copy.start()
@@ -497,18 +519,19 @@
         copy.wait()
 
 
-def edge_planes(act, cot):
+def edge_planes(odd, act):
+    plane = pltpu.VMEM((C, ROWS, LANES), bf16)
     return call(
         edge_kernel,
-        pltpu.VMEM((3, C, ROWS, LANES), bf16),
-        [pltpu.SemaphoreType.DMA((3,))],
-        (act, cot),
+        (plane, plane),
+        [pltpu.SemaphoreType.DMA((2,))],
+        (odd, act),
         mib=4,
-        specs=[IN_HBM] * 2,
-    )
-
-
-def conv(act, cot, low, high, weight, flipped):
+        specs=[SMEM, IN_HBM],
+    )
+
+
+def conv(odd, act, cot, halos, weight, flipped):
     taps = pltpu.VMEM((TAPS, 6 * RPAD * LANES), bf16)
     shape = jax.ShapeDtypeStruct((C, PLANES, ROWS, LANES), bf16)
     return call(
@@ -520,8 +543,9 @@
             pltpu.VMEM((2, PLANES, C * ROWS, LANES), f32),
             pltpu.VMEM((2, 2, C * ROWS, LANES), f32),
         ],
-        (act, cot, low, high, weight, flipped),
-        flops=4 * C * ORDER * PLANES * ROWS * LANES,
+        (odd, act, cot, *halos, weight, flipped),
+        scalars=1,
+        flops=20 * 10**9,
         mib=20,
     )
 
@@ -529,21 +553,27 @@
 def body(activations, cotangent, weight):
     space = ("y", "x", "z_lo")
     size = lax.axis_size(space)
-    up = [(i, i + 1) for i in range(size - 1)]
-    down = [(j, i) for i, j in up]
+    rounds = [
+        [pair for i in range(start, size - 1, 2) for pair in ((i, i + 1), (i + 1, i))]
+        for start in (1, 0)
+    ]
     hold = lax.optimization_barrier
 
-    act = pltpu.with_memory_space_constraint(activations[0], pltpu.HBM)
-    cot = pltpu.with_memory_space_constraint(cotangent[0], pltpu.HBM)
-    for_below = edge_planes(act, cot)
-    high = lax.ppermute(for_below, space, down)
     where = lax.axis_index(space)
     core = lax.axis_index("core").astype(jnp.int32).reshape(1)
     first = (where == 0).astype(jnp.int32).reshape(1)
     last = (where == size - 1).astype(jnp.int32).reshape(1)
-
+    odd = (where % 2).astype(jnp.int32).reshape(1)
+    activations, cotangent, core, first, last, odd = hold(
+        (activations, cotangent, core, first, last, odd)
+    )
+    act = pltpu.with_memory_space_constraint(activations[0], pltpu.HBM)
+    cot = pltpu.with_memory_space_constraint(cotangent[0], pltpu.HBM)
+    act_one, act_two = edge_planes(odd, act)
+    act_one = lax.ppermute(act_one, space, rounds[0])
+    act_two = lax.ppermute(act_two, space, rounds[1])
     turned_shape = pltpu.VMEM((PLANES, ROWS, C, LANES), bf16)
-    sums, wsums, turned_act, turned_cot, flipped, for_above = call(
+    sums, wsums, turned_act, turned_cot, flipped, cot_one, cot_two = call(
         gram_inner,
         (
             pltpu.VMEM((A_BLOCKS, TAPS, LANES), f32),
@@ -551,7 +581,8 @@
             turned_shape,
             turned_shape,
             jax.ShapeDtypeStruct((C, ORDER), bf16),
-            jax.ShapeDtypeStruct((2, C, ROWS, LANES), bf16),
+            jax.ShapeDtypeStruct((C, ROWS, LANES), bf16),
+            jax.ShapeDtypeStruct((C, ROWS, LANES), bf16),
         ),
         [
             pltpu.VMEM((TAPS, PLANES * RPAD * LANES), bf16),
@@ -561,25 +592,25 @@
             pltpu.VMEM((PLANES, C, ROWS, LANES), bf16),
             pltpu.SemaphoreType.DMA((2 * PLANES,)),
         ],
-        (act, cot, weight),
-        specs=[IN_HBM, IN_HBM, WHOLE],
+        (odd, act, cot, weight),
+        specs=[SMEM, IN_HBM, IN_HBM, WHOLE],
         flops=24 * 10**9 // 4,
         mib=MIB_INNER,
     )
-    for_above, sums, wsums = hold((for_above, sums, wsums))
-    low = lax.ppermute(for_above, space, up)
+    cot_one = lax.ppermute(cot_one, space, rounds[0])
+    cot_two = lax.ppermute(cot_two, space, rounds[1])
     blocks_half = jax.ShapeDtypeStruct((HALF, TAPS, LANES), bf16)
     keep, send = call(
         gram_outer,
         (blocks_half, blocks_half),
         [
-            pltpu.VMEM((TAPS, 4 * RPAD * LANES), bf16),
+            pltpu.VMEM((TAPS, 6 * RPAD * LANES), bf16),
             pltpu.VMEM((C, 2 * RPAD * LANES), bf16),
             pltpu.VMEM((2, HALF, TAPS, LANES), bf16),
-            pltpu.VMEM((3, C * ROWS, LANES), f32),
+            pltpu.VMEM((2, C * ROWS, LANES), f32),
         ],
-        (core, first, last, sums, wsums, turned_act, high, turned_cot),
-        scalars=3,
+        (core, first, last, odd, sums, wsums, turned_act, act_one, act_two, turned_cot),
+        scalars=4,
         flops=10**9,
         mib=MIB_OUTER,
     )
@@ -590,11 +621,13 @@
     parts = lax.all_to_all(mine, ("y", "x"), 0, 0, tiled=True)
     depth = lax.axis_size(("z_hi", "z_lo"))
     block = call(sum_kernel, jax.ShapeDtypeStruct((depth, TAPS, LANES), bf16), [], (parts,), mib=4)
-    block, act, cot, high, weight = hold((block, turned_act, turned_cot, high, weight))
+    block, act, cot = hold((block, turned_act, turned_cot))
     parts = lax.all_to_all(block, ("z_hi", "z_lo"), 0, 0, tiled=True)
-    out, back = conv(act, cot, low, high, weight, flipped)
+    halos = (act_one, act_two, cot_one, cot_two)
+    out, back = conv(odd, act, cot, halos, weight, flipped)
     parts, out, back = hold((parts, out, back))
-    block = call(sum_kernel, blocks_half, [], (parts,), mib=4)
+    block = settle_all(jnp.sum(parts.astype(f32), axis=0))
+    block = jnp.broadcast_to(block, (HALF, TAPS, LANES))
     whole = lax.all_to_all(block, ("y", "x"), 0, 0, tiled=True)
     other = lax.ppermute(whole, "core", swap)
     precond = call(

time: 79.4 us -> 76.4 us (0.962)
  waiting for transfers between devices: 15.7 us -> 10.9 us
  starting transfers between devices: 28.2 us -> 29.1 us
  local copies, waits for them, and re-layouts: 0.01 us -> 0.88 us
    ppermute x2 -> x4, starting transfers between devices: 2.89 us -> 9.83 us  [the longest x1 5.43 us: body(): act_two = lax.ppermute(act_two, space, rounds[1])]
    all_to_all x1, starting transfers between devices: 9.25 us -> 6.21 us  [body(): parts = lax.all_to_all(block, ('z_hi', 'z_lo'), 0, 0, tiled=True)]
    ppermute x2 -> x4, waiting for transfers between devices: 2.63 us -> 0.01 us  [the longest x1 0.01 us: body(): act_two = lax.ppermute(act_two, space, rounds[1])]
    all_to_all x1, waiting for transfers between devices: 7.9 us -> 5.76 us  [body(): parts = lax.all_to_all(mine, ('y', 'x'), 0, 0, tiled=True)]
    ppermute x1, starting transfers between devices: 3.24 us -> 1.33 us  [body(): arrived = lax.ppermute(send, 'core', swap)]
    all_to_all x1, starting transfers between devices: 8.71 us -> 7.56 us  [body(): parts = lax.all_to_all(mine, ('y', 'x'), 0, 0, tiled=True)]
    unnamed x2 -> x4, local copies, waits for them, and re-layouts: 0.01 us -> 0.82 us
    pallas_call x8 -> x7, Pallas kernels: 23.2 us -> 23.1 us  [call(): pl.pallas_call(kernel, out_shape=shapes, in_specs=specs or [SMEM] * scala...]
  transfers between devices with their start and end apart: 6 -> 8, of which waited for: 5 -> 4; matrix products, arithmetic and copies ran while one was open for 0% -> 0% of each run, Pallas kernels for 18% -> 19%
where the time goes in v4:
time: 76.4 us; the launch traced here: 76 us
  starting transfers between devices  29.1 us (38%)
  Pallas kernels  23.1 us (30%)
  blocking collectives  11.1 us (15%)
  waiting for transfers between devices  10.9 us (14%)
  local copies, waits for them, and re-layouts  0.88 us (1%)
  between operations  0.77 us (1%)
    pallas_call x7, Pallas kernels, call(): pl.pallas_call(kernel, out_shape=shapes, in_specs=specs or [SMEM] * scala...  23.1 us
    all_to_all x1, blocking collectives, body(): whole = lax.all_to_all(block, ('y', 'x'), 0, 0, tiled=True)  11.1 us
    all_to_all x1, starting transfers between devices, body(): parts = lax.all_to_all(mine, ('y', 'x'), 0, 0, tiled=True)  7.56 us
    all_to_all x1, starting transfers between devices, body(): parts = lax.all_to_all(block, ('z_hi', 'z_lo'), 0, 0, tiled=True)  6.21 us
    all_to_all x1, waiting for transfers between devices, body(): parts = lax.all_to_all(mine, ('y', 'x'), 0, 0, tiled=True)  5.76 us
    ppermute x1, starting transfers between devices, body(): act_two = lax.ppermute(act_two, space, rounds[1])  5.43 us
    ppermute x1, starting transfers between devices, body(): other = lax.ppermute(whole, 'core', swap)  4.14 us
    ppermute x1, starting transfers between devices, body(): cot_two = lax.ppermute(cot_two, space, rounds[1])  3.07 us
  transfers between devices with their start and end apart: 8, of which 4 were waited for; matrix products, arithmetic and copies ran while one was open for 0% of the time, Pallas kernels for 19%

profile of v4, /device:TPU:1, one launch (start us, length us, event | category | flops | bytes accessed | tf_op | source)
XLA Modules:
  0.0 76.0 jit_solution(10645003819092102863)
XLA Ops:
  0.6 1.0 %shard_map.59 = (bf16[32,16,128]{2,1,0:T(8,128)(2,1)S(1)}, bf16[32,16,128]{2,1,0:T(8,128)(2,1)S(1)}) custom-call(s32[1]{0:T(128)} %bitcast.3.odd_ref, bf16[32,4,16,128]{3,2,1,0:T(8,128)(2,1)} %bitcast.8), custom_call_target="tpu_custom_call" | custom-call | bytes 1048576 | tf_op jit(solution)/shard_map/pallas_call | solution.py:499
  1.6 0.7 collective-permute-start
  2.3 5.4 %collective-permute-start.1 = (bf16[32,16,128]{2,1,0:T(8,128)(2,1)S(1)}, bf16[32,16,128]{2,1,0:T(8,128)(2,1)S(1)}, u32[]{:S(2)}, u32[]{:S(2)}) collective-permute-start(bf16[32,16,128]{2,1,0:T(8,128)(2,1)S(1)} %get-tuple-element.38), channel_id=1, source_target_pairs={{0,1},{1,0},{2,3},{3,2},{4,5},{5,4},{6,7},{7,6},{8,9},{9,8},{10,11... | collective-permute-start | bytes 393224 | tf_op jit(solution)/shard_map/ppermute | solution.py:574
  7.8 0.8 %copy-done = bf16[32,864]{1,0:T(8,128)(2,1)S(1)} copy-done((bf16[32,864]{1,0:T(8,128)(2,1)S(1)}, bf16[32,864]{1,0:T(8,128)(2,1)}, u32[]{:S(2)}) %copy-start) | copy-done | bytes 55320
  8.6 7.3 %shard_map.58 = (f32[29,96,128]{2,1,0:T(8,128)S(1)}, f32[3,96,128]{2,1,0:T(8,128)S(1)}, bf16[4,16,32,128]{3,2,1,0:T(8,128)(2,1)S(1)}, bf16[4,16,32,128]{3,2,1,0:...) custom-call(s32[1]{0:T(128)} %bitcast.3.odd_ref, ...), custom_call_target="tpu_custom_call" | custom-call | flops 6000000000 | bytes 1048576 | tf_op jit(solution)/shard_map/pallas_call | solution.py:499
  15.9 0.0 collective-permute-done.1.two_ref.act_two
  15.9 1.8 %shard_map.60 = (bf16[16,96,128]{2,1,0:T(8,128)(2,1)S(1)}, bf16[16,96,128]{2,1,0:T(8,128)(2,1)S(1)}) custom-call(s32[1]{0:T(128)} %bitcast.core_ref, s32[1]{0:T(128)} %bitcast.1.first_ref, s32[1]{0:T(128)} %bitcast.2.last_ref, s32[1]{0:T(128)} %bitcast.3.odd_ref, f32[29,96,128]{2,1,0:T(8,128)S(1)} %get-tuple-element.34.in_ref, ...), custom_call_target="tpu_custom_call" | custom-call | flops 1000000000 | bytes 1048576 | tf_op jit(solution)/shard_map/pallas_call | solution.py:499
  17.8 1.3 %collective-permute-start.2 = (bf16[16,96,128]{2,1,0:T(8,128)(2,1)S(1)}, bf16[16,96,128]{2,1,0:T(8,128)(2,1)S(1)}, u32[]{:S(2)}, u32[]{:S(2)}) collective-permute-start(bf16[16,96,128]{2,1,0:T(8,128)(2,1)S(1)} %get-tuple-element.41), channel_id=1, source_target_pairs={{0,64},{64,0},{1,65},{65,1},{2,66},{66,2},{3,67},{67,3},{4,68},{68... | collective-permute-start | bytes 1179656 | tf_op jit(solution)/shard_map/ppermute | solution.py:619
  19.1 1.3 %collective-permute-done.2.arrived_ref = bf16[16,96,128]{2,1,0:T(8,128)(2,1)S(1)} collective-permute-done((bf16[16,96,128]{2,1,0:T(8,128)(2,1)S(1)}, bf16[16,96,128]{2,1,0:T(8,128)(2,1)S(1)}, u32[]{:S(2)}, u32[]{:S(2)}) %collective-permute-start.2) | collective-permute-done | bytes 393248 | tf_op jit(solution)/shard_map/ppermute | solution.py:619
  20.4 0.9 %shard_map.61 = bf16[16,96,128]{2,1,0:T(8,128)(2,1)} custom-call(bf16[16,96,128]{2,1,0:T(8,128)(2,1)S(1)} %get-tuple-element.40.keep_ref, bf16[16,96,128]{2,1,0:T(8,128)(2,1)S(1)} %collective-permute-done.2.arrived_ref), custom_call_target="tpu_custom_call" | custom-call | bytes 1048576 | tf_op jit(solution)/shard_map/pallas_call | solution.py:499
  21.3 7.6 %all-to-all-start = ((bf16[16,96,128]{2,1,0:T(8,128)(2,1)}), bf16[16,96,128]{2,1,0:T(8,128)(2,1)S(1)}, u32[]{:S(2)}, u32[]{:S(2)}) async-start(bf16[16,96,128]{2,1,0:T(8,128)(2,1)} %shard_map.61), calls=%async_computation | async-start | bytes 786432 | tf_op jit(solution)/shard_map/all_to_all | solution.py:621
  28.9 0.7 collective-permute-start.3
  29.6 3.1 %collective-permute-start.4 = (bf16[32,16,128]{2,1,0:T(8,128)(2,1)S(1)}, bf16[32,16,128]{2,1,0:T(8,128)(2,1)S(1)}, u32[]{:S(2)}, u32[]{:S(2)}) collective-permute-start(bf16[32,16,128]{2,1,0:T(8,128)(2,1)S(1)} %get-tuple-element.46), channel_id=1, source_target_pairs={{0,1},{1,0},{2,3},{3,2},{4,5},{5,4},{6,7},{7,6},{8,9},{9,8},{10,11... | collective-permute-start | bytes 393224 | tf_op jit(solution)/shard_map/ppermute | solution.py:601
  32.7 5.8 %all-to-all-done.parts_ref = bf16[16,96,128]{2,1,0:T(8,128)(2,1)S(1)} async-done(((bf16[16,96,128]{2,1,0:T(8,128)(2,1)}), bf16[16,96,128]{2,1,0:T(8,128)(2,1)S(1)}, u32[]{:S(2)}, u32[]{:S(2)}) %all-to-all-start) | async-done | bytes 393248 | tf_op jit(solution)/shard_map/all_to_all | solution.py:621
  38.4 0.7 shard_map.62
  39.2 6.2 %all-to-all-start.1 = ((bf16[8,96,128]{2,1,0:T(8,128)(2,1)}), bf16[8,96,128]{2,1,0:T(8,128)(2,1)S(1)}, u32[]{:S(2)}, u32[]{:S(2)}) async-start(bf16[8,96,128]{2,1,0:T(8,128)(2,1)} %shard_map.62), calls=%async_computation.1 | async-start | bytes 393216 | tf_op jit(solution)/shard_map/all_to_all | solution.py:625
  45.4 6.3 %shard_map.63 = (bf16[32,4,16,128]{3,2,1,0:T(8,128)(2,1)}, bf16[32,4,16,128]{3,2,1,0:T(8,128)(2,1)}) custom-call(s32[1]{0:T(128)} %bitcast.3.odd_ref, bf16[4,16,32,128]{3,2,1,0:T(8,128)(2,1)S(1)} %get-tuple-element.43.act_ref, bf16[4,16,32,128]{3,2,1,0:T(8,128)(2,1)S(1)} %get-tuple-element.44.cot_ref, ...), custom_call_target="tpu_custom_call" | custom-call | flops 20000000000 | bytes 1048576 | tf_op jit(solution)/shard_map/pallas_call | solution.py:499
  51.7 2.4 %all-to-all-done.1 = bf16[8,96,128]{2,1,0:T(8,128)(2,1)S(1)} async-done(((bf16[8,96,128]{2,1,0:T(8,128)(2,1)}), bf16[8,96,128]{2,1,0:T(8,128)(2,1)S(1)}, u32[]{:S(2)}, u32[]{:S(2)}) %all-to-all-start.1) | async-done | bytes 196640 | tf_op jit(solution)/shard_map/all_to_all | solution.py:625
  54.1 0.1 fusion.1
  54.2 0.1 broadcast_in_dim.11
  54.3 11.1 %all_to_all.15.mine_ref = bf16[16,96,128]{2,1,0:T(8,128)(2,1)S(1)} all-to-all(bf16[16,96,128]{2,1,0:T(8,128)(2,1)S(1)} %broadcast_in_dim.11), channel_id=1, replica_groups=mesh['z_hi'=2,'core'=2,'y'=4,'x'=4,'z_lo'=4] {'y','x'}, dimensions={0} | all-to-all | bytes 786432 | tf_op jit(solution)/shard_map/all_to_all | solution.py:631
  65.4 4.1 %collective-permute-start.5 = (bf16[16,96,128]{2,1,0:T(8,128)(2,1)S(1)}, bf16[16,96,128]{2,1,0:T(8,128)(2,1)S(1)}, u32[]{:S(2)}, u32[]{:S(2)}) collective-permute-start(bf16[16,96,128]{2,1,0:T(8,128)(2,1)S(1)} %all_to_all.15.mine_ref), channel_id=1, source_target_pairs={{0,64},{64,0},{1,65},{65,1},{2,66},{66,2},{3,67},{67,3},{4,68},{68... | collective-permute-start | bytes 1179656 | tf_op jit(solution)/shard_map/ppermute | solution.py:632
  69.6 1.3 %collective-permute-done.5.other_ref = bf16[16,96,128]{2,1,0:T(8,128)(2,1)S(1)} collective-permute-done((bf16[16,96,128]{2,1,0:T(8,128)(2,1)S(1)}, bf16[16,96,128]{2,1,0:T(8,128)(2,1)S(1)}, u32[]{:S(2)}, u32[]{:S(2)}) %collective-permute-start.5) | collective-permute-done | bytes 393248 | tf_op jit(solution)/shard_map/ppermute | solution.py:632
  70.9 5.1 %shard_map.64 = f32[32,864]{1,0:T(8,128)} custom-call(s32[1]{0:T(128)} %bitcast.core_ref, bf16[16,96,128]{2,1,0:T(8,128)(2,1)S(1)} %all_to_all.15.mine_ref, bf16[16,96,128]{2,1,0:T(8,128)(2,1)S(1)} %collective-permute-done.5.other_ref), custom_call_target="tpu_custom_call" | custom-call | flops 1000000000 | bytes 1048576 | tf_op jit(solution)/shard_map/pallas_call | solution.py:499
  (10 shorter events, 0.1 us)
Async XLA Ops:
  1.6 14.3 %collective-permute-start = (bf16[32,16,128]{2,1,0:T(8,128)(2,1)S(1)}, bf16[32,16,128]{2,1,0:T(8,128)(2,1)S(1)}, u32[]{:S(2)}, u32[]{:S(2)}) collective-permute-start(bf16[32,16,128]{2,1,0:T(8,128)(2,1)S(1)} %get-tuple-element.37), channel_id=1, source_target_pairs={{1,2},{2,1},{3,4},{4,3},{5,6},{6,5},{7,8},{8,7},{9,10},{10,9},{11,... | collective-permute-start | bytes 393224 | tf_op jit(solution)/shard_map/ppermute | solution.py:573
  2.3 13.6 %collective-permute-start.1 = (bf16[32,16,128]{2,1,0:T(8,128)(2,1)S(1)}, bf16[32,16,128]{2,1,0:T(8,128)(2,1)S(1)}, u32[]{:S(2)}, u32[]{:S(2)}) collective-permute-start(bf16[32,16,128]{2,1,0:T(8,128)(2,1)S(1)} %get-tuple-element.38), channel_id=1, source_target_pairs={{0,1},{1,0},{2,3},{3,2},{4,5},{5,4},{6,7},{7,6},{8,9},{9,8},{10,11... | collective-permute-start | bytes 393224 | tf_op jit(solution)/shard_map/ppermute | solution.py:574
  7.8 0.8 %copy-start = (bf16[32,864]{1,0:T(8,128)(2,1)S(1)}, bf16[32,864]{1,0:T(8,128)(2,1)}, u32[]{:S(2)}) copy-start(bf16[32,864]{1,0:T(8,128)(2,1)} %w_ref.3) | copy-start | bytes 165892
  17.8 2.7 %collective-permute-start.2 = (bf16[16,96,128]{2,1,0:T(8,128)(2,1)S(1)}, bf16[16,96,128]{2,1,0:T(8,128)(2,1)S(1)}, u32[]{:S(2)}, u32[]{:S(2)}) collective-permute-start(bf16[16,96,128]{2,1,0:T(8,128)(2,1)S(1)} %get-tuple-element.41), channel_id=1, source_target_pairs={{0,64},{64,0},{1,65},{65,1},{2,66},{66,2},{3,67},{67,3},{4,68},{68... | collective-permute-start | bytes 1179656 | tf_op jit(solution)/shard_map/ppermute | solution.py:619
  20.4 24.9 %copy-start.1 = (bf16[32,864]{1,0:T(8,128)(2,1)S(1)}, bf16[32,864]{1,0:T(8,128)(2,1)}, u32[]{:S(2)}) copy-start(bf16[32,864]{1,0:T(8,128)(2,1)} %w_ref.3) | copy-start | bytes 165892
  21.3 17.1 %all-to-all-start = ((bf16[16,96,128]{2,1,0:T(8,128)(2,1)}), bf16[16,96,128]{2,1,0:T(8,128)(2,1)S(1)}, u32[]{:S(2)}, u32[]{:S(2)}) async-start(bf16[16,96,128]{2,1,0:T(8,128)(2,1)} %shard_map.61), calls=%async_computation | async-start | bytes 786432 | tf_op jit(solution)/shard_map/all_to_all | solution.py:621
  28.9 16.5 %collective-permute-start.3 = (bf16[32,16,128]{2,1,0:T(8,128)(2,1)S(1)}, bf16[32,16,128]{2,1,0:T(8,128)(2,1)S(1)}, u32[]{:S(2)}, u32[]{:S(2)}) collective-permute-start(bf16[32,16,128]{2,1,0:T(8,128)(2,1)S(1)} %get-tuple-element.45), channel_id=1, source_target_pairs={{1,2},{2,1},{3,4},{4,3},{5,6},{6,5},{7,8},{8,7},{9,10},{10,9},{11,... | collective-permute-start | bytes 393224 | tf_op jit(solution)/shard_map/ppermute | solution.py:600
  29.6 15.8 %collective-permute-start.4 = (bf16[32,16,128]{2,1,0:T(8,128)(2,1)S(1)}, bf16[32,16,128]{2,1,0:T(8,128)(2,1)S(1)}, u32[]{:S(2)}, u32[]{:S(2)}) collective-permute-start(bf16[32,16,128]{2,1,0:T(8,128)(2,1)S(1)} %get-tuple-element.46), channel_id=1, source_target_pairs={{0,1},{1,0},{2,3},{3,2},{4,5},{5,4},{6,7},{7,6},{8,9},{9,8},{10,11... | collective-permute-start | bytes 393224 | tf_op jit(solution)/shard_map/ppermute | solution.py:601
  39.2 14.9 %all-to-all-start.1 = ((bf16[8,96,128]{2,1,0:T(8,128)(2,1)}), bf16[8,96,128]{2,1,0:T(8,128)(2,1)S(1)}, u32[]{:S(2)}, u32[]{:S(2)}) async-start(bf16[8,96,128]{2,1,0:T(8,128)(2,1)} %shard_map.62), calls=%async_computation.1 | async-start | bytes 393216 | tf_op jit(solution)/shard_map/all_to_all | solution.py:625
  65.4 5.5 %collective-permute-start.5 = (bf16[16,96,128]{2,1,0:T(8,128)(2,1)S(1)}, bf16[16,96,128]{2,1,0:T(8,128)(2,1)S(1)}, u32[]{:S(2)}, u32[]{:S(2)}) collective-permute-start(bf16[16,96,128]{2,1,0:T(8,128)(2,1)S(1)} %all_to_all.15.mine_ref), channel_id=1, source_target_pairs={{0,64},{64,0},{1,65},{65,1},{2,66},{66,2},{3,67},{67,3},{4,68},{68... | collective-permute-start | bytes 1179656 | tf_op jit(solution)/shard_map/ppermute | solution.py:632

commit v5 on v4

--- a/solution.py
+++ b/solution.py
@@ -114,8 +114,8 @@
 
 
 def gram_inner(
-    odd_ref, act_hbm, cot_hbm, w_ref,
-    out_ref, wg_ref, turned_act, turned_cot, flipped_ref, one_ref, two_ref,
+    odd_ref, act_hbm, cot_hbm,
+    out_ref, wg_ref, turned_act, turned_cot, one_ref, two_ref,
     taps, cots, store, act_ref, cot_ref, sems,
 ):
     fetches = []
@@ -126,7 +126,6 @@
             )
     for fetch in fetches:
         fetch.start()
-    flip_taps(w_ref, flipped_ref)
     for x in range(PLANES):
         zero_rows(taps, lane(x * RPAD))
         zero_rows(cots, lane(x * RPAD))
@@ -156,23 +155,30 @@
     def add(key, value):
         sums[key] = value if key not in sums else sums[key] + value
 
-    for x in range(PLANES):
-        stay = jnp.concatenate(
+    stays = [
+        jnp.concatenate(
             [taps[:, pl.ds(plane_at(x), WIDTH)], cots[:, pl.ds(plane_at(x), WIDTH)]], 0
         )
+        for x in range(PLANES)
+    ]
+    for x in range(PLANES):
+        stay = stays[x]
         level = dot_nt(shifted(taps, x, (0, 1, 2)), stay)
         zero, one, two = blocks(level, 3)
         cot_rows = [dot_nt(shifted(cots, x, near), stay)]
         if x + 1 < PLANES:
-            up = dot_nt(shifted(taps, x + 1, (0, 1, 2, -1, -2)), stay)
-            add("x1", up)
+            moving = shifted(taps, x + 1, (0, 1, 2, -1, -2))
+            if x == 0:
+                add("x1", dot_nt(moving, stay))
+            else:
+                pair = dot_nt(moving, jnp.concatenate([stay, stays[x - 1]], 0))
+                add("x1", pair[:, :LANES])
+                add("x2", pair[:, LANES:])
             cot_rows.append(dot_nt(shifted(cots, x + 1, near), stay))
             add("w2", cot_rows[1])
         if x >= 1:
             add("w0", dot_nt(shifted(cots, x - 1, near), stay))
         add("w1", cot_rows[0])
-        if x + 2 < PLANES:
-            add("x2", dot_nt(shifted(taps, x + 2, (0, 1, 2, -1, -2)), stay))
         edge = {}
         for name, row in (("F", 0), ("L", ROWS - 1)):
             stay_row = taps[:, pl.ds(plane_at(x, row), LANES)]
@@ -340,9 +346,9 @@
 
 
 def conv_kernel(
-    odd_ref, act_ref, cot_ref, act_one, act_two, cot_one, cot_two, w_ref, flipped_ref,
+    odd_ref, act_ref, cot_ref, act_one, act_two, cot_one, cot_two, w_ref,
     out_ref, back_ref,
-    act_taps, cot_taps, store, halos,
+    act_taps, cot_taps, store, halos, flipped_ref,
 ):
     step = 2
 
@@ -378,6 +384,7 @@
         for channel in range(C):
             target[channel, x] = store[which, x, pl.ds(channel, ROWS, stride=C), :].astype(bf16)
 
+    flip_taps(w_ref, flipped_ref)
     weights = (w_ref[...], flipped_ref[...])
     fills = [(which, index) for which in (0, 1) for index in range(PLANES + 2)]
     for _ in range(3):
@@ -531,7 +538,7 @@
     )
 
 
-def conv(odd, act, cot, halos, weight, flipped):
+def conv(odd, act, cot, halos, weight):
     taps = pltpu.VMEM((TAPS, 6 * RPAD * LANES), bf16)
     shape = jax.ShapeDtypeStruct((C, PLANES, ROWS, LANES), bf16)
     return call(
@@ -542,8 +549,9 @@
             taps,
             pltpu.VMEM((2, PLANES, C * ROWS, LANES), f32),
             pltpu.VMEM((2, 2, C * ROWS, LANES), f32),
+            pltpu.VMEM((C, ORDER), bf16),
         ],
-        (odd, act, cot, *halos, weight, flipped),
+        (odd, act, cot, *halos, weight),
         scalars=1,
         flops=20 * 10**9,
         mib=20,
@@ -573,14 +581,13 @@
     act_one = lax.ppermute(act_one, space, rounds[0])
     act_two = lax.ppermute(act_two, space, rounds[1])
     turned_shape = pltpu.VMEM((PLANES, ROWS, C, LANES), bf16)
-    sums, wsums, turned_act, turned_cot, flipped, cot_one, cot_two = call(
+    sums, wsums, turned_act, turned_cot, cot_one, cot_two = call(
         gram_inner,
         (
             pltpu.VMEM((A_BLOCKS, TAPS, LANES), f32),
             pltpu.VMEM((3, TAPS, LANES), f32),
             turned_shape,
             turned_shape,
-            jax.ShapeDtypeStruct((C, ORDER), bf16),
             jax.ShapeDtypeStruct((C, ROWS, LANES), bf16),
             jax.ShapeDtypeStruct((C, ROWS, LANES), bf16),
         ),
@@ -592,8 +599,8 @@
             pltpu.VMEM((PLANES, C, ROWS, LANES), bf16),
             pltpu.SemaphoreType.DMA((2 * PLANES,)),
         ],
-        (odd, act, cot, weight),
-        specs=[SMEM, IN_HBM, IN_HBM, WHOLE],
+        (odd, act, cot),
+        specs=[SMEM, IN_HBM, IN_HBM],
         flops=24 * 10**9 // 4,
         mib=MIB_INNER,
     )
@@ -624,7 +631,7 @@
     block, act, cot = hold((block, turned_act, turned_cot))
     parts = lax.all_to_all(block, ("z_hi", "z_lo"), 0, 0, tiled=True)
     halos = (act_one, act_two, cot_one, cot_two)
-    out, back = conv(odd, act, cot, halos, weight, flipped)
+    out, back = conv(odd, act, cot, halos, weight)
     parts, out, back = hold((parts, out, back))
     block = settle_all(jnp.sum(parts.astype(f32), axis=0))
     block = jnp.broadcast_to(block, (HALF, TAPS, LANES))

time: 76.4 us -> 75.3 us (0.986)
  local copies, waits for them, and re-layouts: 0.88 us -> 0.06 us
    unnamed x4 -> x2, local copies, waits for them, and re-layouts: 0.82 us -> 0.01 us
  transfers between devices with their start and end apart: 8 -> 8, of which waited for: 4 -> 4; matrix products, arithmetic and copies ran while one was open for 0% -> 0% of each run, Pallas kernels for 19% -> 18%
where the time goes in v5:
time: 75.3 us; the launch traced here: 74.9 us
  starting transfers between devices  29.7 us (39%)
  Pallas kernels  22.5 us (30%)
  blocking collectives  11.1 us (15%)
  waiting for transfers between devices  10.6 us (14%)
  between operations  0.76 us (1%)
    pallas_call x7, Pallas kernels, call(): pl.pallas_call(kernel, out_shape=shapes, in_specs=specs or [SMEM] * scala...  22.5 us
    all_to_all x1, blocking collectives, body(): whole = lax.all_to_all(block, ('y', 'x'), 0, 0, tiled=True)  11.1 us
    all_to_all x1, starting transfers between devices, body(): parts = lax.all_to_all(mine, ('y', 'x'), 0, 0, tiled=True)  7.52 us
    all_to_all x1, starting transfers between devices, body(): parts = lax.all_to_all(block, ('z_hi', 'z_lo'), 0, 0, tiled=True)  6.79 us
    all_to_all x1, waiting for transfers between devices, body(): parts = lax.all_to_all(mine, ('y', 'x'), 0, 0, tiled=True)  5.75 us
    ppermute x1, starting transfers between devices, body(): act_two = lax.ppermute(act_two, space, rounds[1])  5.43 us
    ppermute x1, starting transfers between devices, body(): other = lax.ppermute(whole, 'core', swap)  4.14 us
    ppermute x1, starting transfers between devices, body(): cot_two = lax.ppermute(cot_two, space, rounds[1])  3.08 us
  transfers between devices with their start and end apart: 8, of which 4 were waited for; matrix products, arithmetic and copies ran while one was open for 0% of the time, Pallas kernels for 18%

profile of v5, /device:TPU:1, one launch (start us, length us, event | category | flops | bytes accessed | tf_op | source)
XLA Modules:
  0.0 74.9 jit_solution(7278610667653139756)
XLA Ops:
  0.6 1.0 %shard_map.59 = (bf16[32,16,128]{2,1,0:T(8,128)(2,1)S(1)}, bf16[32,16,128]{2,1,0:T(8,128)(2,1)S(1)}) custom-call(s32[1]{0:T(128)} %bitcast.3.odd_ref, bf16[32,4,16,128]{3,2,1,0:T(8,128)(2,1)} %bitcast.8), custom_call_target="tpu_custom_call" | custom-call | bytes 1048576 | tf_op jit(solution)/shard_map/pallas_call | solution.py:506
  1.6 0.7 collective-permute-start
  2.3 5.4 %collective-permute-start.1 = (bf16[32,16,128]{2,1,0:T(8,128)(2,1)S(1)}, bf16[32,16,128]{2,1,0:T(8,128)(2,1)S(1)}, u32[]{:S(2)}, u32[]{:S(2)}) collective-permute-start(bf16[32,16,128]{2,1,0:T(8,128)(2,1)S(1)} %get-tuple-element.37), channel_id=1, source_target_pairs={{0,1},{1,0},{2,3},{3,2},{4,5},{5,4},{6,7},{7,6},{8,9},{9,8},{10,11... | collective-permute-start | bytes 393224 | tf_op jit(solution)/shard_map/ppermute | solution.py:582
  7.8 6.4 %shard_map.58 = (f32[29,96,128]{2,1,0:T(8,128)S(1)}, f32[3,96,128]{2,1,0:T(8,128)S(1)}, bf16[4,16,32,128]{3,2,1,0:T(8,128)(2,1)S(1)}, bf16[4,16,32,128]{3,2,1,0:...) custom-call(s32[1]{0:T(128)} %bitcast.3.odd_ref, bf16[32,4,16,128]{3,2,1,0:T(8,128)(2,1)} %bitcast.9, ...), custom_call_target="tpu_custom_call" | custom-call | flops 6000000000 | bytes 1048576 | tf_op jit(solution)/shard_map/pallas_call | solution.py:506
  14.2 0.0 collective-permute-done.1.two_ref.act_two
  14.2 1.9 %shard_map.60 = (bf16[16,96,128]{2,1,0:T(8,128)(2,1)S(1)}, bf16[16,96,128]{2,1,0:T(8,128)(2,1)S(1)}) custom-call(s32[1]{0:T(128)} %bitcast.core_ref, s32[1]{0:T(128)} %bitcast.1.first_ref, s32[1]{0:T(128)} %bitcast.2.last_ref, s32[1]{0:T(128)} %bitcast.3.odd_ref, f32[29,96,128]{2,1,0:T(8,128)S(1)} %get-tuple-element.33.in_ref, ...), custom_call_target="tpu_custom_call" | custom-call | flops 1000000000 | bytes 1048576 | tf_op jit(solution)/shard_map/pallas_call | solution.py:506
  16.1 1.4 %collective-permute-start.2 = (bf16[16,96,128]{2,1,0:T(8,128)(2,1)S(1)}, bf16[16,96,128]{2,1,0:T(8,128)(2,1)S(1)}, u32[]{:S(2)}, u32[]{:S(2)}) collective-permute-start(bf16[16,96,128]{2,1,0:T(8,128)(2,1)S(1)} %get-tuple-element.40), channel_id=1, source_target_pairs={{0,64},{64,0},{1,65},{65,1},{2,66},{66,2},{3,67},{67,3},{4,68},{68... | collective-permute-start | bytes 1179656 | tf_op jit(solution)/shard_map/ppermute | solution.py:626
  17.4 1.3 %collective-permute-done.2.arrived_ref = bf16[16,96,128]{2,1,0:T(8,128)(2,1)S(1)} collective-permute-done((bf16[16,96,128]{2,1,0:T(8,128)(2,1)S(1)}, bf16[16,96,128]{2,1,0:T(8,128)(2,1)S(1)}, u32[]{:S(2)}, u32[]{:S(2)}) %collective-permute-start.2) | collective-permute-done | bytes 393248 | tf_op jit(solution)/shard_map/ppermute | solution.py:626
  18.8 0.9 %shard_map.61 = bf16[16,96,128]{2,1,0:T(8,128)(2,1)} custom-call(bf16[16,96,128]{2,1,0:T(8,128)(2,1)S(1)} %get-tuple-element.39.keep_ref, bf16[16,96,128]{2,1,0:T(8,128)(2,1)S(1)} %collective-permute-done.2.arrived_ref), custom_call_target="tpu_custom_call" | custom-call | bytes 1048576 | tf_op jit(solution)/shard_map/pallas_call | solution.py:506
  19.7 7.5 %all-to-all-start = ((bf16[16,96,128]{2,1,0:T(8,128)(2,1)}), bf16[16,96,128]{2,1,0:T(8,128)(2,1)S(1)}, u32[]{:S(2)}, u32[]{:S(2)}) async-start(bf16[16,96,128]{2,1,0:T(8,128)(2,1)} %shard_map.61), calls=%async_computation | async-start | bytes 786432 | tf_op jit(solution)/shard_map/all_to_all | solution.py:628
  27.2 0.7 collective-permute-start.3
  27.9 3.1 %collective-permute-start.4 = (bf16[32,16,128]{2,1,0:T(8,128)(2,1)S(1)}, bf16[32,16,128]{2,1,0:T(8,128)(2,1)S(1)}, u32[]{:S(2)}, u32[]{:S(2)}) collective-permute-start(bf16[32,16,128]{2,1,0:T(8,128)(2,1)S(1)} %get-tuple-element.45), channel_id=1, source_target_pairs={{0,1},{1,0},{2,3},{3,2},{4,5},{5,4},{6,7},{7,6},{8,9},{9,8},{10,11... | collective-permute-start | bytes 393224 | tf_op jit(solution)/shard_map/ppermute | solution.py:608
  31.0 5.7 %all-to-all-done.parts_ref = bf16[16,96,128]{2,1,0:T(8,128)(2,1)S(1)} async-done(((bf16[16,96,128]{2,1,0:T(8,128)(2,1)}), bf16[16,96,128]{2,1,0:T(8,128)(2,1)S(1)}, u32[]{:S(2)}, u32[]{:S(2)}) %all-to-all-start) | async-done | bytes 393248 | tf_op jit(solution)/shard_map/all_to_all | solution.py:628
  36.7 0.7 shard_map.62
  37.4 6.8 %all-to-all-start.1 = ((bf16[8,96,128]{2,1,0:T(8,128)(2,1)}), bf16[8,96,128]{2,1,0:T(8,128)(2,1)S(1)}, u32[]{:S(2)}, u32[]{:S(2)}) async-start(bf16[8,96,128]{2,1,0:T(8,128)(2,1)} %shard_map.62), calls=%async_computation.1 | async-start | bytes 393216 | tf_op jit(solution)/shard_map/all_to_all | solution.py:632
  44.2 0.0 collective-permute-done.4.cot_two
  44.3 6.6 %shard_map.63 = (bf16[32,4,16,128]{3,2,1,0:T(8,128)(2,1)}, bf16[32,4,16,128]{3,2,1,0:T(8,128)(2,1)}) custom-call(s32[1]{0:T(128)} %bitcast.3.odd_ref, bf16[4,16,32,128]{3,2,1,0:T(8,128)(2,1)S(1)} %get-tuple-element.42.act_ref, bf16[4,16,32,128]{3,2,1,0:T(8,128)(2,1)S(1)} %get-tuple-element.43.cot_ref, ...), custom_call_target="tpu_custom_call" | custom-call | flops 20000000000 | bytes 1048576 | tf_op jit(solution)/shard_map/pallas_call | solution.py:506
  50.8 2.1 %all-to-all-done.1 = bf16[8,96,128]{2,1,0:T(8,128)(2,1)S(1)} async-done(((bf16[8,96,128]{2,1,0:T(8,128)(2,1)}), bf16[8,96,128]{2,1,0:T(8,128)(2,1)S(1)}, u32[]{:S(2)}, u32[]{:S(2)}) %all-to-all-start.1) | async-done | bytes 196640 | tf_op jit(solution)/shard_map/all_to_all | solution.py:632
  53.0 0.1 fusion.1
  53.1 0.1 broadcast_in_dim.11
  53.1 11.1 %all_to_all.15.mine_ref = bf16[16,96,128]{2,1,0:T(8,128)(2,1)S(1)} all-to-all(bf16[16,96,128]{2,1,0:T(8,128)(2,1)S(1)} %broadcast_in_dim.11), channel_id=1, replica_groups=mesh['z_hi'=2,'core'=2,'y'=4,'x'=4,'z_lo'=4] {'y','x'}, dimensions={0} | all-to-all | bytes 786432 | tf_op jit(solution)/shard_map/all_to_all | solution.py:638
  64.3 4.1 %collective-permute-start.5 = (bf16[16,96,128]{2,1,0:T(8,128)(2,1)S(1)}, bf16[16,96,128]{2,1,0:T(8,128)(2,1)S(1)}, u32[]{:S(2)}, u32[]{:S(2)}) collective-permute-start(bf16[16,96,128]{2,1,0:T(8,128)(2,1)S(1)} %all_to_all.15.mine_ref), channel_id=1, source_target_pairs={{0,64},{64,0},{1,65},{65,1},{2,66},{66,2},{3,67},{67,3},{4,68},{68... | collective-permute-start | bytes 1179656 | tf_op jit(solution)/shard_map/ppermute | solution.py:639
  68.4 1.3 %collective-permute-done.5.other_ref = bf16[16,96,128]{2,1,0:T(8,128)(2,1)S(1)} collective-permute-done((bf16[16,96,128]{2,1,0:T(8,128)(2,1)S(1)}, bf16[16,96,128]{2,1,0:T(8,128)(2,1)S(1)}, u32[]{:S(2)}, u32[]{:S(2)}) %collective-permute-start.5) | collective-permute-done | bytes 393248 | tf_op jit(solution)/shard_map/ppermute | solution.py:639
  69.8 5.1 %shard_map.64 = f32[32,864]{1,0:T(8,128)} custom-call(s32[1]{0:T(128)} %bitcast.core_ref, bf16[16,96,128]{2,1,0:T(8,128)(2,1)S(1)} %all_to_all.15.mine_ref, bf16[16,96,128]{2,1,0:T(8,128)(2,1)S(1)} %collective-permute-done.5.other_ref), custom_call_target="tpu_custom_call" | custom-call | flops 1000000000 | bytes 1048576 | tf_op jit(solution)/shard_map/pallas_call | solution.py:506
  (8 shorter events, 0.1 us)
Async XLA Ops:
  1.6 12.5 %collective-permute-start = (bf16[32,16,128]{2,1,0:T(8,128)(2,1)S(1)}, bf16[32,16,128]{2,1,0:T(8,128)(2,1)S(1)}, u32[]{:S(2)}, u32[]{:S(2)}) collective-permute-start(bf16[32,16,128]{2,1,0:T(8,128)(2,1)S(1)} %get-tuple-element.36), channel_id=1, source_target_pairs={{1,2},{2,1},{3,4},{4,3},{5,6},{6,5},{7,8},{8,7},{9,10},{10,9},{11,... | collective-permute-start | bytes 393224 | tf_op jit(solution)/shard_map/ppermute | solution.py:581
  2.3 11.9 %collective-permute-start.1 = (bf16[32,16,128]{2,1,0:T(8,128)(2,1)S(1)}, bf16[32,16,128]{2,1,0:T(8,128)(2,1)S(1)}, u32[]{:S(2)}, u32[]{:S(2)}) collective-permute-start(bf16[32,16,128]{2,1,0:T(8,128)(2,1)S(1)} %get-tuple-element.37), channel_id=1, source_target_pairs={{0,1},{1,0},{2,3},{3,2},{4,5},{5,4},{6,7},{7,6},{8,9},{9,8},{10,11... | collective-permute-start | bytes 393224 | tf_op jit(solution)/shard_map/ppermute | solution.py:582
  16.1 2.7 %collective-permute-start.2 = (bf16[16,96,128]{2,1,0:T(8,128)(2,1)S(1)}, bf16[16,96,128]{2,1,0:T(8,128)(2,1)S(1)}, u32[]{:S(2)}, u32[]{:S(2)}) collective-permute-start(bf16[16,96,128]{2,1,0:T(8,128)(2,1)S(1)} %get-tuple-element.40), channel_id=1, source_target_pairs={{0,64},{64,0},{1,65},{65,1},{2,66},{66,2},{3,67},{67,3},{4,68},{68... | collective-permute-start | bytes 1179656 | tf_op jit(solution)/shard_map/ppermute | solution.py:626
  18.8 25.5 %copy-start = (bf16[32,864]{1,0:T(8,128)(2,1)S(1)}, bf16[32,864]{1,0:T(8,128)(2,1)}, u32[]{:S(2)}) copy-start(bf16[32,864]{1,0:T(8,128)(2,1)} %w_ref.1) | copy-start | bytes 165892
  19.7 17.0 %all-to-all-start = ((bf16[16,96,128]{2,1,0:T(8,128)(2,1)}), bf16[16,96,128]{2,1,0:T(8,128)(2,1)S(1)}, u32[]{:S(2)}, u32[]{:S(2)}) async-start(bf16[16,96,128]{2,1,0:T(8,128)(2,1)} %shard_map.61), calls=%async_computation | async-start | bytes 786432 | tf_op jit(solution)/shard_map/all_to_all | solution.py:628
  27.2 17.1 %collective-permute-start.3 = (bf16[32,16,128]{2,1,0:T(8,128)(2,1)S(1)}, bf16[32,16,128]{2,1,0:T(8,128)(2,1)S(1)}, u32[]{:S(2)}, u32[]{:S(2)}) collective-permute-start(bf16[32,16,128]{2,1,0:T(8,128)(2,1)S(1)} %get-tuple-element.44), channel_id=1, source_target_pairs={{1,2},{2,1},{3,4},{4,3},{5,6},{6,5},{7,8},{8,7},{9,10},{10,9},{11,... | collective-permute-start | bytes 393224 | tf_op jit(solution)/shard_map/ppermute | solution.py:607
  27.9 16.4 %collective-permute-start.4 = (bf16[32,16,128]{2,1,0:T(8,128)(2,1)S(1)}, bf16[32,16,128]{2,1,0:T(8,128)(2,1)S(1)}, u32[]{:S(2)}, u32[]{:S(2)}) collective-permute-start(bf16[32,16,128]{2,1,0:T(8,128)(2,1)S(1)} %get-tuple-element.45), channel_id=1, source_target_pairs={{0,1},{1,0},{2,3},{3,2},{4,5},{5,4},{6,7},{7,6},{8,9},{9,8},{10,11... | collective-permute-start | bytes 393224 | tf_op jit(solution)/shard_map/ppermute | solution.py:608
  37.4 15.5 %all-to-all-start.1 = ((bf16[8,96,128]{2,1,0:T(8,128)(2,1)}), bf16[8,96,128]{2,1,0:T(8,128)(2,1)S(1)}, u32[]{:S(2)}, u32[]{:S(2)}) async-start(bf16[8,96,128]{2,1,0:T(8,128)(2,1)} %shard_map.62), calls=%async_computation.1 | async-start | bytes 393216 | tf_op jit(solution)/shard_map/all_to_all | solution.py:632
  64.3 5.5 %collective-permute-start.5 = (bf16[16,96,128]{2,1,0:T(8,128)(2,1)S(1)}, bf16[16,96,128]{2,1,0:T(8,128)(2,1)S(1)}, u32[]{:S(2)}, u32[]{:S(2)}) collective-permute-start(bf16[16,96,128]{2,1,0:T(8,128)(2,1)S(1)} %all_to_all.15.mine_ref), channel_id=1, source_target_pairs={{0,64},{64,0},{1,65},{65,1},{2,66},{66,2},{3,67},{67,3},{4,68},{68... | collective-permute-start | bytes 1179656 | tf_op jit(solution)/shard_map/ppermute | solution.py:639

commit v6 on v5

--- a/solution.py
+++ b/solution.py
@@ -563,7 +563,7 @@
     size = lax.axis_size(space)
     rounds = [
         [pair for i in range(start, size - 1, 2) for pair in ((i, i + 1), (i + 1, i))]
-        for start in (1, 0)
+        for start in (0, 1)
     ]
     hold = lax.optimization_barrier
 
@@ -571,7 +571,7 @@
     core = lax.axis_index("core").astype(jnp.int32).reshape(1)
     first = (where == 0).astype(jnp.int32).reshape(1)
     last = (where == size - 1).astype(jnp.int32).reshape(1)
-    odd = (where % 2).astype(jnp.int32).reshape(1)
+    odd = ((where + 1) % 2).astype(jnp.int32).reshape(1)
     activations, cotangent, core, first, last, odd = hold(
         (activations, cotangent, core, first, last, odd)
     )

time: 75.3 us -> 75 us (level)
  starting transfers between devices: 29.7 us -> 27 us
  waiting for transfers between devices: 10.6 us -> 12.9 us
    ppermute x1, starting transfers between devices: 5.43 us -> 0.66 us  [body(): act_two = lax.ppermute(act_two, space, rounds[1])]
    all_to_all x1, starting transfers between devices: 7.52 us -> 10.9 us  [body(): parts = lax.all_to_all(mine, ('y', 'x'), 0, 0, tiled=True)]
    ppermute x1, starting transfers between devices: 3.08 us -> 0.66 us  [body(): cot_two = lax.ppermute(cot_two, space, rounds[1])]
    all_to_all x1, waiting for transfers between devices: 5.75 us -> 8.05 us  [body(): parts = lax.all_to_all(mine, ('y', 'x'), 0, 0, tiled=True)]
    ppermute x1, starting transfers between devices: 0.67 us -> 2.55 us  [body(): act_one = lax.ppermute(act_one, space, rounds[0])]
where the time goes in v6:
time: 75 us; the launch traced here: 74.6 us
  starting transfers between devices  27 us (36%)
  Pallas kernels  22.6 us (30%)
  waiting for transfers between devices  12.9 us (17%)
  blocking collectives  11.1 us (15%)
  between operations  0.78 us (1%)
    pallas_call x7, Pallas kernels, call(): pl.pallas_call(kernel, out_shape=shapes, in_specs=specs or [SMEM] * scala...  22.6 us
    all_to_all x1, blocking collectives, body(): whole = lax.all_to_all(block, ('y', 'x'), 0, 0, tiled=True)  11.1 us
    all_to_all x1, starting transfers between devices, body(): parts = lax.all_to_all(mine, ('y', 'x'), 0, 0, tiled=True)  10.9 us
    all_to_all x1, waiting for transfers between devices, body(): parts = lax.all_to_all(mine, ('y', 'x'), 0, 0, tiled=True)  8.05 us
    all_to_all x1, starting transfers between devices, body(): parts = lax.all_to_all(block, ('z_hi', 'z_lo'), 0, 0, tiled=True)  6.36 us
    ppermute x1, starting transfers between devices, body(): other = lax.ppermute(whole, 'core', swap)  4.14 us
    ppermute x1, starting transfers between devices, body(): act_one = lax.ppermute(act_one, space, rounds[0])  2.55 us
    all_to_all x1, waiting for transfers between devices, body(): parts = lax.all_to_all(block, ('z_hi', 'z_lo'), 0, 0, tiled=True)  2.09 us
  transfers between devices with their start and end apart: 8, of which 4 were waited for; matrix products, arithmetic and copies ran while one was open for 0% of the time, Pallas kernels for 18%

profile of v6, /device:TPU:1, one launch (start us, length us, event | category | flops | bytes accessed | tf_op | source)
XLA Modules:
  0.0 74.6 jit_solution(15522889912815617330)
XLA Ops:
  0.6 1.0 %shard_map.59 = (bf16[32,16,128]{2,1,0:T(8,128)(2,1)S(1)}, bf16[32,16,128]{2,1,0:T(8,128)(2,1)S(1)}) custom-call(s32[1]{0:T(128)} %bitcast.3.odd_ref, bf16[32,4,16,128]{3,2,1,0:T(8,128)(2,1)} %bitcast.8), custom_call_target="tpu_custom_call" | custom-call | bytes 1048576 | tf_op jit(solution)/shard_map/pallas_call | solution.py:506
  1.6 2.6 %collective-permute-start = (bf16[32,16,128]{2,1,0:T(8,128)(2,1)S(1)}, bf16[32,16,128]{2,1,0:T(8,128)(2,1)S(1)}, u32[]{:S(2)}, u32[]{:S(2)}) collective-permute-start(bf16[32,16,128]{2,1,0:T(8,128)(2,1)S(1)} %get-tuple-element.36), channel_id=1, source_target_pairs={{0,1},{1,0},{2,3},{3,2},{4,5},{5,4},{6,7},{7,6},{8,9},{9,8},{10,11... | collective-permute-start | bytes 393224 | tf_op jit(solution)/shard_map/ppermute | solution.py:581
  4.2 0.7 collective-permute-start.1
  4.9 6.4 %shard_map.58 = (f32[29,96,128]{2,1,0:T(8,128)S(1)}, f32[3,96,128]{2,1,0:T(8,128)S(1)}, bf16[4,16,32,128]{3,2,1,0:T(8,128)(2,1)S(1)}, bf16[4,16,32,128]{3,2,1,0:...) custom-call(s32[1]{0:T(128)} %bitcast.3.odd_ref, bf16[32,4,16,128]{3,2,1,0:T(8,128)(2,1)} %bitcast.9, ...), custom_call_target="tpu_custom_call" | custom-call | flops 6000000000 | bytes 1048576 | tf_op jit(solution)/shard_map/pallas_call | solution.py:506
  11.3 0.0 collective-permute-done.one_ref.act_one
  11.3 1.9 %shard_map.60 = (bf16[16,96,128]{2,1,0:T(8,128)(2,1)S(1)}, bf16[16,96,128]{2,1,0:T(8,128)(2,1)S(1)}) custom-call(s32[1]{0:T(128)} %bitcast.core_ref, s32[1]{0:T(128)} %bitcast.1.first_ref, s32[1]{0:T(128)} %bitcast.2.last_ref, s32[1]{0:T(128)} %bitcast.3.odd_ref, f32[29,96,128]{2,1,0:T(8,128)S(1)} %get-tuple-element.33.in_ref, ...), custom_call_target="tpu_custom_call" | custom-call | flops 1000000000 | bytes 1048576 | tf_op jit(solution)/shard_map/pallas_call | solution.py:506
  13.2 1.0 %collective-permute-start.2 = (bf16[16,96,128]{2,1,0:T(8,128)(2,1)S(1)}, bf16[16,96,128]{2,1,0:T(8,128)(2,1)S(1)}, u32[]{:S(2)}, u32[]{:S(2)}) collective-permute-start(bf16[16,96,128]{2,1,0:T(8,128)(2,1)S(1)} %get-tuple-element.40), channel_id=1, source_target_pairs={{0,64},{64,0},{1,65},{65,1},{2,66},{66,2},{3,67},{67,3},{4,68},{68... | collective-permute-start | bytes 1179656 | tf_op jit(solution)/shard_map/ppermute | solution.py:626
  14.2 1.3 %collective-permute-done.2.arrived_ref = bf16[16,96,128]{2,1,0:T(8,128)(2,1)S(1)} collective-permute-done((bf16[16,96,128]{2,1,0:T(8,128)(2,1)S(1)}, bf16[16,96,128]{2,1,0:T(8,128)(2,1)S(1)}, u32[]{:S(2)}, u32[]{:S(2)}) %collective-permute-start.2) | collective-permute-done | bytes 393248 | tf_op jit(solution)/shard_map/ppermute | solution.py:626
  15.6 0.9 %shard_map.61 = bf16[16,96,128]{2,1,0:T(8,128)(2,1)} custom-call(bf16[16,96,128]{2,1,0:T(8,128)(2,1)S(1)} %get-tuple-element.39.keep_ref, bf16[16,96,128]{2,1,0:T(8,128)(2,1)S(1)} %collective-permute-done.2.arrived_ref), custom_call_target="tpu_custom_call" | custom-call | bytes 1048576 | tf_op jit(solution)/shard_map/pallas_call | solution.py:506
  16.4 10.9 %all-to-all-start = ((bf16[16,96,128]{2,1,0:T(8,128)(2,1)}), bf16[16,96,128]{2,1,0:T(8,128)(2,1)S(1)}, u32[]{:S(2)}, u32[]{:S(2)}) async-start(bf16[16,96,128]{2,1,0:T(8,128)(2,1)} %shard_map.61), calls=%async_computation | async-start | bytes 786432 | tf_op jit(solution)/shard_map/all_to_all | solution.py:628
  27.3 0.8 %collective-permute-start.3 = (bf16[32,16,128]{2,1,0:T(8,128)(2,1)S(1)}, bf16[32,16,128]{2,1,0:T(8,128)(2,1)S(1)}, u32[]{:S(2)}, u32[]{:S(2)}) collective-permute-start(bf16[32,16,128]{2,1,0:T(8,128)(2,1)S(1)} %get-tuple-element.44), channel_id=1, source_target_pairs={{0,1},{1,0},{2,3},{3,2},{4,5},{5,4},{6,7},{7,6},{8,9},{9,8},{10,11... | collective-permute-start | bytes 393224 | tf_op jit(solution)/shard_map/ppermute | solution.py:607
  28.1 0.7 collective-permute-start.4
  28.8 8.0 %all-to-all-done.parts_ref = bf16[16,96,128]{2,1,0:T(8,128)(2,1)S(1)} async-done(((bf16[16,96,128]{2,1,0:T(8,128)(2,1)}), bf16[16,96,128]{2,1,0:T(8,128)(2,1)S(1)}, u32[]{:S(2)}, u32[]{:S(2)}) %all-to-all-start) | async-done | bytes 393248 | tf_op jit(solution)/shard_map/all_to_all | solution.py:628
  36.8 0.7 %shard_map.62 = bf16[8,96,128]{2,1,0:T(8,128)(2,1)} custom-call(bf16[16,96,128]{2,1,0:T(8,128)(2,1)S(1)} %all-to-all-done.parts_ref), custom_call_target="tpu_custom_call" | custom-call | bytes 1048576 | tf_op jit(solution)/shard_map/pallas_call | solution.py:506
  37.6 6.4 %all-to-all-start.1 = ((bf16[8,96,128]{2,1,0:T(8,128)(2,1)}), bf16[8,96,128]{2,1,0:T(8,128)(2,1)S(1)}, u32[]{:S(2)}, u32[]{:S(2)}) async-start(bf16[8,96,128]{2,1,0:T(8,128)(2,1)} %shard_map.62), calls=%async_computation.1 | async-start | bytes 393216 | tf_op jit(solution)/shard_map/all_to_all | solution.py:632
  43.9 0.0 collective-permute-done.3.cot_one
  44.0 6.6 %shard_map.63 = (bf16[32,4,16,128]{3,2,1,0:T(8,128)(2,1)}, bf16[32,4,16,128]{3,2,1,0:T(8,128)(2,1)}) custom-call(s32[1]{0:T(128)} %bitcast.3.odd_ref, bf16[4,16,32,128]{3,2,1,0:T(8,128)(2,1)S(1)} %get-tuple-element.42.act_ref, bf16[4,16,32,128]{3,2,1,0:T(8,128)(2,1)S(1)} %get-tuple-element.43.cot_ref, ...), custom_call_target="tpu_custom_call" | custom-call | flops 20000000000 | bytes 1048576 | tf_op jit(solution)/shard_map/pallas_call | solution.py:506
  50.5 2.1 %all-to-all-done.1 = bf16[8,96,128]{2,1,0:T(8,128)(2,1)S(1)} async-done(((bf16[8,96,128]{2,1,0:T(8,128)(2,1)}), bf16[8,96,128]{2,1,0:T(8,128)(2,1)S(1)}, u32[]{:S(2)}, u32[]{:S(2)}) %all-to-all-start.1) | async-done | bytes 196640 | tf_op jit(solution)/shard_map/all_to_all | solution.py:632
  52.7 0.1 fusion.1
  52.8 0.1 broadcast_in_dim.11
  52.9 11.1 %all_to_all.15.mine_ref = bf16[16,96,128]{2,1,0:T(8,128)(2,1)S(1)} all-to-all(bf16[16,96,128]{2,1,0:T(8,128)(2,1)S(1)} %broadcast_in_dim.11), channel_id=1, replica_groups=mesh['z_hi'=2,'core'=2,'y'=4,'x'=4,'z_lo'=4] {'y','x'}, dimensions={0} | all-to-all | bytes 786432 | tf_op jit(solution)/shard_map/all_to_all | solution.py:638
  64.0 4.1 %collective-permute-start.5 = (bf16[16,96,128]{2,1,0:T(8,128)(2,1)S(1)}, bf16[16,96,128]{2,1,0:T(8,128)(2,1)S(1)}, u32[]{:S(2)}, u32[]{:S(2)}) collective-permute-start(bf16[16,96,128]{2,1,0:T(8,128)(2,1)S(1)} %all_to_all.15.mine_ref), channel_id=1, source_target_pairs={{0,64},{64,0},{1,65},{65,1},{2,66},{66,2},{3,67},{67,3},{4,68},{68... | collective-permute-start | bytes 1179656 | tf_op jit(solution)/shard_map/ppermute | solution.py:639
  68.1 1.3 %collective-permute-done.5.other_ref = bf16[16,96,128]{2,1,0:T(8,128)(2,1)S(1)} collective-permute-done((bf16[16,96,128]{2,1,0:T(8,128)(2,1)S(1)}, bf16[16,96,128]{2,1,0:T(8,128)(2,1)S(1)}, u32[]{:S(2)}, u32[]{:S(2)}) %collective-permute-start.5) | collective-permute-done | bytes 393248 | tf_op jit(solution)/shard_map/ppermute | solution.py:639
  69.5 5.1 %shard_map.64 = f32[32,864]{1,0:T(8,128)} custom-call(s32[1]{0:T(128)} %bitcast.core_ref, bf16[16,96,128]{2,1,0:T(8,128)(2,1)S(1)} %all_to_all.15.mine_ref, bf16[16,96,128]{2,1,0:T(8,128)(2,1)S(1)} %collective-permute-done.5.other_ref), custom_call_target="tpu_custom_call" | custom-call | flops 1000000000 | bytes 1048576 | tf_op jit(solution)/shard_map/pallas_call | solution.py:506
  (8 shorter events, 0.1 us)
Async XLA Ops:
  1.6 9.7 %collective-permute-start = (bf16[32,16,128]{2,1,0:T(8,128)(2,1)S(1)}, bf16[32,16,128]{2,1,0:T(8,128)(2,1)S(1)}, u32[]{:S(2)}, u32[]{:S(2)}) collective-permute-start(bf16[32,16,128]{2,1,0:T(8,128)(2,1)S(1)} %get-tuple-element.36), channel_id=1, source_target_pairs={{0,1},{1,0},{2,3},{3,2},{4,5},{5,4},{6,7},{7,6},{8,9},{9,8},{10,11... | collective-permute-start | bytes 393224 | tf_op jit(solution)/shard_map/ppermute | solution.py:581
  4.2 7.1 %collective-permute-start.1 = (bf16[32,16,128]{2,1,0:T(8,128)(2,1)S(1)}, bf16[32,16,128]{2,1,0:T(8,128)(2,1)S(1)}, u32[]{:S(2)}, u32[]{:S(2)}) collective-permute-start(bf16[32,16,128]{2,1,0:T(8,128)(2,1)S(1)} %get-tuple-element.37), channel_id=1, source_target_pairs={{1,2},{2,1},{3,4},{4,3},{5,6},{6,5},{7,8},{8,7},{9,10},{10,9},{11,... | collective-permute-start | bytes 393224 | tf_op jit(solution)/shard_map/ppermute | solution.py:582
  13.2 2.4 %collective-permute-start.2 = (bf16[16,96,128]{2,1,0:T(8,128)(2,1)S(1)}, bf16[16,96,128]{2,1,0:T(8,128)(2,1)S(1)}, u32[]{:S(2)}, u32[]{:S(2)}) collective-permute-start(bf16[16,96,128]{2,1,0:T(8,128)(2,1)S(1)} %get-tuple-element.40), channel_id=1, source_target_pairs={{0,64},{64,0},{1,65},{65,1},{2,66},{66,2},{3,67},{67,3},{4,68},{68... | collective-permute-start | bytes 1179656 | tf_op jit(solution)/shard_map/ppermute | solution.py:626
  15.6 28.4 %copy-start = (bf16[32,864]{1,0:T(8,128)(2,1)S(1)}, bf16[32,864]{1,0:T(8,128)(2,1)}, u32[]{:S(2)}) copy-start(bf16[32,864]{1,0:T(8,128)(2,1)} %w_ref.1) | copy-start | bytes 165892
  16.4 20.4 %all-to-all-start = ((bf16[16,96,128]{2,1,0:T(8,128)(2,1)}), bf16[16,96,128]{2,1,0:T(8,128)(2,1)S(1)}, u32[]{:S(2)}, u32[]{:S(2)}) async-start(bf16[16,96,128]{2,1,0:T(8,128)(2,1)} %shard_map.61), calls=%async_computation | async-start | bytes 786432 | tf_op jit(solution)/shard_map/all_to_all | solution.py:628
  27.3 16.6 %collective-permute-start.3 = (bf16[32,16,128]{2,1,0:T(8,128)(2,1)S(1)}, bf16[32,16,128]{2,1,0:T(8,128)(2,1)S(1)}, u32[]{:S(2)}, u32[]{:S(2)}) collective-permute-start(bf16[32,16,128]{2,1,0:T(8,128)(2,1)S(1)} %get-tuple-element.44), channel_id=1, source_target_pairs={{0,1},{1,0},{2,3},{3,2},{4,5},{5,4},{6,7},{7,6},{8,9},{9,8},{10,11... | collective-permute-start | bytes 393224 | tf_op jit(solution)/shard_map/ppermute | solution.py:607
  28.1 15.9 %collective-permute-start.4 = (bf16[32,16,128]{2,1,0:T(8,128)(2,1)S(1)}, bf16[32,16,128]{2,1,0:T(8,128)(2,1)S(1)}, u32[]{:S(2)}, u32[]{:S(2)}) collective-permute-start(bf16[32,16,128]{2,1,0:T(8,128)(2,1)S(1)} %get-tuple-element.45), channel_id=1, source_target_pairs={{1,2},{2,1},{3,4},{4,3},{5,6},{6,5},{7,8},{8,7},{9,10},{10,9},{11,... | collective-permute-start | bytes 393224 | tf_op jit(solution)/shard_map/ppermute | solution.py:608
  37.6 15.1 %all-to-all-start.1 = ((bf16[8,96,128]{2,1,0:T(8,128)(2,1)}), bf16[8,96,128]{2,1,0:T(8,128)(2,1)S(1)}, u32[]{:S(2)}, u32[]{:S(2)}) async-start(bf16[8,96,128]{2,1,0:T(8,128)(2,1)} %shard_map.62), calls=%async_computation.1 | async-start | bytes 393216 | tf_op jit(solution)/shard_map/all_to_all | solution.py:632
  64.0 5.5 %collective-permute-start.5 = (bf16[16,96,128]{2,1,0:T(8,128)(2,1)S(1)}, bf16[16,96,128]{2,1,0:T(8,128)(2,1)S(1)}, u32[]{:S(2)}, u32[]{:S(2)}) collective-permute-start(bf16[16,96,128]{2,1,0:T(8,128)(2,1)S(1)} %all_to_all.15.mine_ref), channel_id=1, source_target_pairs={{0,64},{64,0},{1,65},{65,1},{2,66},{66,2},{3,67},{67,3},{4,68},{68... | collective-permute-start | bytes 1179656 | tf_op jit(solution)/shard_map/ppermute | solution.py:639
